TPU v7x, 32 devices: a whole 2x2x4 slice. The times are simulated.
32 devices in a mesh: section: 4 (over x, core), space: 8 (over z, y).
Axes of the slice: x: 2, y: 2, z: 4, core: 2. Of those that a mesh axis runs over, the one named last changes fastest.
Arguments:
- volume: bfloat16 [4, 16, 8, 8, 64], P('section', 'space'), may hold values from -6 to 6
- w_first: bfloat16 [1728, 128], replicated, may hold values from -0.25 to 0.25
- w_enc: bfloat16 [3456, 128], replicated, may hold values from -0.1875 to 0.1875
- w_down: bfloat16 [1024, 256], replicated, may hold values from -0.25 to 0.25
- w_bottom: bfloat16 [6912, 256], replicated, may hold values from -0.125 to 0.125
- w_up: bfloat16 [256, 1024], replicated, may hold values from -0.375 to 0.375
- w_join: bfloat16 [6912, 128], replicated, may hold values from -0.125 to 0.125
- cotangent: bfloat16 [4, 16, 8, 8, 128], P('section', 'space'), may hold values from -6 to 6
Outputs:
- decoded: bfloat16 [4, 16, 8, 8, 128], P('section', 'space')
- grad_first: float32 [1728, 128], P(None, 'space')
- grad_enc: float32 [3456, 128], P(None, 'space')
- grad_down: float32 [1024, 256], P(None, 'space')
- grad_bottom: float32 [6912, 256], P(None, 'space')
- grad_up: float32 [256, 1024], P(None, 'space')
- grad_join: float32 [6912, 128], P(None, 'space')
All inputs are finite; a program needn't handle non-finite values.
Results may differ from a plain program's by a relative error of at most 0.025.
Values may be sent and summed in bfloat16 or wider, within the bound.
No kernel may reach another device: no remote copies, remote signals or barrier semaphores. Data moves between devices by JAX's collectives and lax.ppermute only.
A program may use at most 128 MiB of HBM per device.

v0:
```python
import math

import jax
import jax.numpy as jnp
from jax import lax
from jax.sharding import PartitionSpec as P


def padded_2(array, sides, width):
    for axis, dim in sides:
        devices, length = (lax.axis_size(axis), array.shape[dim])
        up = [(i, (i + 1) % devices) for i in range(devices - 1)]
        down = [(j, i) for i, j in up]
        last = lax.slice_in_dim(array, length - width, length, axis=dim)
        leading = lax.slice_in_dim(array, 0, width, axis=dim)
        before = lax.ppermute(last, axis, up)
        after = lax.ppermute(leading, axis, down)
        array = jnp.concatenate([before, array, after], axis=dim)
    return array


def pad_sides(rimmed):
    return jnp.pad(rimmed, ((0, 0), (1, 1), (1, 1), (0, 0)))


def fine_rims(field):
    return pad_sides(padded_2(field, (("space", 0),), 1))


def coarse_rims(field):
    return pad_sides(padded_2(field, (("space", 0),), 1))


def silu_slope(pre):
    logistic = jax.nn.sigmoid(pre)
    return logistic * (1.0 + pre * (1.0 - logistic))


def to_blocks(field):
    size_x, size_y, size_z, width = field.shape
    blocks = field.reshape(size_x // 2, 2, size_y // 2, 2, size_z // 2, 2, width).transpose(
        0, 2, 4, 1, 3, 5, 6
    )
    return blocks.reshape(-1, 8 * width)


def from_blocks(flat, coarse, width):
    size_x, size_y, size_z = coarse
    spread = flat.reshape(size_x, size_y, size_z, 2, 2, 2, width).transpose(0, 3, 1, 4, 2, 5, 6)
    return spread.reshape(2 * size_x, 2 * size_y, 2 * size_z, width)


def convolve(padded, weight, extent):
    size_x, size_y, size_z = extent
    width_in = padded.shape[-1]
    summed = jnp.zeros((size_x * size_y * size_z, weight.shape[-1]), jnp.float32)
    for across in range(3):
        for upward in range(3):
            for inward in range(3):
                tap_index = across * 9 + upward * 3 + inward
                window_part = padded[
                    across : across + size_x, upward : upward + size_y, inward : inward + size_z
                ].reshape(-1, width_in)
                summed = summed + jnp.dot(
                    window_part,
                    weight[tap_index * width_in : (tap_index + 1) * width_in],
                    preferred_element_type=jnp.float32,
                )
    return summed.reshape(size_x, size_y, size_z, -1)


def transpose_conv(padded_grad, weight, extent):
    size_x, size_y, size_z = extent
    width_out = padded_grad.shape[-1]
    width_in = weight.shape[0] // 27
    summed = jnp.zeros((size_x * size_y * size_z, width_in), jnp.float32)
    for across in range(3):
        for upward in range(3):
            for inward in range(3):
                tap_index = across * 9 + upward * 3 + inward
                window_part = padded_grad[
                    2 - across : 2 - across + size_x,
                    2 - upward : 2 - upward + size_y,
                    2 - inward : 2 - inward + size_z,
                ].reshape(-1, width_out)
                block = weight[tap_index * width_in : (tap_index + 1) * width_in]
                summed = summed + lax.dot_general(
                    window_part, block, (((1,), (1,)), ((), ())), preferred_element_type=jnp.float32
                )
    return summed.reshape(size_x, size_y, size_z, width_in)


def weight_grad(padded_in, grad_pre, extent):
    size_x, size_y, size_z = extent
    width_in = padded_in.shape[-1]
    flat_grad = grad_pre.reshape(-1, grad_pre.shape[-1])
    blocks = []
    for across in range(3):
        for upward in range(3):
            for inward in range(3):
                window_part = padded_in[
                    across : across + size_x, upward : upward + size_y, inward : inward + size_z
                ].reshape(-1, width_in)
                blocks.append(
                    lax.dot_general(
                        window_part,
                        flat_grad,
                        (((0,), (0,)), ((), ())),
                        preferred_element_type=jnp.float32,
                    )
                )
    return jnp.concatenate(blocks, 0)


def activate(pre):
    return jax.nn.silu(pre).astype(jnp.bfloat16)


def pulled(grad_in, pre):
    return (grad_in.astype(jnp.float32) * silu_slope(pre)).astype(jnp.bfloat16)


def body(volume, w_first, w_enc, w_down, w_bottom, w_up, w_join, cotangent):
    section_count = lax.axis_size("section")
    space_count = lax.axis_size("space")
    field = volume[0]
    grad_out = cotangent[0]
    fine = field.shape[:3]
    coarse = (fine[0] // 2, fine[1] // 2, fine[2] // 2)
    width = w_enc.shape[1]
    wide = w_bottom.shape[1]
    pad_volume = fine_rims(field)
    pre_first = convolve(pad_volume, w_first, fine)
    act_first = activate(pre_first)
    pad_first = fine_rims(act_first)
    pre_enc = convolve(pad_first, w_enc, fine)
    skip_map = activate(pre_enc)
    skip_blocks = to_blocks(skip_map)
    pre_down = jnp.dot(skip_blocks, w_down, preferred_element_type=jnp.float32).reshape(
        coarse + (wide,)
    )
    act_down = activate(pre_down)
    pad_down = coarse_rims(act_down)
    pre_bottom = convolve(pad_down, w_bottom, coarse)
    act_bottom = activate(pre_bottom)
    bottom_flat = act_bottom.reshape(-1, wide)
    lifted = from_blocks(
        jnp.dot(bottom_flat, w_up, preferred_element_type=jnp.float32), coarse, width
    ).astype(jnp.bfloat16)
    joined = jnp.concatenate([lifted, skip_map], axis=-1)
    pad_joined = fine_rims(joined)
    pre_join = convolve(pad_joined, w_join, fine)
    decoded_map = activate(pre_join)
    step_join = pulled(grad_out, pre_join)
    grad_join = weight_grad(pad_joined, step_join, fine)
    back_pair = transpose_conv(fine_rims(step_join), w_join, fine)
    grad_lift = back_pair[..., :width].astype(jnp.bfloat16)
    grad_skip = back_pair[..., width:]
    lift_blocks = to_blocks(grad_lift)
    grad_up = lax.dot_general(
        bottom_flat, lift_blocks, (((0,), (0,)), ((), ())), preferred_element_type=jnp.float32
    )
    back_bottom = lax.dot_general(
        lift_blocks, w_up, (((1,), (1,)), ((), ())), preferred_element_type=jnp.float32
    )
    back_bottom = back_bottom.reshape(coarse + (wide,)).astype(jnp.bfloat16)
    step_bottom = pulled(back_bottom, pre_bottom)
    grad_bottom = weight_grad(pad_down, step_bottom, coarse)
    back_down = transpose_conv(coarse_rims(step_bottom), w_bottom, coarse).astype(jnp.bfloat16)
    step_down = pulled(back_down, pre_down).reshape(-1, wide)
    grad_down = lax.dot_general(
        skip_blocks, step_down, (((0,), (0,)), ((), ())), preferred_element_type=jnp.float32
    )
    back_skip = from_blocks(
        lax.dot_general(
            step_down, w_down, (((1,), (1,)), ((), ())), preferred_element_type=jnp.float32
        ),
        coarse,
        width,
    )
    step_enc = ((back_skip + grad_skip) * silu_slope(pre_enc)).astype(jnp.bfloat16)
    grad_enc = weight_grad(pad_first, step_enc, fine)
    back_first = transpose_conv(fine_rims(step_enc), w_enc, fine).astype(jnp.bfloat16)
    step_first = pulled(back_first, pre_first)
    grad_first = weight_grad(pad_volume, step_first, fine)
    part_first, part_enc, part_down, part_bottom, part_up, part_join = (
        lax.psum_scatter(
            grad_first.astype(jnp.bfloat16), "space", scatter_dimension=1, tiled=True
        ).astype(jnp.float32),
        lax.psum_scatter(
            grad_enc.astype(jnp.bfloat16), "space", scatter_dimension=1, tiled=True
        ).astype(jnp.float32),
        lax.psum_scatter(
            grad_down.astype(jnp.bfloat16), "space", scatter_dimension=1, tiled=True
        ).astype(jnp.float32),
        lax.psum_scatter(
            grad_bottom.astype(jnp.bfloat16), "space", scatter_dimension=1, tiled=True
        ).astype(jnp.float32),
        lax.psum_scatter(
            grad_up.astype(jnp.bfloat16), "space", scatter_dimension=1, tiled=True
        ).astype(jnp.float32),
        lax.psum_scatter(
            grad_join.astype(jnp.bfloat16), "space", scatter_dimension=1, tiled=True
        ).astype(jnp.float32),
    )
    sum_first, sum_enc, sum_down, sum_bottom, sum_up, sum_join = (
        lax.psum(part_first.astype(jnp.bfloat16), "section").astype(jnp.float32),
        lax.psum(part_enc.astype(jnp.bfloat16), "section").astype(jnp.float32),
        lax.psum(part_down.astype(jnp.bfloat16), "section").astype(jnp.float32),
        lax.psum(part_bottom.astype(jnp.bfloat16), "section").astype(jnp.float32),
        lax.psum(part_up.astype(jnp.bfloat16), "section").astype(jnp.float32),
        lax.psum(part_join.astype(jnp.bfloat16), "section").astype(jnp.float32),
    )
    factor = 1.0 / math.sqrt(section_count * space_count * fine[0] * fine[1] * fine[2])
    return (
        decoded_map[None],
        sum_first * factor,
        sum_enc * factor,
        sum_down * factor,
        sum_bottom * factor,
        sum_up * factor,
        sum_join * factor,
    )


def solution(mesh):
    return jax.shard_map(
        body,
        mesh=mesh,
        in_specs=(
            P("section", "space", None, None, None),
            P(),
            P(),
            P(),
            P(),
            P(),
            P(),
            P("section", "space", None, None, None),
        ),
        out_specs=(
            P("section", "space", None, None, None),
            P(None, "space"),
            P(None, "space"),
            P(None, "space"),
            P(None, "space"),
            P(None, "space"),
            P(None, "space"),
        ),
        check_vma=False,
    )
```

profile of v0, /device:TPU:0, one launch (start us, length us, event | category | flops | bytes accessed | tf_op | source)
XLA Modules:
  0.0 691.1 jit_solution(1434829963881902161)
XLA Ops:
  8.1 1.3 collective-permute-start.1
  9.4 5.5 collective-permute-start
  14.9 1.4 collective-permute-done
  20.9 1.3 collective-permute-start.3
  22.2 5.4 collective-permute-start.2
  27.9 1.2 collective-permute-done.2
  34.1 1.3 collective-permute-start.5
  35.4 5.7 collective-permute-start.4
  41.2 1.3 collective-permute-done.4
  71.8 1.3 collective-permute-start.7
  73.1 5.7 collective-permute-start.6
  86.0 1.3 collective-permute-start.9
  87.3 5.7 collective-permute-start.8
  96.3 1.2 copy-done.4
  103.3 1.3 collective-permute-start.11
  104.6 5.4 collective-permute-start.10
  112.6 1.1 fusion.306
  113.7 1.1 fusion.318
  116.2 1.1 convolution_add_fusion.142
  117.3 1.1 convolution_add_fusion.141
  119.5 1.1 convolution_add_fusion.139
  120.6 1.1 convolution_add_fusion.138
  121.6 1.1 convolution_add_fusion.137
  122.7 1.1 convolution_add_fusion.136
  123.8 1.1 convolution_add_fusion.135
  124.9 1.1 convolution_add_fusion.134
  126.0 1.1 convolution_add_fusion.133
  127.1 1.1 convolution_add_fusion.132
  128.2 1.1 convolution_add_fusion.131
  129.3 1.1 convolution_add_fusion.130
  130.3 1.1 convolution_add_fusion.129
  131.4 1.1 convolution_add_fusion.128
  132.5 1.1 convolution_add_fusion.127
  133.6 1.1 convolution_add_fusion.126
  134.7 1.1 convolution_add_fusion.125
  135.8 1.1 convolution_add_fusion.124
  138.0 1.1 convolution_add_fusion.122
  139.1 1.1 convolution_add_fusion.121
  140.2 1.1 fusion.237
  142.2 1.3 collective-permute-start.13
  143.5 5.6 collective-permute-start.12
  172.0 1.6 copy.152
  180.4 3.9 copy.158
  208.4 5.9 copy.154
  215.0 1.1 convolution_convert_fusion.1
  216.9 12.5 %reduce-scatter.19.cloned.1.call-done = bf16[16,1728]{1,0:T(8,128)(2,1)} async-done(((bf16[128,1728]{1,0:T(8,128)(2,1)}), bf16[16,1728]{1,0:T(8,128)(2,1)}) %reduce-scatter.19.cloned.1.call-update) | async-done | bytes 55312
  229.3 1.1 copy.151
  230.4 15.5 %psum.42 = bf16[1728,16]{1,0:T(8,128)(2,1)S(1)} all-reduce(bf16[1728,16]{1,0:T(8,128)(2,1)S(1)} %copy.151), channel_id=1, replica_groups=mesh['section'=4,'space'=8] {'section'}, use_global_device_ids=true, to_apply=%region_1.2 | all-reduce | flops 27648 | bytes 110592 | tf_op jit(solution)/shard_map/psum | solution.py:207
  245.9 48.1 %reduce-scatter.25.cloned.1.call-done = bf16[128,256]{1,0:T(8,128)(2,1)} async-done(((bf16[1024,256]{1,0:T(8,128)(2,1)}), bf16[128,256]{1,0:T(8,128)(2,1)}) %reduce-scatter.25.cloned.1.call-update) | async-done | bytes 65552
  294.0 1.6 copy.157
  295.6 62.8 %reduce-scatter.21.cloned.1.call-done = bf16[16,3456]{1,0:T(8,128)(2,1)} async-done(((bf16[128,3456]{1,0:T(8,128)(2,1)}), bf16[16,3456]{1,0:T(8,128)(2,1)}) %reduce-scatter.21.cloned.1.call-update) | async-done | bytes 110608
  358.3 2.1 copy.153
  360.4 66.5 %reduce-scatter.27.cloned.1.call-done = bf16[16,6912]{1,0:T(8,128)(2,1)} async-done(((bf16[128,6912]{1,0:T(8,128)(2,1)}), bf16[16,6912]{1,0:T(8,128)(2,1)}) %reduce-scatter.27.cloned.1.call-update) | async-done | bytes 221200
  426.9 2.5 copy.159
  429.4 79.4 %reduce-scatter.23.cloned.1.call-done = bf16[32,6912]{1,0:T(8,128)(2,1)} async-done(((bf16[256,6912]{1,0:T(8,128)(2,1)}), bf16[32,6912]{1,0:T(8,128)(2,1)}) %reduce-scatter.23.cloned.1.call-update) | async-done | bytes 442384
  508.8 2.6 copy.155
  511.4 62.5 %reduce-scatter.17.cloned.1.call-done = bf16[1024,32]{0,1:T(8,128)(2,1)} async-done(((bf16[1024,256]{0,1:T(8,128)(2,1)}), bf16[1024,32]{0,1:T(8,128)(2,1)}) %reduce-scatter.17.cloned.1.call-update) | async-done | bytes 65552 | tf_op jit(solution)/shard_map/reduce_scatter | solution.py:193
  574.9 93.4 %all-reduce.10.cloned.1.call-done = (bf16[3456,16]{1,0:T(8,128)(2,1)}, bf16[1024,32]{0,1:T(8,128)(2,1)}, bf16[6912,32]{1,0:T(8,128)(2,1)}, bf16[256,128]{1,0:T(8,128)(2,1)}, bf16[6912,16]{1,0:T(8,128)(2,1)}) async-done(((bf16[3456,16]{1,0:T(8,128)(2,1)}, bf16[1024,32]{0,1:T(8,128)(2,1)}, bf16[6912,32]{1,0:T(8,128)(2,1)}, bf16[256,128]{1,0:T(8,128)(2,1)}, bf16[6912,16]{1,0:T(8,128)(2,1)}), ...) | async-done | bytes 905232 | tf_op jit(solution)/shard_map/psum | solution.py:208
  668.3 1.3 convert_multiply_fusion.2
  669.6 1.2 copy.63
  671.5 3.5 convert_multiply_fusion.1
  675.0 3.4 copy.64
  679.1 2.0 convert_multiply_fusion
  681.0 3.2 copy.65
  (473 shorter events, 119.2 us)
Async XLA Ops:
  7.2 26.7 %copy-start = (bf16[1024,256]{1,0:T(8,128)(2,1)S(1)}, bf16[1024,256]{1,0:T(8,128)(2,1)}, u32[]{:S(2)}) copy-start(bf16[1024,256]{1,0:T(8,128)(2,1)} %param.11) | copy-start | bytes 1572868
  7.2 10.9 %copy-start.6 = (bf16[1,2,8,8,64]{4,3,2,1,0:T(8,128)(2,1)S(1)}, bf16[1,2,8,8,64]{4,3,2,1,0:T(8,128)(2,1)}, u32[]{:S(2)}) copy-start(bf16[1,2,8,8,64]{4,3,2,1,0:T(8,128)(2,1)} %param.8) | copy-start | bytes 49156
  7.2 10.1 %copy-start.7 = (bf16[1728,128]{1,0:T(8,128)(2,1)S(1)}, bf16[1728,128]{1,0:T(8,128)(2,1)}, u32[]{:S(2)}) copy-start(bf16[1728,128]{1,0:T(8,128)(2,1)} %param.9) | copy-start | bytes 1327108
  7.2 222.1 %reduce-scatter.19.cloned.1.call-start = ((), (), s32[]{:S(2)}) async-start(), calls=%async_computation.7 | async-start | bytes 516096
  8.1 6.8 collective-permute-start.1
  9.4 6.9 %collective-permute-start = (bf16[1,8,8,64]{3,2,1,0:T(8,128)(2,1)S(1)}, bf16[1,8,8,64]{3,2,1,0:T(8,128)(2,1)S(1)}, u32[]{:S(2)}, u32[]{:S(2)}) collective-permute-start(bf16[1,8,8,64]{3,2,1,0:T(8,128)(2,1)S(1)} %get-tuple-element.233), channel_id=1, source_target_pairs={{0,1},{1,2},{2,3},{3,4},{4,5},{5,6},{6,7},{8,9},{9,10},{10,11},{11... | collective-permute-start | bytes 24584 | tf_op jit(solution)/shard_map/ppermute | solution.py:16
  16.3 2.3 copy-start.14
  18.5 9.2 %copy-start.3 = (bf16[256,1024]{1,0:T(8,128)(2,1)S(1)}, bf16[256,1024]{1,0:T(8,128)(2,1)}, u32[]{:S(2)}) copy-start(bf16[256,1024]{1,0:T(8,128)(2,1)} %param.13) | copy-start | bytes 1572868
  20.5 8.8 %copy-start.2 = (bf16[3456,128]{1,0:T(8,128)(2,1)S(1)}, bf16[3456,128]{1,0:T(8,128)(2,1)}, u32[]{:S(2)}) copy-start(bf16[3456,128]{1,0:T(8,128)(2,1)} %param.10) | copy-start | bytes 2654212
  20.9 7.0 %collective-permute-start.3 = (bf16[1,8,8,128]{3,2,1,0:T(8,128)(2,1)S(1)}, bf16[1,8,8,128]{3,2,1,0:T(8,128)(2,1)S(1)}, u32[]{:S(2)}, u32[]{:S(2)}) collective-permute-start(bf16[1,8,8,128]{3,2,1,0:T(8,128)(2,1)S(1)} %get-tuple-element.230), channel_id=1, source_target_pairs={{1,0},{2,1},{3,2},{4,3},{5,4},{6,5},{7,6},{9,8},{10,9},{11,10},{12... | collective-permute-start | bytes 49160 | tf_op jit(solution)/shard_map/ppermute | solution.py:17
  22.2 6.9 collective-permute-start.2
  27.9 2.7 copy-start.12
  29.1 1.5 copy-start.16
  34.1 7.1 %collective-permute-start.5 = (bf16[1,4,4,256]{3,2,1,0:T(4,128)(2,1)S(1)}, bf16[1,4,4,256]{3,2,1,0:T(4,128)(2,1)S(1)}, u32[]{:S(2)}, u32[]{:S(2)}) collective-permute-start(bf16[1,4,4,256]{3,2,1,0:T(4,128)(2,1)S(1)} %fusion.507), channel_id=1, source_target_pairs={{1,0},{2,1},{3,2},{4,3},{5,4},{6,5},{7,6},{9,8},{10,9},{11,10},{12... | collective-permute-start | bytes 24584 | tf_op jit(solution)/shard_map/ppermute | solution.py:17
  35.4 7.1 %collective-permute-start.4 = (bf16[1,4,4,256]{3,2,1,0:T(4,128)(2,1)S(1)}, bf16[1,4,4,256]{3,2,1,0:T(4,128)(2,1)S(1)}, u32[]{:S(2)}, u32[]{:S(2)}) collective-permute-start(bf16[1,4,4,256]{3,2,1,0:T(4,128)(2,1)S(1)} %fusion.507), channel_id=1, source_target_pairs={{0,1},{1,2},{2,3},{3,4},{4,5},{5,6},{6,7},{8,9},{9,10},{10,11},{11... | collective-permute-start | bytes 24584 | tf_op jit(solution)/shard_map/ppermute | solution.py:16
  41.2 26.0 %copy-start.22 = (bf16[1,4,4,256]{3,2,1,0:T(4,128)(2,1)}, bf16[1,4,4,256]{3,2,1,0:T(4,128)(2,1)S(1)}, u32[]{:S(2)}) copy-start(bf16[1,4,4,256]{3,2,1,0:T(4,128)(2,1)S(1)} %collective-permute-done.5) | copy-start | bytes 24580
  42.5 17.3 %copy-start.24 = (bf16[1,4,4,256]{3,2,1,0:T(4,128)(2,1)}, bf16[1,4,4,256]{3,2,1,0:T(4,128)(2,1)S(1)}, u32[]{:S(2)}) copy-start(bf16[1,4,4,256]{3,2,1,0:T(4,128)(2,1)S(1)} %collective-permute-done.4) | copy-start | bytes 24580
  71.5 9.2 %copy-start.18 = (bf16[16,256]{1,0:T(8,128)(2,1)}, bf16[16,256]{1,0:T(8,128)(2,1)S(1)}, u32[]{:S(2)}) copy-start(bf16[16,256]{1,0:T(8,128)(2,1)S(1)} %get-tuple-element.235) | copy-start | bytes 24580
  71.8 8.3 %collective-permute-start.7 = (bf16[1,8,8,256]{3,2,1,0:T(8,128)(2,1)S(1)}, bf16[1,8,8,256]{3,2,1,0:T(8,128)(2,1)S(1)}, u32[]{:S(2)}, u32[]{:S(2)}) collective-permute-start(bf16[1,8,8,256]{3,2,1,0:T(8,128)(2,1)S(1)} %get-tuple-element.218), channel_id=1, source_target_pairs={{1,0},{2,1},{3,2},{4,3},{5,4},{6,5},{7,6},{9,8},{10,9},{11,10},{12... | collective-permute-start | bytes 98312 | tf_op jit(solution)/shard_map/ppermute | solution.py:17
  73.1 7.3 %collective-permute-start.6 = (bf16[1,8,8,256]{3,2,1,0:T(8,128)(2,1)S(1)}, bf16[1,8,8,256]{3,2,1,0:T(8,128)(2,1)S(1)}, u32[]{:S(2)}, u32[]{:S(2)}) collective-permute-start(bf16[1,8,8,256]{3,2,1,0:T(8,128)(2,1)S(1)} %get-tuple-element.217), channel_id=1, source_target_pairs={{0,1},{1,2},{2,3},{3,4},{4,5},{5,6},{6,7},{8,9},{9,10},{10,11},{11... | collective-permute-start | bytes 98312 | tf_op jit(solution)/shard_map/ppermute | solution.py:16
  80.1 1.5 copy-start.1
  80.4 2.1 copy-start.8
  81.8 1.9 copy-start.27
  83.6 2.0 copy-start.26
  85.8 8.0 %copy-start.9 = (bf16[1,8,8,256]{3,2,1,0:T(8,128)(2,1)S(1)}, bf16[1,8,8,256]{3,2,1,0:T(8,128)(2,1)}, u32[]{:S(2)}) copy-start(bf16[1,8,8,256]{3,2,1,0:T(8,128)(2,1)} %copy-done.8) | copy-start | bytes 98308
  86.0 10.2 %collective-permute-start.9 = (bf16[1,8,8,128]{3,2,1,0:T(8,128)(2,1)S(1)}, bf16[1,8,8,128]{3,2,1,0:T(8,128)(2,1)S(1)}, u32[]{:S(2)}, u32[]{:S(2)}) collective-permute-start(bf16[1,8,8,128]{3,2,1,0:T(8,128)(2,1)S(1)} %get-tuple-element.226), channel_id=1, source_target_pairs={{1,0},{2,1},{3,2},{4,3},{5,4},{6,5},{7,6},{9,8},{10,9},{11,10},{12... | collective-permute-start | bytes 49160 | tf_op jit(solution)/shard_map/ppermute | solution.py:17
  87.3 10.1 %collective-permute-start.8 = (bf16[1,8,8,128]{3,2,1,0:T(8,128)(2,1)S(1)}, bf16[1,8,8,128]{3,2,1,0:T(8,128)(2,1)S(1)}, u32[]{:S(2)}, u32[]{:S(2)}) collective-permute-start(bf16[1,8,8,128]{3,2,1,0:T(8,128)(2,1)S(1)} %get-tuple-element.225), channel_id=1, source_target_pairs={{0,1},{1,2},{2,3},{3,4},{4,5},{5,6},{6,7},{8,9},{9,10},{10,11},{11... | collective-permute-start | bytes 49160 | tf_op jit(solution)/shard_map/ppermute | solution.py:16
  96.2 1.2 copy-start.4
  103.3 7.6 %collective-permute-start.11 = (bf16[1,4,4,256]{3,2,1,0:T(4,128)(2,1)S(1)}, bf16[1,4,4,256]{3,2,1,0:T(4,128)(2,1)S(1)}, u32[]{:S(2)}, u32[]{:S(2)}) collective-permute-start(bf16[1,4,4,256]{3,2,1,0:T(4,128)(2,1)S(1)} %bitcast.1561), channel_id=1, source_target_pairs={{1,0},{2,1},{3,2},{4,3},{5,4},{6,5},{7,6},{9,8},{10,9},{11,10},{12... | collective-permute-start | bytes 24584 | tf_op jit(solution)/shard_map/ppermute | solution.py:17
  104.6 6.8 collective-permute-start.10
  141.2 0.6 copy-start.20
  142.2 7.8 %collective-permute-start.13 = (bf16[1,8,8,128]{3,2,1,0:T(8,128)(2,1)S(1)}, bf16[1,8,8,128]{3,2,1,0:T(8,128)(2,1)S(1)}, u32[]{:S(2)}, u32[]{:S(2)}) collective-permute-start(bf16[1,8,8,128]{3,2,1,0:T(8,128)(2,1)S(1)} %get-tuple-element.222), channel_id=1, source_target_pairs={{1,0},{2,1},{3,2},{4,3},{5,4},{6,5},{7,6},{9,8},{10,9},{11,10},{12... | collective-permute-start | bytes 49160 | tf_op jit(solution)/shard_map/ppermute | solution.py:17
  143.5 6.9 collective-permute-start.12
  153.1 2.6 copy-start.15
  161.6 2.7 copy-start.19
  161.6 132.4 %reduce-scatter.25.cloned.1.call-start = ((), (), s32[]{:S(2)}) async-start(), calls=%async_computation.10 | async-start | bytes 589824
  164.6 2.0 copy-start.17
  165.6 192.7 %reduce-scatter.21.cloned.1.call-start = ((), (), s32[]{:S(2)}) async-start(), calls=%async_computation.8 | async-start | bytes 995328
  168.9 1.9 copy-start.13
  173.6 253.3 %reduce-scatter.27.cloned.1.call-start = ((), (), s32[]{:S(2)}) async-start(), calls=%async_computation.11 | async-start | bytes 1990656
  184.3 3.6 copy-start.25
  184.3 324.4 %reduce-scatter.23.cloned.1.call-start = ((), (), s32[]{:S(2)}) async-start(), calls=%async_computation.9 | async-start | bytes 3981312
  187.1 8.9 %copy-start.28 = (f32[4,4,256]{2,1,0:T(4,128)S(1)}, f32[4,4,256]{2,1,0:T(4,128)}, u32[]{:S(2)}) copy-start(f32[4,4,256]{2,1,0:T(4,128)} %reshape.1247) | copy-start | bytes 49156
  196.0 8.0 %copy-start.23 = (bf16[1,4,4,256]{3,2,1,0:T(4,128)(2,1)S(1)}, bf16[1,4,4,256]{3,2,1,0:T(4,128)(2,1)}, u32[]{:S(2)}) copy-start(bf16[1,4,4,256]{3,2,1,0:T(4,128)(2,1)} %copy-done.22) | copy-start | bytes 24580
  214.3 0.7 copy-start.21
  214.3 359.6 %reduce-scatter.17.cloned.1.call-start = ((), (), s32[]{:S(2)}) async-start(), calls=%async_computation.6 | async-start | bytes 589824 | tf_op jit(solution)/shard_map/reduce_scatter | solution.py:193
  216.2 452.2 %all-reduce.10.cloned.1.call-start = ((), (), s32[]{:S(2)}) async-start(), calls=%async_computation.12 | async-start | bytes 9109504 | tf_op jit(solution)/shard_map/psum | solution.py:208
  668.3 2.5 copy-start.11
  675.0 3.4 copy-start.10
  675.0 4.1 copy-start.5
Sparse Core Ops, SparseCore 0:
  161.7 67.5 reduce-scatter.18
  233.0 60.8 reduce-scatter.24
  298.0 60.2 reduce-scatter.20
  361.6 65.2 reduce-scatter.26
  430.8 77.9 reduce-scatter.22
  512.3 61.4 reduce-scatter.16
  577.2 91.1 all-reduce.9
where the time goes:
time: 693 us; the launch traced here: 691 us
  waiting for transfers between devices  430 us (62%)
  matrix products  131 us (19%)
  starting transfers between devices  48.5 us (7%)
  local copies, waits for them, and re-layouts  39.4 us (6%)
  between operations  15.9 us (2%)
  blocking collectives  15.5 us (2%)
  other arithmetic  10.3 us (1%)
    unnamed x12, waiting for transfers between devices  269 us
    psum x1, waiting for transfers between devices, body(): lax.psum(part_enc.astype(jnp.bfloat16), 'section').astype(jnp.float32)  93.4 us
    reduce_scatter x1, waiting for transfers between devices, body(): lax.psum_scatter(grad_down.astype(jnp.bfloat16), 'space', scatter_dimensi...  62.5 us
    dot_general x108, matrix products, weight_grad(): lax.dot_general(window_part, flat_grad, (((0,), (0,)), ((), ())), preferr...  49.8 us
    dot_general x108, matrix products, convolve(): jnp.dot(window_part, weight[tap_index * width_in:(tap_index + 1) * width_...  40.3 us
    ppermute x7, starting transfers between devices, padded_2(): before = lax.ppermute(last, axis, up)  39.2 us
    dot_general x81, matrix products, transpose_conv(): lax.dot_general(window_part, block, (((1,), (1,)), ((), ())), preferred_e...  37.8 us
    unnamed x72, local copies, waits for them, and re-layouts  35.4 us
  transfers between devices with their start and end apart: 21, of which 13 were waited for; matrix products, arithmetic and copies ran while one was open for 10% of the time, Pallas kernels for 0%

commit v1 on v0

v1 whole, which is shorter than its diff:
```python
import functools
import math

import jax
import jax.numpy as jnp
import numpy as np
from jax import lax
from jax.experimental import pallas as pl
from jax.experimental.pallas import tpu as pltpu
from jax.sharding import PartitionSpec as P

BF = jnp.bfloat16
F32 = jnp.float32
LANES = 128


def dot(a, b):
    return jnp.dot(a, b, preferred_element_type=F32)


def dot_t(a, b):
    return lax.dot_general(a, b, (((1,), (1,)), ((), ())), preferred_element_type=F32)


def sigmoid(z):
    return 1.0 / (1.0 + jnp.exp(-z))


def silu(z):
    return (z * sigmoid(z)).astype(BF)


def slope(z):
    s = sigmoid(z)
    return s * (1.0 + z * (1.0 - s))


def windows(field, size_y, size_z):
    rows, width = field.shape
    place = lax.broadcasted_iota(jnp.int32, (rows, width), 0)
    at_z = lax.rem(place, size_z)
    at_y = lax.rem(lax.div(place, size_z), size_y)
    shifted = []
    for oz in (-1, 0, 1):
        part = field
        if oz:
            part = pltpu.roll(field, (-oz) % rows, 0)
            part = jnp.where(at_z == (size_z - 1 if oz > 0 else 0), 0.0, part)
        shifted.append(part)
    out = []
    for oy in (-1, 0, 1):
        for part in shifted:
            if oy:
                part = pltpu.roll(part, (-oy * size_z) % rows, 0)
                part = jnp.where(at_y == (size_y - 1 if oy > 0 else 0), 0.0, part)
            out.append(part)
    return out


def fill(u_ref, field, plane, sizes, offset=0, stride=None):
    rows, width = field.shape
    stride = width if stride is None else stride
    for t, part in enumerate(windows(field, *sizes)):
        lane = t * stride + offset
        u_ref[plane : plane + rows, lane : lane + width] = part.astype(BF)


def clear_rims(u_ref, plane):
    rows, lanes = u_ref.shape
    zero = jnp.zeros((plane, lanes), BF)
    u_ref[0:plane, :] = zero
    u_ref[rows - plane : rows, :] = zero


def conv(u_ref, w_ref, rows, plane):
    depth = u_ref.shape[1]
    total = None
    for ox in range(3):
        part = dot(u_ref[ox * plane : ox * plane + rows, :], w_ref[ox * depth : (ox + 1) * depth, :])
        total = part if total is None else total + part
    return total


def conv_back(u_ref, w_ref, rows, plane):
    width = w_ref.shape[0] // 27
    total = None
    for ox in range(3):
        taps = [(2 - ox) * 9 + 8 - t for t in range(9)]
        flipped = jnp.concatenate([w_ref[tap * width : (tap + 1) * width, :] for tap in taps], axis=1)
        part = dot_t(u_ref[ox * plane : ox * plane + rows, :], flipped)
        total = part if total is None else total + part
    return total


def own_rows(field, t_ref, count, position):
    t_ref[...] = field.T
    return t_ref[pl.ds(pl.multiple_of(position * count, count), count), :].astype(BF)


def to_blocks(shuffle, field, d_ref, pairs, plane):
    width = field.shape[1]
    for i in range(pairs):
        moved = dot(shuffle, field[i * 8 * plane : (i + 1) * 8 * plane]).astype(BF)
        for t in range(8):
            d_ref[i * plane : (i + 1) * plane, t * width : (t + 1) * width] = moved[
                t * plane : (t + 1) * plane
            ]


def from_blocks(unshuffle, flat, pairs, plane, width):
    parts = []
    for i in range(pairs):
        rows = flat[i * plane : (i + 1) * plane]
        stacked = jnp.concatenate([rows[:, t * width : (t + 1) * width] for t in range(8)], axis=0)
        parts.append(dot(unshuffle, stacked))
    return jnp.concatenate(parts, axis=0)


def step_kernel(
    geo,
    place_ref,
    near_ref,
    far_ref,
    shuffle_ref,
    unshuffle_ref,
    w_first,
    w_enc,
    w_down,
    w_bottom,
    w_up,
    w_join,
    decoded_ref,
    pack_ref,
    blocks,
    uv,
    u1,
    uj,
    ut,
    uc,
    utc,
    d_ref,
    lb_ref,
    wa,
    wb,
    out_map,
    tr_fine,
    tr_wide,
    tr_up,
    z1_ref,
    z2_ref,
):
    (n, sx, ny, nz, c0, c1, c2, masks, spots) = geo
    position = place_ref[0]
    plane, nx = ny * nz, sx * n
    rows = nx * plane
    cplane, cx = plane // 4, nx // 2
    crows = cx * cplane
    fine, coarse = (ny, nz), (ny // 2, nz // 2)
    half = n // 2 if n > 1 else 1
    for m, mask in enumerate(masks):
        source = near_ref if m < half else far_ref
        blocks[lax.bitwise_xor(position, mask)] = source[m % half]

    def emit(name, grad):
        at, _ = spots[name]
        count, width = grad.shape
        for v in range(0, width, LANES):
            piece = grad[:, v : v + LANES]
            if piece.shape[1] < LANES:
                piece = jnp.concatenate([piece, jnp.zeros((count, LANES - piece.shape[1]), F32)], 1)
            pack_ref[at : at + count, :] = piece.astype(BF)
            at += count

    lane = lax.broadcasted_iota(jnp.int32, (plane, LANES), 1)
    vol_rows = sx // 2 * plane
    pairs = [
        blocks[j, i * plane : (i + 1) * plane, :].astype(F32) for j in range(n) for i in range(sx // 2)
    ]
    turned = [pltpu.roll(p, c0, 1) for p in pairs]
    zero = jnp.zeros((plane, LANES), F32)
    beside = []
    for i in range(len(pairs) + 1):
        before = turned[i - 1] if i else zero
        after = turned[i] if i < len(pairs) else zero
        beside.append(jnp.where(lane < c0, before, after))
        if i < len(pairs):
            beside.append(pairs[i])
    fill(uv, jnp.concatenate(beside, 0), 0, fine)
    for t in range(9):
        a, b, c = [w_first[(ox * 9 + t) * c0 : (ox * 9 + t + 1) * c0, :] for ox in range(3)]
        wa[t * 2 * c0 : (t + 1) * 2 * c0, :] = jnp.concatenate([a, b], 0)
        wb[t * 2 * c0 : (t + 1) * 2 * c0, :] = jnp.concatenate([jnp.zeros_like(c), c], 0)
    z1 = dot(uv[0:rows, :], wa[...]) + dot(uv[plane : plane + rows, :], wb[...])
    z1_ref[...] = z1
    clear_rims(u1, plane)
    fill(u1, silu(z1).astype(F32), plane, fine)
    z2 = conv(u1, w_enc, rows, plane)
    z2_ref[...] = z2
    skip = silu(z2)
    clear_rims(uj, plane)
    fill(uj, skip.astype(F32), plane, fine, c1, 2 * c1)
    to_blocks(shuffle_ref[...], skip, d_ref, cx, cplane)
    z3 = dot(d_ref[...], w_down[...])
    clear_rims(uc, cplane)
    fill(uc, silu(z3).astype(F32), cplane, coarse)
    z4 = conv(uc, w_bottom, crows, cplane)
    g2 = silu(z4)
    lifted = from_blocks(unshuffle_ref[...], dot(g2, w_up[...]).astype(BF), cx, cplane, c1)
    fill(uj, lifted, plane, fine, 0, 2 * c1)
    z7 = conv(uj, w_join, rows, plane)
    out_map[...] = silu(z7)
    kept = sx * plane
    decoded_ref[...] = out_map[pl.ds(pl.multiple_of(position * kept, kept), kept), :]

    cot = jnp.concatenate([blocks[j, vol_rows:, :] for j in range(n)], 0).astype(F32)
    t7 = (cot * slope(z7)).astype(BF).astype(F32)
    clear_rims(ut, plane)
    fill(ut, t7, plane, fine)
    mine = own_rows(t7, tr_fine, c1 // n, position)
    depth = uj.shape[1]
    emit("join", jnp.concatenate([dot(mine, uj[ox * plane : ox * plane + rows, :]) for ox in range(3)], 1))
    b7 = conv_back(ut, w_join, rows, plane)
    e_lift = b7[:, :c1].astype(BF)
    e_skip = b7[:, c1:]

    to_blocks(shuffle_ref[...], e_lift, lb_ref, cx, cplane)
    mine = own_rows(lb_ref[...].astype(F32), tr_up, 8 * c1 // n, position)
    emit("up", dot(mine, g2))
    e3 = dot_t(lb_ref[...], w_up[...]).astype(BF).astype(F32)
    t4 = (e3 * slope(z4)).astype(BF).astype(F32)
    clear_rims(utc, cplane)
    fill(utc, t4, cplane, coarse)
    mine = own_rows(t4, tr_wide, c2 // n, position)
    emit("bottom", jnp.concatenate([dot(mine, uc[ox * cplane : ox * cplane + crows, :]) for ox in range(3)], 1))
    e4 = conv_back(utc, w_bottom, crows, cplane).astype(BF).astype(F32)
    t3 = (e4 * slope(z3)).astype(BF)
    mine = own_rows(t3.astype(F32), tr_wide, c2 // n, position)
    emit("down", dot(mine, d_ref[...]))
    e5 = dot_t(t3, w_down[...])
    high = e5.astype(BF)
    low = (e5 - high.astype(F32)).astype(BF)
    e5 = from_blocks(unshuffle_ref[...], high, cx, cplane, c1) + from_blocks(
        unshuffle_ref[...], low, cx, cplane, c1
    )
    t2 = ((e5 + e_skip) * slope(z2_ref[...])).astype(BF).astype(F32)
    fill(ut, t2, plane, fine)
    mine = own_rows(t2, tr_fine, c1 // n, position)
    emit("enc", jnp.concatenate([dot(mine, u1[ox * plane : ox * plane + rows, :]) for ox in range(3)], 1))
    e6 = conv_back(ut, w_enc, rows, plane).astype(BF).astype(F32)
    t1 = (e6 * slope(z1_ref[...])).astype(BF).astype(F32)
    mine = own_rows(t1, tr_fine, c1 // n, position)
    pair = dot(mine, uv[0:rows, :])
    last = dot(mine, uv[plane : plane + rows, :])
    halves = []
    for ox in range(3):
        for t in range(9):
            source = last if ox == 2 else pair
            halves.append((source[:, t * LANES : (t + 1) * LANES], ox > 0))
    if len(halves) % 2:
        halves.append((jnp.zeros_like(halves[0][0]), False))
    lane = lax.broadcasted_iota(jnp.int32, halves[0][0].shape, 1)
    packed = []
    for (a, a_high), (b, b_high) in zip(halves[::2], halves[1::2]):
        a = pltpu.roll(a, c0, 1) if a_high else a
        b = b if b_high else pltpu.roll(b, c0, 1)
        packed.append(jnp.where(lane < c0, a, b))
    emit("first", jnp.concatenate(packed, 1))


def finish_kernel(factor, order, spots, a_ref, b_ref, *outs):
    for name, out in zip(order, outs):
        at, _ = spots[name]
        count, width = out.shape
        for v in range(0, width, LANES):
            take = min(LANES, width - v)
            total = a_ref[at : at + count, :].astype(F32) + b_ref[at : at + count, :].astype(F32)
            out[:, v : v + take] = (total * factor)[:, :take]
            at += count


def exchange(array, axis, mask):
    devices = lax.axis_size(axis)
    return lax.ppermute(array, axis, [(i, i ^ mask) for i in range(devices)])


def one_hot_shuffle(ny, nz):
    plane = ny * nz
    shuffle = np.zeros((2 * plane, 2 * plane), np.float32)
    row = 0
    for ox in range(2):
        for oy in range(2):
            for oz in range(2):
                for y in range(ny // 2):
                    for z in range(nz // 2):
                        shuffle[row, ox * plane + (2 * y + oy) * nz + 2 * z + oz] = 1.0
                        row += 1
    return shuffle


def body(volume, w_first, w_enc, w_down, w_bottom, w_up, w_join, cotangent):
    n = lax.axis_size("space")
    crops = lax.axis_size("section")
    _, sx, ny, nz, c0 = volume.shape
    c1, c2 = w_enc.shape[1], w_bottom.shape[1]
    plane, nx = ny * nz, sx * n
    rows = nx * plane
    cplane, crows = plane // 4, rows // 8
    vol = volume.reshape(sx // 2, 2, plane, c0).transpose(0, 2, 1, 3).reshape(sx // 2 * plane, 2 * c0)
    near = jnp.concatenate([vol, cotangent.reshape(sx * plane, c1)], 0)[None]
    masks, step = [0], n // 2
    far = near
    while step:
        masks = masks + [m ^ step for m in masks]
        far = exchange(near, "space", step)
        step //= 2
        if step:
            near = jnp.concatenate([near, far], 0)

    order = ("first", "enc", "down", "bottom", "up", "join")
    shapes = {
        "first": (c1 // n, 27 * c0),
        "enc": (c1 // n, 27 * c1),
        "down": (c2 // n, 8 * c1),
        "bottom": (c2 // n, 27 * c2),
        "up": (8 * c1 // n, c2),
        "join": (c1 // n, 54 * c1),
    }
    spots, at = {}, 0
    for name in order:
        count, width = shapes[name]
        spots[name] = (at, count)
        at += count * -(-width // LANES)
    total_rows = -(-at // 32) * 32
    geo = (n, sx, ny, nz, c0, c1, c2, tuple(masks), spots)
    shuffle = one_hot_shuffle(ny, nz)
    position = lax.axis_index("space").astype(jnp.int32).reshape(1)
    whole = pl.BlockSpec(memory_space=pltpu.VMEM)
    decoded, pack = pl.pallas_call(
        functools.partial(step_kernel, geo),
        out_shape=(
            jax.ShapeDtypeStruct((sx * plane, c1), BF),
            jax.ShapeDtypeStruct((total_rows, LANES), BF),
        ),
        in_specs=[pl.BlockSpec(memory_space=pltpu.SMEM)] + [whole] * 10,
        out_specs=(whole, whole),
        scratch_shapes=[
            pltpu.VMEM((n,) + near.shape[1:], BF),
            pltpu.VMEM((rows + plane, 9 * 2 * c0), BF),
            pltpu.VMEM((rows + 2 * plane, 9 * c1), BF),
            pltpu.VMEM((rows + 2 * plane, 18 * c1), BF),
            pltpu.VMEM((rows + 2 * plane, 9 * c1), BF),
            pltpu.VMEM((crows + 2 * cplane, 9 * c2), BF),
            pltpu.VMEM((crows + 2 * cplane, 9 * c2), BF),
            pltpu.VMEM((crows, 8 * c1), BF),
            pltpu.VMEM((crows, 8 * c1), BF),
            pltpu.VMEM((18 * c0, c1), BF),
            pltpu.VMEM((18 * c0, c1), BF),
            pltpu.VMEM((rows, c1), BF),
            pltpu.VMEM((c1, rows), F32),
            pltpu.VMEM((c2, crows), F32),
            pltpu.VMEM((8 * c1, crows), F32),
            pltpu.VMEM((rows, c1), F32),
            pltpu.VMEM((rows, c1), F32),
        ],
        compiler_params=pltpu.CompilerParams(vmem_limit_bytes=58 * 1024 * 1024),
    )(
        position,
        near,
        far,
        jnp.asarray(shuffle, BF),
        jnp.asarray(shuffle.T, BF),
        w_first,
        w_enc,
        w_down,
        w_bottom,
        w_up,
        w_join,
    )
    mask = 1
    other = exchange(pack, "section", mask)
    while 2 * mask < crops:
        pack = (pack.astype(F32) + other.astype(F32)).astype(BF)
        mask *= 2
        other = exchange(pack, "section", mask)
    factor = 1.0 / math.sqrt(crops * rows)
    grads = pl.pallas_call(
        functools.partial(finish_kernel, factor, order, spots),
        out_shape=tuple(jax.ShapeDtypeStruct(shapes[name], F32) for name in order),
        in_specs=[whole, whole],
        out_specs=tuple(whole for _ in order),
        compiler_params=pltpu.CompilerParams(vmem_limit_bytes=40 * 1024 * 1024),
    )(pack, other)
    return (decoded.reshape((1, sx, ny, nz, c1)),) + tuple(g.T for g in grads)


def solution(mesh):
    field = P("section", "space", None, None, None)
    split = P(None, "space")
    return jax.shard_map(
        body,
        mesh=mesh,
        in_specs=(field,) + (P(),) * 6 + (field,),
        out_specs=(field,) + (split,) * 6,
        check_vma=False,
    )
```

time: 693 us -> 86.8 us (0.13)
  waiting for transfers between devices: 430 us -> 34.3 us
  matrix products: 131 us -> 0 us
  starting transfers between devices: 48.5 us -> 9.06 us
  Pallas kernels: 0 us -> 37.9 us
  local copies, waits for them, and re-layouts: 39.4 us -> 2.32 us
  blocking collectives: 15.5 us -> 0 us
  between operations: 15.9 us -> 0.66 us
  other arithmetic: 10.3 us -> 2.24 us
    unnamed x12 -> x0, waiting for transfers between devices: 269 us -> none
    dot_general x303 -> x0, matrix products: 131 us -> none  [the longest x108 49.8 us: weight_grad(): lax.dot_general(window_part, flat_grad, (((0,), (0,)), ((), ())), preferr...]
    psum x1 -> x0, waiting for transfers between devices: 93.4 us -> none  [body(): lax.psum(part_enc.astype(jnp.bfloat16), 'section').astype(jnp.float32)]
    reduce_scatter x1 -> x0, waiting for transfers between devices: 62.5 us -> none  [body(): lax.psum_scatter(grad_down.astype(jnp.bfloat16), 'space', scatter_dimensi...]
    ppermute x14 -> x5, starting transfers between devices: 48.2 us -> 9.06 us  [exchange(): return lax.ppermute(array, axis, [(i, i ^ mask) for i in range(devices)])]
    pallas_call x0 -> x2, Pallas kernels: none -> 37.9 us  [the longest x1 36.6 us: body(): pl.pallas_call(functools.partial(step_kernel, geo), out_shape=(jax.ShapeD...]
    unnamed x72 -> x5, local copies, waits for them, and re-layouts: 35.4 us -> 1.43 us
    ppermute x14 -> x5, waiting for transfers between devices: 5.16 us -> 34.3 us  [exchange(): return lax.ppermute(array, axis, [(i, i ^ mask) for i in range(devices)])]
  transfers between devices with their start and end apart: 21 -> 5, of which waited for: 13 -> 5; matrix products, arithmetic and copies ran while one was open for 10% -> 0% of each run, Pallas kernels for 0% -> 0%
where the time goes in v1:
time: 86.8 us; the launch traced here: 86.5 us
  Pallas kernels  37.9 us (44%)
  waiting for transfers between devices  34.3 us (40%)
  starting transfers between devices  9.06 us (10%)
  local copies, waits for them, and re-layouts  2.32 us (3%)
  other arithmetic  2.24 us (3%)
    pallas_call x1, Pallas kernels, body(): pl.pallas_call(functools.partial(step_kernel, geo), out_shape=(jax.ShapeD...  36.6 us
    ppermute x5, waiting for transfers between devices, exchange(): return lax.ppermute(array, axis, [(i, i ^ mask) for i in range(devices)])  34.3 us
    ppermute x5, starting transfers between devices, exchange(): return lax.ppermute(array, axis, [(i, i ^ mask) for i in range(devices)])  9.06 us
  transfers between devices with their start and end apart: 5, of which 5 were waited for; matrix products, arithmetic and copies ran while one was open for 0% of the time, Pallas kernels for 0%

profile of v1, /device:TPU:0, one launch (start us, length us, event | category | flops | bytes accessed | tf_op | source)
XLA Modules:
  0.0 86.5 jit_solution(9387643061747361538)
XLA Ops:
  0.6 0.8 copy.20
  1.4 0.1 reshape.31
  1.5 0.8 maximum_bitcast_fusion
  2.3 4.0 %collective-permute-start = (bf16[1,192,128]{2,1,0:T(8,128)(2,1)S(1)}, bf16[1,192,128]{2,1,0:T(8,128)(2,1)S(1)}, u32[]{:S(2)}, u32[]{:S(2)}) collective-permute-start(bf16[1,192,128]{2,1,0:T(8,128)(2,1)S(1)} %maximum_bitcast_fusion), channel_id=1, source_target_pairs={{0,4},{1,5},{2,6},{3,7},{4,0},{5,1},{6,2},{7,3},{8,12},{9,13},{10,... | collective-permute-start | bytes 147464 | tf_op jit(solution)/shard_map/ppermute | solution.py:283
  6.3 2.6 %collective-permute-done = bf16[1,192,128]{2,1,0:T(8,128)(2,1)S(1)} collective-permute-done((bf16[1,192,128]{2,1,0:T(8,128)(2,1)S(1)}, bf16[1,192,128]{2,1,0:T(8,128)(2,1)S(1)}, u32[]{:S(2)}, u32[]{:S(2)}) %collective-permute-start) | collective-permute-done | bytes 49184 | tf_op jit(solution)/shard_map/ppermute | solution.py:283
  8.9 1.4 %collective-permute-start.1 = (bf16[2,192,128]{2,1,0:T(8,128)(2,1)S(1)}, bf16[2,192,128]{2,1,0:T(8,128)(2,1)S(1)}, u32[]{:S(2)}, u32[]{:S(2)}) collective-permute-start(bf16[2,192,128]{2,1,0:T(8,128)(2,1)S(1)} %pad_maximum_fusion.1), channel_id=1, source_target_pairs={{0,2},{1,3},{2,0},{3,1},{4,6},{5,7},{6,4},{7,5},{8,10},{9,11},{10,... | collective-permute-start | bytes 294920 | tf_op jit(solution)/shard_map/ppermute | solution.py:283
  10.4 3.2 %collective-permute-done.1 = bf16[2,192,128]{2,1,0:T(8,128)(2,1)S(1)} collective-permute-done((bf16[2,192,128]{2,1,0:T(8,128)(2,1)S(1)}, bf16[2,192,128]{2,1,0:T(8,128)(2,1)S(1)}, u32[]{:S(2)}, u32[]{:S(2)}) %collective-permute-start.1) | collective-permute-done | bytes 98336 | tf_op jit(solution)/shard_map/ppermute | solution.py:283
  13.6 0.0 copy-start
  13.6 1.8 %collective-permute-start.2 = (bf16[4,192,128]{2,1,0:T(8,128)(2,1)S(1)}, bf16[4,192,128]{2,1,0:T(8,128)(2,1)S(1)}, u32[]{:S(2)}, u32[]{:S(2)}) collective-permute-start(bf16[4,192,128]{2,1,0:T(8,128)(2,1)S(1)} %pad_maximum_fusion.near_ref), channel_id=1, source_target_pairs={{0,1},{1,0},{2,3},{3,2},{4,5},{5,4},{6,7},{7,6},{8,9},{9,8},{10,11... | collective-permute-start | bytes 589832 | tf_op jit(solution)/shard_map/ppermute | solution.py:283
  15.4 3.9 %collective-permute-done.2.far_ref = bf16[4,192,128]{2,1,0:T(8,128)(2,1)S(1)} collective-permute-done((bf16[4,192,128]{2,1,0:T(8,128)(2,1)S(1)}, bf16[4,192,128]{2,1,0:T(8,128)(2,1)S(1)}, u32[]{:S(2)}, u32[]{:S(2)}) %collective-permute-start.2) | collective-permute-done | bytes 196640 | tf_op jit(solution)/shard_map/ppermute | solution.py:283
  19.4 0.0 copy-start.1
  19.4 0.0 copy-done
  19.4 0.7 copy-done.1
  20.1 36.6 %shard_map.153 = (bf16[128,128]{1,0:T(8,128)(2,1)}, bf16[3776,128]{1,0:T(8,128)(2,1)}) custom-call(s32[1]{0:T(128)} %bitcast.place_ref, bf16[4,192,128]{2,1,0:T(8,128)(2,1)} %copy-done, bf16[4,192,128]{2,1,0:T(8,128)(2,1)} %copy-done.1, bf16[128,128]{1,0:T(8,128)(2,1)} %constant.8.clone.shuffle_ref, bf16[128,128]{1,0:T(8,128)(2,1)} %constant.9.clone.unshuffle_ref, ...), custom_call_target="tpu_custom_call" | custom-call | tf_op jit(solution)/shard_map/pallas_call | solution.py:338
  56.6 0.0 collective-permute-start.3
  56.6 2.8 %collective-permute-done.3 = bf16[3776,128]{1,0:T(8,128)(2,1)S(1)} collective-permute-done((bf16[3776,128]{1,0:T(8,128)(2,1)}, bf16[3776,128]{1,0:T(8,128)(2,1)S(1)}, u32[]{:S(2)}, u32[]{:S(2)}) %collective-permute-start.3) | collective-permute-done | bytes 966688 | tf_op jit(solution)/shard_map/ppermute | solution.py:283
  59.4 1.4 %add_convert_fusion.a_ref = bf16[3776,128]{1,0:T(8,128)(2,1)S(1)} fusion(bf16[3776,128]{1,0:T(8,128)(2,1)S(1)} %collective-permute-done.3, bf16[3776,128]{1,0:T(8,128)(2,1)} %get-tuple-element.16), kind=kLoop, calls=%fused_computation | loop fusion | flops 1933312 | bytes 2899968 | tf_op jit(solution)/shard_map/convert_element_type | solution.py:382
  60.9 1.8 %collective-permute-start.4 = (bf16[3776,128]{1,0:T(8,128)(2,1)S(1)}, bf16[3776,128]{1,0:T(8,128)(2,1)S(1)}, u32[]{:S(2)}, u32[]{:S(2)}) collective-permute-start(bf16[3776,128]{1,0:T(8,128)(2,1)S(1)} %add_convert_fusion.a_ref), channel_id=1, source_target_pairs={{0,16},{8,24},{16,0},{24,8},{1,17},{9,25},{17,1},{25,9},{2,18},{10... | collective-permute-start | bytes 2899976 | tf_op jit(solution)/shard_map/ppermute | solution.py:283
  62.6 21.7 %collective-permute-done.4.b_ref = bf16[3776,128]{1,0:T(8,128)(2,1)S(1)} collective-permute-done((bf16[3776,128]{1,0:T(8,128)(2,1)S(1)}, bf16[3776,128]{1,0:T(8,128)(2,1)S(1)}, u32[]{:S(2)}, u32[]{:S(2)}) %collective-permute-start.4) | collective-permute-done | bytes 966688 | tf_op jit(solution)/shard_map/ppermute | solution.py:283
  84.4 1.4 %shard_map.154 = (f32[16,1728]{1,0:T(8,128)}, f32[16,3456]{1,0:T(8,128)}, f32[32,1024]{1,0:T(8,128)}, f32[32,6912]{1,0:T(8,128)}, f32[128,256]{1,0:T(8,128)S(1)}, /*index=5*/f32[16,6912]{1,0:T(8,128)}) custom-call(bf16[3776,128]{1,0:T(8,128)(2,1)S(1)} %add_convert_fusion.a_ref, bf16[3776,128]{1,0:T(8,128)(2,1)S(1)} %collective-permute-done.4.b_ref), custom_call_target="tpu_custom_call" | custom-call | tf_op jit(solution)/shard_map/pallas_call | solution.py:386
  85.7 0.8 copy.18
  (2 shorter events, 0.0 us)
Async XLA Ops:
  2.3 6.6 %collective-permute-start = (bf16[1,192,128]{2,1,0:T(8,128)(2,1)S(1)}, bf16[1,192,128]{2,1,0:T(8,128)(2,1)S(1)}, u32[]{:S(2)}, u32[]{:S(2)}) collective-permute-start(bf16[1,192,128]{2,1,0:T(8,128)(2,1)S(1)} %maximum_bitcast_fusion), channel_id=1, source_target_pairs={{0,4},{1,5},{2,6},{3,7},{4,0},{5,1},{6,2},{7,3},{8,12},{9,13},{10,... | collective-permute-start | bytes 147464 | tf_op jit(solution)/shard_map/ppermute | solution.py:283
  8.9 4.7 %collective-permute-start.1 = (bf16[2,192,128]{2,1,0:T(8,128)(2,1)S(1)}, bf16[2,192,128]{2,1,0:T(8,128)(2,1)S(1)}, u32[]{:S(2)}, u32[]{:S(2)}) collective-permute-start(bf16[2,192,128]{2,1,0:T(8,128)(2,1)S(1)} %pad_maximum_fusion.1), channel_id=1, source_target_pairs={{0,2},{1,3},{2,0},{3,1},{4,6},{5,7},{6,4},{7,5},{8,10},{9,11},{10,... | collective-permute-start | bytes 294920 | tf_op jit(solution)/shard_map/ppermute | solution.py:283
  13.6 5.8 %copy-start = (bf16[4,192,128]{2,1,0:T(8,128)(2,1)}, bf16[4,192,128]{2,1,0:T(8,128)(2,1)S(1)}, u32[]{:S(2)}) copy-start(bf16[4,192,128]{2,1,0:T(8,128)(2,1)S(1)} %pad_maximum_fusion.near_ref) | copy-start | bytes 589828
  13.6 5.7 %collective-permute-start.2 = (bf16[4,192,128]{2,1,0:T(8,128)(2,1)S(1)}, bf16[4,192,128]{2,1,0:T(8,128)(2,1)S(1)}, u32[]{:S(2)}, u32[]{:S(2)}) collective-permute-start(bf16[4,192,128]{2,1,0:T(8,128)(2,1)S(1)} %pad_maximum_fusion.near_ref), channel_id=1, source_target_pairs={{0,1},{1,0},{2,3},{3,2},{4,5},{5,4},{6,7},{7,6},{8,9},{9,8},{10,11... | collective-permute-start | bytes 589832 | tf_op jit(solution)/shard_map/ppermute | solution.py:283
  19.4 0.7 copy-start.1
  56.6 2.8 %collective-permute-start.3 = (bf16[3776,128]{1,0:T(8,128)(2,1)}, bf16[3776,128]{1,0:T(8,128)(2,1)S(1)}, u32[]{:S(2)}, u32[]{:S(2)}) collective-permute-start(bf16[3776,128]{1,0:T(8,128)(2,1)} %get-tuple-element.16), channel_id=1, source_target_pairs={{0,8},{8,0},{16,24},{24,16},{1,9},{9,1},{17,25},{25,17},{2,10},{10... | collective-permute-start | bytes 2899976 | tf_op jit(solution)/shard_map/ppermute | solution.py:283
  60.9 23.5 %collective-permute-start.4 = (bf16[3776,128]{1,0:T(8,128)(2,1)S(1)}, bf16[3776,128]{1,0:T(8,128)(2,1)S(1)}, u32[]{:S(2)}, u32[]{:S(2)}) collective-permute-start(bf16[3776,128]{1,0:T(8,128)(2,1)S(1)} %add_convert_fusion.a_ref), channel_id=1, source_target_pairs={{0,16},{8,24},{16,0},{24,8},{1,17},{9,25},{17,1},{25,9},{2,18},{10... | collective-permute-start | bytes 2899976 | tf_op jit(solution)/shard_map/ppermute | solution.py:283

commit v2 on v1

v2 whole, which is shorter than its diff:
```python
import functools
import math

import jax
import jax.numpy as jnp
import numpy as np
from jax import lax
from jax.experimental import pallas as pl
from jax.experimental.pallas import tpu as pltpu
from jax.sharding import PartitionSpec as P

BF = jnp.bfloat16
F32 = jnp.float32
LANES = 128
MIB = 1024 * 1024


def dot(a, b):
    return jnp.dot(a, b, preferred_element_type=F32)


def dot_t(a, b):
    return lax.dot_general(a, b, (((1,), (1,)), ((), ())), preferred_element_type=F32)


def sigmoid(z):
    return 1.0 / (1.0 + jnp.exp(-z))


def silu(z):
    return (z * sigmoid(z)).astype(BF)


def slope(z):
    s = sigmoid(z)
    return s * (1.0 + z * (1.0 - s))


def z_windows(field, size_z):
    rows = field.shape[0]
    at_z = lax.rem(lax.broadcasted_iota(jnp.int32, field.shape, 0), size_z)
    out = []
    for oz in (-1, 0, 1):
        part = field
        if oz:
            part = pltpu.roll(field, (-oz) % rows, 0)
            part = jnp.where(at_z == (size_z - 1 if oz > 0 else 0), 0.0, part)
        out.append(part)
    return out


def yz_windows(field, size_y, size_z):
    rows = field.shape[0]
    place = lax.broadcasted_iota(jnp.int32, field.shape, 0)
    at_y = lax.rem(lax.div(place, size_z), size_y)
    shifted = z_windows(field, size_z)
    out = []
    for oy in (-1, 0, 1):
        for part in shifted:
            if oy:
                part = pltpu.roll(part, (-oy * size_z) % rows, 0)
                part = jnp.where(at_y == (size_y - 1 if oy > 0 else 0), 0.0, part)
            out.append(part)
    return out


def fill(u_ref, parts, plane=0, offset=0, stride=None):
    rows, width = parts[0].shape
    stride = width if stride is None else stride
    for t, part in enumerate(parts):
        lane = t * stride + offset
        u_ref[plane : plane + rows, lane : lane + width] = part.astype(BF)


def clear_rims(u_ref, plane):
    rows, lanes = u_ref.shape
    zero = jnp.zeros((plane, lanes), BF)
    u_ref[0:plane, :] = zero
    u_ref[rows - plane : rows, :] = zero


def moved(field, ox, oy):
    nx, ny, nz, width = field.shape
    if ox:
        rim = jnp.zeros((1, ny, nz, width), F32)
        field = jnp.concatenate([field[1:], rim] if ox > 0 else [rim, field[:-1]], 0)
    if oy:
        rim = jnp.zeros((nx, 1, nz, width), F32)
        field = jnp.concatenate([field[:, 1:], rim] if oy > 0 else [rim, field[:, :-1]], 1)
    return field


def grouped(width, extent, product):
    total = None
    for first in range(0, 9, 2):
        groups = [first, first + 1] if first < 8 else [first]
        both = product(groups)
        for i, g in enumerate(groups):
            part = both[:, i * width : (i + 1) * width].reshape(extent + (width,))
            part = moved(part, g // 3 - 1, g % 3 - 1)
            total = part if total is None else total + part
    return total.reshape(-1, width)


def conv_z(uz, w_ref, extent):
    depth = w_ref.shape[0] // 9

    def product(groups):
        side = [w_ref[g * depth : (g + 1) * depth, :] for g in groups]
        return dot(uz, side[0] if len(side) == 1 else jnp.concatenate(side, 1))

    return grouped(w_ref.shape[1], extent, product)


def conv_z_back(uz, w_ref, extent):
    width = w_ref.shape[0] // 27

    def product(groups):
        side = []
        for g in groups:
            taps = [(8 - g) * 3 + 2 - t for t in range(3)]
            side.append(jnp.concatenate([w_ref[p * width : (p + 1) * width, :] for p in taps], 1))
        return dot_t(uz, side[0] if len(side) == 1 else jnp.concatenate(side, 0))

    return grouped(width, extent, product)


def conv(u_ref, w_ref, rows, plane):
    depth = u_ref.shape[1]
    total = None
    for ox in range(3):
        part = dot(u_ref[ox * plane : ox * plane + rows, :], w_ref[ox * depth : (ox + 1) * depth, :])
        total = part if total is None else total + part
    return total


def conv_back(u_ref, w_ref, rows, plane):
    width = w_ref.shape[0] // 27
    total = None
    for ox in range(3):
        taps = [(2 - ox) * 9 + 8 - t for t in range(9)]
        flipped = jnp.concatenate([w_ref[tap * width : (tap + 1) * width, :] for tap in taps], axis=1)
        part = dot_t(u_ref[ox * plane : ox * plane + rows, :], flipped)
        total = part if total is None else total + part
    return total


def own_columns(field, count, position):
    shape = (count, field.shape[1])
    wanted = lax.broadcasted_iota(jnp.int32, shape, 0) + position * count
    pick = (lax.broadcasted_iota(jnp.int32, shape, 1) == wanted).astype(F32).astype(BF)
    return dot_t(pick, field)


def tap_grad(grad, field, extent):
    nx, ny, nz = extent
    count, rows = grad.shape
    place = lax.broadcasted_iota(jnp.int32, grad.shape, 1)
    at = (lax.div(place, ny * nz), lax.rem(lax.div(place, nz), ny), lax.rem(place, nz))
    parts = []
    for ox in (-1, 0, 1):
        for oy in (-1, 0, 1):
            for oz in (-1, 0, 1):
                by = ((ox * ny) + oy) * nz + oz
                part = pltpu.roll(grad, by % rows, 1) if by else grad
                inside = None
                for index, size, o in zip(at, extent, (ox, oy, oz)):
                    if o:
                        here = index != (0 if o > 0 else size - 1)
                        inside = here if inside is None else inside & here
                parts.append(part if inside is None else jnp.where(inside, part, 0.0))
    return dot(jnp.concatenate(parts, 0).astype(BF), field)


def emit(pack_ref, spot, grad, taps=1):
    count, width = grad.shape[0] // taps, grad.shape[1]
    at = spot
    if width == LANES:
        pack_ref[at : at + taps * count, :] = grad.astype(BF)
        return
    for tap in range(taps):
        for v in range(0, width, LANES):
            pack_ref[at : at + count, :] = grad[tap * count : (tap + 1) * count, v : v + LANES].astype(BF)
            at += count


def to_blocks(shuffle, field, d_ref, pairs, plane):
    width = field.shape[1]
    for i in range(pairs):
        mixed = dot(shuffle, field[i * 8 * plane : (i + 1) * 8 * plane]).astype(BF)
        for t in range(8):
            d_ref[i * plane : (i + 1) * plane, t * width : (t + 1) * width] = mixed[
                t * plane : (t + 1) * plane
            ]


def from_blocks(unshuffle, flat, pairs, plane, width):
    parts = []
    for i in range(pairs):
        rows = flat[i * plane : (i + 1) * plane]
        stacked = jnp.concatenate([rows[:, t * width : (t + 1) * width] for t in range(8)], axis=0)
        parts.append(dot(unshuffle, stacked))
    return jnp.concatenate(parts, axis=0)


def upper_kernel(
    geo,
    place_ref,
    near_ref,
    far_ref,
    shuffle_ref,
    unshuffle_ref,
    w_first,
    w_enc,
    w_down,
    w_bottom,
    w_up,
    w_join,
    decoded_ref,
    keep_ref,
    send_ref,
    vol_ref,
    z1_ref,
    h1_ref,
    z2_ref,
    d_ref,
    z3_ref,
    t4_ref,
    skip_back_ref,
    blocks,
    uv,
    u1,
    uj,
    ut,
    uc,
    joined,
    lb_ref,
    out_map,
    pack,
):
    (n, sx, ny, nz, c0, c1, c2, masks, spots) = geo
    position = place_ref[0]
    plane, nx = ny * nz, sx * n
    rows = nx * plane
    cplane, cx = plane // 4, nx // 2
    crows = cx * cplane
    fine, coarse = (nx, ny, nz), (cx, ny // 2, nz // 2)
    half = n // 2 if n > 1 else 1
    for m, mask in enumerate(masks):
        source = near_ref if m < half else far_ref
        blocks[lax.bitwise_xor(position, mask)] = source[m % half]

    lane = lax.broadcasted_iota(jnp.int32, (plane, LANES), 1)
    vol_rows = sx // 2 * plane
    planes = []
    for j in range(n):
        for i in range(sx // 2):
            pair = blocks[j, i * plane : (i + 1) * plane, :].astype(F32)
            turned = pltpu.roll(pair, c0, 1)
            planes.append(jnp.where(lane < c0, pair, turned))
            planes.append(jnp.where(lane < c0, turned, pair))
    twice = jnp.concatenate(planes, 0)
    vol_ref[...] = twice.astype(BF)
    before, middle, after = z_windows(twice, nz)
    lane = lax.broadcasted_iota(jnp.int32, (rows, LANES), 1)
    uv[:, 0:LANES] = jnp.where(lane < c0, before, middle).astype(BF)
    uv[:, LANES:] = after.astype(BF)
    z1 = conv_z(uv[:, 0 : 3 * c0], w_first, fine)
    z1_ref[...] = z1
    h1 = silu(z1)
    h1_ref[...] = h1
    fill(u1, z_windows(h1.astype(F32), nz))
    z2 = conv_z(u1[...], w_enc, fine)
    z2_ref[...] = z2
    skip = silu(z2)
    joined[:, c1:] = skip
    fill(uj, z_windows(skip.astype(F32), nz), 0, c1, 2 * c1)
    to_blocks(shuffle_ref[...], skip, d_ref, cx, cplane)
    z3 = dot(d_ref[...], w_down[...])
    z3_ref[...] = z3
    g1 = silu(z3)
    clear_rims(uc, cplane)
    fill(uc, yz_windows(g1.astype(F32), *coarse[1:]), cplane)
    z4 = conv(uc, w_bottom, crows, cplane)
    g2 = silu(z4)
    lifted = from_blocks(unshuffle_ref[...], dot(g2, w_up[...]).astype(BF), cx, cplane, c1)
    joined[:, 0:c1] = lifted.astype(BF)
    fill(uj, z_windows(lifted, nz), 0, 0, 2 * c1)
    z7 = conv_z(uj[...], w_join, fine)
    out_map[...] = silu(z7)
    kept = sx * plane
    decoded_ref[...] = out_map[pl.ds(pl.multiple_of(position * kept, kept), kept), :]

    cot = jnp.concatenate([blocks[j, vol_rows:, :] for j in range(n)], 0).astype(F32)
    t7 = (cot * slope(z7)).astype(BF)
    clear_rims(ut, plane)
    fill(ut, yz_windows(t7.astype(F32), ny, nz), plane)
    emit(pack, spots["join"], tap_grad(own_columns(t7, c1 // n, position), joined[...], fine), 27)
    b7 = conv_back(ut, w_join, rows, plane)
    skip_back_ref[...] = b7[:, c1:]

    to_blocks(shuffle_ref[...], b7[:, :c1].astype(BF), lb_ref, cx, cplane)
    emit(pack, spots["up"], dot(own_columns(lb_ref[...], 8 * c1 // n, position).astype(BF), g2))
    e3 = dot_t(lb_ref[...], w_up[...]).astype(BF).astype(F32)
    t4 = (e3 * slope(z4)).astype(BF)
    t4_ref[...] = t4
    emit(pack, spots["bottom"], tap_grad(own_columns(t4, c2 // n, position), g1, coarse), 27)
    core = place_ref[1]
    size = keep_ref.shape[0]
    keep_ref[...] = pack[pl.ds(pl.multiple_of(core * size, size), size), :]
    send_ref[...] = pack[pl.ds(pl.multiple_of((1 - core) * size, size), size), :]


def lower_kernel(
    geo,
    place_ref,
    unshuffle_ref,
    w_enc,
    w_down,
    w_bottom,
    vol_ref,
    z1_ref,
    h1_ref,
    z2_ref,
    d_ref,
    z3_ref,
    t4_ref,
    skip_back_ref,
    pack,
    utc,
    ut,
):
    (n, sx, ny, nz, c0, c1, c2, masks, spots) = geo
    position = place_ref[0]
    plane, nx = ny * nz, sx * n
    cplane, cx = plane // 4, nx // 2
    crows = cx * cplane
    fine, coarse = (nx, ny, nz), (cx, ny // 2, nz // 2)
    clear_rims(utc, cplane)
    fill(utc, yz_windows(t4_ref[...].astype(F32), *coarse[1:]), cplane)
    e4 = conv_back(utc, w_bottom, crows, cplane).astype(BF).astype(F32)
    t3 = (e4 * slope(z3_ref[...])).astype(BF)
    emit(pack, spots["down"], dot(own_columns(t3, c2 // n, position).astype(BF), d_ref[...]))
    e5 = dot_t(t3, w_down[...])
    high = e5.astype(BF)
    low = (e5 - high.astype(F32)).astype(BF)
    e5 = from_blocks(unshuffle_ref[...], high, cx, cplane, c1) + from_blocks(
        unshuffle_ref[...], low, cx, cplane, c1
    )
    t2 = ((e5 + skip_back_ref[...]) * slope(z2_ref[...])).astype(BF)
    fill(ut, z_windows(t2.astype(F32), nz))
    emit(pack, spots["enc"], tap_grad(own_columns(t2, c1 // n, position), h1_ref[...], fine), 27)
    e6 = conv_z_back(ut[...], w_enc, fine).astype(BF).astype(F32)
    t1 = (e6 * slope(z1_ref[...])).astype(BF)
    count = c1 // n
    taps = tap_grad(own_columns(t1, count, position), vol_ref[...], fine)
    lane = lax.broadcasted_iota(jnp.int32, (count, LANES), 1)
    at = spots["first"]
    for tap in range(0, 27, 2):
        a = taps[tap * count : (tap + 1) * count]
        b = taps[(tap + 1) * count : (tap + 2) * count] if tap < 26 else a
        pack[at : at + count, :] = jnp.where(lane < c0, a, b).astype(BF)
        at += count


def unpack(source, spot, out, factor):
    count, width = out.shape
    at = spot
    for v in range(0, width, LANES):
        take = min(LANES, width - v)
        out[:, v : v + take] = (source(at, count) * factor)[:, :take]
        at += count


def finish_first(factor, spots, place_ref, mine_ref, other_ref, bottom_ref, up_ref, join_ref, both):
    core = place_ref[1]
    both[core] = mine_ref[...]
    both[1 - core] = other_ref[...]
    size = mine_ref.shape[0]

    def source(at, count):
        if (at + count - 1) // size == at // size:
            return both[at // size, at % size : at % size + count, :].astype(F32)
        cut = size - at % size
        return jnp.concatenate(
            [both[0, size - cut : size, :].astype(F32), both[1, 0 : count - cut, :].astype(F32)], 0
        )

    unpack(source, spots["bottom"], bottom_ref, factor)
    unpack(source, spots["join"], join_ref, factor)
    rows, width = up_ref.shape[1], up_ref.shape[0]
    for v in range(0, width, LANES):
        up_ref[v : v + LANES, :] = (source(spots["up"] + v // LANES * rows, rows) * factor).T


def finish_second(factor, spots, a_ref, b_ref, first_ref, enc_ref, down_ref):
    def source(at, count):
        return a_ref[at : at + count, :].astype(F32) + b_ref[at : at + count, :].astype(F32)

    unpack(source, spots["first"], first_ref, factor)
    unpack(source, spots["enc"], enc_ref, factor)
    unpack(source, spots["down"], down_ref, factor)


def exchange(array, axis, mask):
    devices = lax.axis_size(axis)
    return lax.ppermute(array, axis, [(i, i ^ mask) for i in range(devices)])


def add(a, b):
    return (a.astype(F32) + b.astype(F32)).astype(BF)


def one_hot_shuffle(ny, nz):
    plane = ny * nz
    shuffle = np.zeros((2 * plane, 2 * plane), np.float32)
    row = 0
    for ox in range(2):
        for oy in range(2):
            for oz in range(2):
                for y in range(ny // 2):
                    for z in range(nz // 2):
                        shuffle[row, ox * plane + (2 * y + oy) * nz + 2 * z + oz] = 1.0
                        row += 1
    return shuffle


def call(kernel, outs, scratch, scalars, flops=0, vmem=30):
    whole = pl.BlockSpec(memory_space=pltpu.VMEM)

    def run(*args):
        specs = [pl.BlockSpec(memory_space=pltpu.SMEM)] * scalars + [whole] * (len(args) - scalars)
        return pl.pallas_call(
            kernel,
            out_shape=tuple(jax.ShapeDtypeStruct(s, d) for s, d in outs),
            in_specs=specs,
            out_specs=tuple(whole for _ in outs),
            scratch_shapes=[pltpu.VMEM(s, d) for s, d in scratch],
            compiler_params=pltpu.CompilerParams(vmem_limit_bytes=vmem * MIB),
            cost_estimate=pl.CostEstimate(flops=flops, bytes_accessed=2 * MIB, transcendentals=0),
        )(*args)

    return run


def body(volume, w_first, w_enc, w_down, w_bottom, w_up, w_join, cotangent):
    n = lax.axis_size("space")
    crops = lax.axis_size("section")
    _, sx, ny, nz, c0 = volume.shape
    c1, c2 = w_enc.shape[1], w_bottom.shape[1]
    plane, nx = ny * nz, sx * n
    rows = nx * plane
    cplane, crows = plane // 4, rows // 8
    vol = volume.reshape(sx // 2, 2, plane, c0).transpose(0, 2, 1, 3).reshape(sx // 2 * plane, 2 * c0)
    near = jnp.concatenate([vol, cotangent.reshape(sx * plane, c1)], 0)[None]
    masks, step = [0], n // 2
    far = near
    while step:
        masks = masks + [m ^ step for m in masks]
        far = exchange(near, "space", step)
        step //= 2
        if step:
            near = jnp.concatenate([near, far], 0)

    fine_own, wide_own = c1 // n, c2 // n
    shapes = {
        "first": (fine_own, 27 * c0),
        "enc": (fine_own, 27 * c1),
        "down": (wide_own, 8 * c1),
        "bottom": (wide_own, 27 * c2),
        "up": (8 * c1 // n, c2),
        "join": (fine_own, 54 * c1),
    }

    def layout(names):
        spots, at = {}, 0
        for name in names:
            spots[name] = at
            count, width = shapes[name]
            at += count * -(-width // LANES)
        return spots, -(-at // 32) * 32

    upper_spots, upper_rows = layout(("bottom", "up", "join"))
    lower_spots, lower_rows = layout(("down", "enc", "first"))
    geo = (n, sx, ny, nz, c0, c1, c2, tuple(masks))
    shuffle = one_hot_shuffle(ny, nz)
    unshuffle = jnp.asarray(shuffle.T, BF)
    shuffle = jnp.asarray(shuffle, BF)
    section = lax.axis_index("section")
    place = jnp.stack([lax.axis_index("space"), section % 2]).astype(jnp.int32)
    size = upper_rows // 2
    decoded, keep, send, vol2, z1, h1, z2, blocks, z3, t4, skip_back = call(
        functools.partial(upper_kernel, geo + (upper_spots,)),
        [
            ((sx * plane, c1), BF),
            ((size, LANES), BF),
            ((size, LANES), BF),
            ((rows, 2 * c0), BF),
            ((rows, c1), F32),
            ((rows, c1), BF),
            ((rows, c1), F32),
            ((crows, 8 * c1), BF),
            ((crows, c2), F32),
            ((crows, c2), BF),
            ((rows, c1), F32),
        ],
        [
            ((n,) + near.shape[1:], BF),
            ((rows, 2 * LANES), BF),
            ((rows, 3 * c1), BF),
            ((rows, 6 * c1), BF),
            ((rows + 2 * plane, 9 * c1), BF),
            ((crows + 2 * cplane, 9 * c2), BF),
            ((rows, 2 * c1), BF),
            ((crows, 8 * c1), BF),
            ((rows, c1), BF),
            ((upper_rows, LANES), BF),
        ],
        1,
        flops=10**10,
    )(place, near, far, shuffle, unshuffle, w_first, w_enc, w_down, w_bottom, w_up, w_join)
    total = add(keep, exchange(send, "section", 1))
    mask = 2
    while mask < crops:
        total = add(total, exchange(total, "section", mask))
        mask *= 2
    other = exchange(total, "section", 1)

    (pack,) = call(
        functools.partial(lower_kernel, geo + (lower_spots,)),
        [((lower_rows, LANES), BF)],
        [((crows + 2 * cplane, 9 * c2), BF), ((rows, 3 * c1), BF)],
        1,
        flops=6 * 10**9,
    )(place, unshuffle, w_enc, w_down, w_bottom, vol2, z1, h1, z2, blocks, z3, t4, skip_back)
    mask = 1
    pack_other = exchange(pack, "section", mask)
    while 2 * mask < crops:
        pack = add(pack, pack_other)
        mask *= 2
        pack_other = exchange(pack, "section", mask)

    factor = 1.0 / math.sqrt(crops * rows)
    grad_bottom, grad_up, grad_join = call(
        functools.partial(finish_first, factor, upper_spots),
        [(shapes["bottom"], F32), (shapes["up"][::-1], F32), (shapes["join"], F32)],
        [((2, size, LANES), BF)],
        1,
    )(place, total, other)
    grad_first, grad_enc, grad_down = call(
        functools.partial(finish_second, factor, lower_spots),
        [(shapes[name], F32) for name in ("first", "enc", "down")],
        [],
        0,
    )(pack, pack_other)
    return (
        decoded.reshape((1, sx, ny, nz, c1)),
        grad_first.T,
        grad_enc.T,
        grad_down.T,
        grad_bottom.T,
        grad_up,
        grad_join.T,
    )


def solution(mesh):
    field = P("section", "space", None, None, None)
    split = P(None, "space")
    return jax.shard_map(
        body,
        mesh=mesh,
        in_specs=(field,) + (P(),) * 6 + (field,),
        out_specs=(field,) + (split,) * 6,
        check_vma=False,
    )
```

time: 86.8 us -> 67.3 us (0.78)
  waiting for transfers between devices: 34.3 us -> 19.3 us
  Pallas kernels: 37.9 us -> 24.4 us
  local copies, waits for them, and re-layouts: 2.32 us -> 10.1 us
  starting transfers between devices: 9.06 us -> 11 us
  other arithmetic: 2.24 us -> 1.13 us
    ppermute x5 -> x8, waiting for transfers between devices: 34.3 us -> 19.3 us  [exchange(): return lax.ppermute(array, axis, [(i, i ^ mask) for i in range(devices)])]
    pallas_call x2 -> x4, Pallas kernels: 37.9 us -> 24.4 us  [run(): pl.pallas_call(kernel, out_shape=tuple((jax.ShapeDtypeStruct(s, d) for s,...]
    unnamed x5 -> x20, local copies, waits for them, and re-layouts: 1.43 us -> 9.26 us
    ppermute x5 -> x8, starting transfers between devices: 9.06 us -> 11 us  [exchange(): return lax.ppermute(array, axis, [(i, i ^ mask) for i in range(devices)])]
    convert_element_type x1 -> x3, other arithmetic: 1.45 us -> 0.26 us  [add(): return (a.astype(F32) + b.astype(F32)).astype(BF)]
  transfers between devices with their start and end apart: 5 -> 8, of which waited for: 5 -> 6; matrix products, arithmetic and copies ran while one was open for 0% -> 0% of each run, Pallas kernels for 0% -> 12%
where the time goes in v2:
time: 67.3 us; the launch traced here: 66.7 us
  Pallas kernels  24.4 us (36%)
  waiting for transfers between devices  19.3 us (29%)
  starting transfers between devices  11 us (16%)
  local copies, waits for them, and re-layouts  10.1 us (15%)
  other arithmetic  1.13 us (2%)
  between operations  0.72 us (1%)
    pallas_call x4, Pallas kernels, run(): pl.pallas_call(kernel, out_shape=tuple((jax.ShapeDtypeStruct(s, d) for s,...  24.4 us
    ppermute x8, waiting for transfers between devices, exchange(): return lax.ppermute(array, axis, [(i, i ^ mask) for i in range(devices)])  19.3 us
    ppermute x8, starting transfers between devices, exchange(): return lax.ppermute(array, axis, [(i, i ^ mask) for i in range(devices)])  11 us
    unnamed x20, local copies, waits for them, and re-layouts  9.26 us
  transfers between devices with their start and end apart: 8, of which 6 were waited for; matrix products, arithmetic and copies ran while one was open for 0% of the time, Pallas kernels for 12%

profile of v2, /device:TPU:0, one launch (start us, length us, event | category | flops | bytes accessed | tf_op | source)
XLA Modules:
  0.0 66.7 jit_solution(7360907780511221303)
XLA Ops:
  0.6 0.8 %copy.19 = bf16[1,2,64,64]{3,1,2,0:T(2,128)(2,1)S(1)} copy(bf16[1,2,64,64]{3,2,1,0:T(8,128)(2,1)} %bitcast.17) | data formatting | bytes 32768 | tf_op jit(solution)/shard_map/reshape | solution.py:454
  1.4 0.1 reshape.27
  1.5 0.8 %maximum_bitcast_fusion = bf16[1,192,128]{2,1,0:T(8,128)(2,1)S(1)} fusion(bf16[128,128]{1,0:T(8,128)(2,1)} %bitcast.16, bf16[64,128]{1,0:T(8,128)(2,1)S(1)} %reshape.27), kind=kLoop, calls=%fused_computation.5 | loop fusion | flops 98304 | bytes 98304 | tf_op jit(solution)/shard_map/broadcast_in_dim | solution.py:455
  2.3 4.0 %collective-permute-start = (bf16[1,192,128]{2,1,0:T(8,128)(2,1)S(1)}, bf16[1,192,128]{2,1,0:T(8,128)(2,1)S(1)}, u32[]{:S(2)}, u32[]{:S(2)}) collective-permute-start(bf16[1,192,128]{2,1,0:T(8,128)(2,1)S(1)} %maximum_bitcast_fusion), channel_id=1, source_target_pairs={{0,4},{1,5},{2,6},{3,7},{4,0},{5,1},{6,2},{7,3},{8,12},{9,13},{10,... | collective-permute-start | bytes 147464 | tf_op jit(solution)/shard_map/ppermute | solution.py:407
  6.3 2.6 %collective-permute-done = bf16[1,192,128]{2,1,0:T(8,128)(2,1)S(1)} collective-permute-done((bf16[1,192,128]{2,1,0:T(8,128)(2,1)S(1)}, bf16[1,192,128]{2,1,0:T(8,128)(2,1)S(1)}, u32[]{:S(2)}, u32[]{:S(2)}) %collective-permute-start) | collective-permute-done | bytes 49184 | tf_op jit(solution)/shard_map/ppermute | solution.py:407
  8.9 1.4 %collective-permute-start.1 = (bf16[2,192,128]{2,1,0:T(8,128)(2,1)S(1)}, bf16[2,192,128]{2,1,0:T(8,128)(2,1)S(1)}, u32[]{:S(2)}, u32[]{:S(2)}) collective-permute-start(bf16[2,192,128]{2,1,0:T(8,128)(2,1)S(1)} %pad_maximum_fusion.1), channel_id=1, source_target_pairs={{0,2},{1,3},{2,0},{3,1},{4,6},{5,7},{6,4},{7,5},{8,10},{9,11},{10,... | collective-permute-start | bytes 294920 | tf_op jit(solution)/shard_map/ppermute | solution.py:407
  10.4 3.2 %collective-permute-done.1 = bf16[2,192,128]{2,1,0:T(8,128)(2,1)S(1)} collective-permute-done((bf16[2,192,128]{2,1,0:T(8,128)(2,1)S(1)}, bf16[2,192,128]{2,1,0:T(8,128)(2,1)S(1)}, u32[]{:S(2)}, u32[]{:S(2)}) %collective-permute-start.1) | collective-permute-done | bytes 98336 | tf_op jit(solution)/shard_map/ppermute | solution.py:407
  13.6 1.8 %collective-permute-start.2 = (bf16[4,192,128]{2,1,0:T(8,128)(2,1)S(1)}, bf16[4,192,128]{2,1,0:T(8,128)(2,1)S(1)}, u32[]{:S(2)}, u32[]{:S(2)}) collective-permute-start(bf16[4,192,128]{2,1,0:T(8,128)(2,1)S(1)} %pad_maximum_fusion.near_ref), channel_id=1, source_target_pairs={{0,1},{1,0},{2,3},{3,2},{4,5},{5,4},{6,7},{7,6},{8,9},{9,8},{10,11... | collective-permute-start | bytes 589832 | tf_op jit(solution)/shard_map/ppermute | solution.py:407
  15.4 0.1 pad_add_fusion.place_ref
  15.5 3.9 %collective-permute-done.2.far_ref = bf16[4,192,128]{2,1,0:T(8,128)(2,1)S(1)} collective-permute-done((bf16[4,192,128]{2,1,0:T(8,128)(2,1)S(1)}, bf16[4,192,128]{2,1,0:T(8,128)(2,1)S(1)}, u32[]{:S(2)}, u32[]{:S(2)}) %collective-permute-start.2) | collective-permute-done | bytes 196640 | tf_op jit(solution)/shard_map/ppermute | solution.py:407
  19.4 0.0 copy-start
  19.4 2.0 %copy-done = bf16[6912,256]{1,0:T(8,128)(2,1)S(1)} copy-done((bf16[6912,256]{1,0:T(8,128)(2,1)S(1)}, bf16[6912,256]{1,0:T(8,128)(2,1)}, u32[]{:S(2)}) %copy-start) | copy-done | bytes 3538968
  21.4 0.0 copy-start.2
  21.4 1.5 %copy-done.2 = bf16[6912,128]{1,0:T(8,128)(2,1)S(1)} copy-done((bf16[6912,128]{1,0:T(8,128)(2,1)S(1)}, bf16[6912,128]{1,0:T(8,128)(2,1)}, u32[]{:S(2)}) %copy-start.2) | copy-done | bytes 1769496
  22.9 0.0 copy-start.3
  22.9 1.2 %copy-done.3 = bf16[3456,128]{1,0:T(8,128)(2,1)S(1)} copy-done((bf16[3456,128]{1,0:T(8,128)(2,1)S(1)}, bf16[3456,128]{1,0:T(8,128)(2,1)}, u32[]{:S(2)}) %copy-start.3) | copy-done | bytes 884760
  24.0 0.0 copy-start.5
  24.0 1.0 %copy-done.5 = bf16[256,1024]{1,0:T(8,128)(2,1)S(1)} copy-done((bf16[256,1024]{1,0:T(8,128)(2,1)S(1)}, bf16[256,1024]{1,0:T(8,128)(2,1)}, u32[]{:S(2)}) %copy-start.5) | copy-done | bytes 524312
  25.1 0.0 copy-start.6
  25.1 1.0 %copy-done.6 = bf16[1024,256]{1,0:T(8,128)(2,1)S(1)} copy-done((bf16[1024,256]{1,0:T(8,128)(2,1)S(1)}, bf16[1024,256]{1,0:T(8,128)(2,1)}, u32[]{:S(2)}) %copy-start.6) | copy-done | bytes 524312
  26.1 0.0 copy-start.7
  26.1 1.0 %copy-done.7 = bf16[1728,128]{1,0:T(8,128)(2,1)S(1)} copy-done((bf16[1728,128]{1,0:T(8,128)(2,1)S(1)}, bf16[1728,128]{1,0:T(8,128)(2,1)}, u32[]{:S(2)}) %copy-start.7) | copy-done | bytes 442392
  27.1 0.0 copy-start.8
  27.1 0.8 %copy-done.8 = bf16[128,128]{1,0:T(8,128)(2,1)S(1)} copy-done((bf16[128,128]{1,0:T(8,128)(2,1)S(1)}, bf16[128,128]{1,0:T(8,128)(2,1)}, u32[]{:S(2)}) %copy-start.8) | copy-done | bytes 32792
  27.9 0.0 copy-start.9
  27.9 0.8 %copy-done.9 = bf16[128,128]{1,0:T(8,128)(2,1)S(1)} copy-done((bf16[128,128]{1,0:T(8,128)(2,1)S(1)}, bf16[128,128]{1,0:T(8,128)(2,1)}, u32[]{:S(2)}) %copy-start.9) | copy-done | bytes 32792
  28.6 0.0 copy-start.1
  28.6 0.0 copy-start.4
  28.6 14.5 %shard_map.153 = (bf16[128,128]{1,0:T(8,128)(2,1)}, bf16[1424,128]{1,0:T(8,128)(2,1)S(1)}, bf16[1424,128]{1,0:T(8,128)(2,1)S(1)}, bf16[1024,128]{1,0:T(8,128)(2,...) custom-call(s32[2]{0:T(128)S(1)} %pad_add_fusion.place_ref, ...), custom_call_target="tpu_custom_call" | custom-call | flops 10000000000 | bytes 2097152 | tf_op jit(solution)/shard_map/pallas_call | solution.py:433
  43.2 0.1 collective-permute-start.5
  43.3 1.7 %collective-permute-done.5 = bf16[1424,128]{1,0:T(8,128)(2,1)S(1)} collective-permute-done((bf16[1424,128]{1,0:T(8,128)(2,1)S(1)}, bf16[1424,128]{1,0:T(8,128)(2,1)S(1)}, u32[]{:S(2)}, u32[]{:S(2)}) %collective-permute-start.5) | collective-permute-done | bytes 364576 | tf_op jit(solution)/shard_map/ppermute | solution.py:407
  44.9 0.1 add_convert_fusion.1
  45.0 1.8 %collective-permute-start.6 = (bf16[1424,128]{1,0:T(8,128)(2,1)S(1)}, bf16[1424,128]{1,0:T(8,128)(2,1)S(1)}, u32[]{:S(2)}, u32[]{:S(2)}) collective-permute-start(bf16[1424,128]{1,0:T(8,128)(2,1)S(1)} %add_convert_fusion.1), channel_id=1, source_target_pairs={{0,16},{8,24},{16,0},{24,8},{1,17},{9,25},{17,1},{25,9},{2,18},{10... | collective-permute-start | bytes 1093640 | tf_op jit(solution)/shard_map/ppermute | solution.py:407
  46.8 0.0 copy-done.1
  46.8 0.0 copy-done.4
  46.8 7.3 %shard_map.154 = bf16[928,128]{1,0:T(8,128)(2,1)S(1)} custom-call(s32[2]{0:T(128)S(1)} %pad_add_fusion.place_ref, bf16[128,128]{1,0:T(8,128)(2,1)S(1)} %copy-done.8, bf16[3456,128]{1,0:T(8,128)(2,1)S(1)} %copy-done.4, bf16[1024,256]{1,0:T(8,128)(2,1)S(1)} %copy-done.6, bf16[6912,256]{1,0:T(8,128)(2,1)S(1)} %copy-done.1, ...), custom_call_target="tpu_custom_call" | custom-call | flops 6000000000 | bytes 2097152 | tf_op jit(solution)/shard_map/pallas_call | solution.py:433
  54.1 0.1 collective-permute-start.3
  54.2 1.4 %collective-permute-done.6 = bf16[1424,128]{1,0:T(8,128)(2,1)S(1)} collective-permute-done((bf16[1424,128]{1,0:T(8,128)(2,1)S(1)}, bf16[1424,128]{1,0:T(8,128)(2,1)S(1)}, u32[]{:S(2)}, u32[]{:S(2)}) %collective-permute-start.6) | collective-permute-done | bytes 364576 | tf_op jit(solution)/shard_map/ppermute | solution.py:407
  55.6 0.1 add_convert_fusion.mine_ref
  55.7 0.1 collective-permute-start.7
  55.8 0.0 collective-permute-done.3
  55.8 0.1 add_convert_fusion.2.a_ref
  55.9 1.8 %collective-permute-start.4 = (bf16[928,128]{1,0:T(8,128)(2,1)S(1)}, bf16[928,128]{1,0:T(8,128)(2,1)S(1)}, u32[]{:S(2)}, u32[]{:S(2)}) collective-permute-start(bf16[928,128]{1,0:T(8,128)(2,1)S(1)} %add_convert_fusion.2.a_ref), channel_id=1, source_target_pairs={{0,16},{8,24},{16,0},{24,8},{1,17},{9,25},{17,1},{25,9},{2,18},{10... | collective-permute-start | bytes 712712 | tf_op jit(solution)/shard_map/ppermute | solution.py:407
  57.7 6.5 %collective-permute-done.4.b_ref = bf16[928,128]{1,0:T(8,128)(2,1)S(1)} collective-permute-done((bf16[928,128]{1,0:T(8,128)(2,1)S(1)}, bf16[928,128]{1,0:T(8,128)(2,1)S(1)}, u32[]{:S(2)}, u32[]{:S(2)}) %collective-permute-start.4) | collective-permute-done | bytes 237600 | tf_op jit(solution)/shard_map/ppermute | solution.py:407
  64.1 0.8 %shard_map.155 = (f32[16,1728]{1,0:T(8,128)}, f32[16,3456]{1,0:T(8,128)}, f32[32,1024]{1,0:T(8,128)}) custom-call(bf16[928,128]{1,0:T(8,128)(2,1)S(1)} %add_convert_fusion.2.a_ref, bf16[928,128]{1,0:T(8,128)(2,1)S(1)} %collective-permute-done.4.b_ref), custom_call_target="tpu_custom_call" | custom-call | bytes 2097152 | tf_op jit(solution)/shard_map/pallas_call | solution.py:433
  64.9 0.0 collective-permute-done.7.other_ref
  64.9 1.8 %shard_map.156 = (f32[32,6912]{1,0:T(8,128)}, f32[256,128]{1,0:T(8,128)}, f32[16,6912]{1,0:T(8,128)}) custom-call(s32[2]{0:T(128)S(1)} %pad_add_fusion.place_ref, bf16[1424,128]{1,0:T(8,128)(2,1)S(1)} %add_convert_fusion.mine_ref, bf16[1424,128]{1,0:T(8,128)(2,1)S(1)} %collective-permute-done.7.other_ref), custom_call_target="tpu_custom_call" | custom-call | bytes 2097152 | tf_op jit(solution)/shard_map/pallas_call | solution.py:433
  (2 shorter events, 0.0 us)
Async XLA Ops:
  2.3 6.6 %collective-permute-start = (bf16[1,192,128]{2,1,0:T(8,128)(2,1)S(1)}, bf16[1,192,128]{2,1,0:T(8,128)(2,1)S(1)}, u32[]{:S(2)}, u32[]{:S(2)}) collective-permute-start(bf16[1,192,128]{2,1,0:T(8,128)(2,1)S(1)} %maximum_bitcast_fusion), channel_id=1, source_target_pairs={{0,4},{1,5},{2,6},{3,7},{4,0},{5,1},{6,2},{7,3},{8,12},{9,13},{10,... | collective-permute-start | bytes 147464 | tf_op jit(solution)/shard_map/ppermute | solution.py:407
  8.9 4.7 %collective-permute-start.1 = (bf16[2,192,128]{2,1,0:T(8,128)(2,1)S(1)}, bf16[2,192,128]{2,1,0:T(8,128)(2,1)S(1)}, u32[]{:S(2)}, u32[]{:S(2)}) collective-permute-start(bf16[2,192,128]{2,1,0:T(8,128)(2,1)S(1)} %pad_maximum_fusion.1), channel_id=1, source_target_pairs={{0,2},{1,3},{2,0},{3,1},{4,6},{5,7},{6,4},{7,5},{8,10},{9,11},{10,... | collective-permute-start | bytes 294920 | tf_op jit(solution)/shard_map/ppermute | solution.py:407
  13.6 5.7 %collective-permute-start.2 = (bf16[4,192,128]{2,1,0:T(8,128)(2,1)S(1)}, bf16[4,192,128]{2,1,0:T(8,128)(2,1)S(1)}, u32[]{:S(2)}, u32[]{:S(2)}) collective-permute-start(bf16[4,192,128]{2,1,0:T(8,128)(2,1)S(1)} %pad_maximum_fusion.near_ref), channel_id=1, source_target_pairs={{0,1},{1,0},{2,3},{3,2},{4,5},{5,4},{6,7},{7,6},{8,9},{9,8},{10,11... | collective-permute-start | bytes 589832 | tf_op jit(solution)/shard_map/ppermute | solution.py:407
  19.4 2.0 %copy-start = (bf16[6912,256]{1,0:T(8,128)(2,1)S(1)}, bf16[6912,256]{1,0:T(8,128)(2,1)}, u32[]{:S(2)}) copy-start(bf16[6912,256]{1,0:T(8,128)(2,1)} %w_bottom.3) | copy-start | bytes 10616836
  21.4 1.5 %copy-start.2 = (bf16[6912,128]{1,0:T(8,128)(2,1)S(1)}, bf16[6912,128]{1,0:T(8,128)(2,1)}, u32[]{:S(2)}) copy-start(bf16[6912,128]{1,0:T(8,128)(2,1)} %w_join.1) | copy-start | bytes 5308420
  22.9 1.2 %copy-start.3 = (bf16[3456,128]{1,0:T(8,128)(2,1)S(1)}, bf16[3456,128]{1,0:T(8,128)(2,1)}, u32[]{:S(2)}) copy-start(bf16[3456,128]{1,0:T(8,128)(2,1)} %w_enc.3) | copy-start | bytes 2654212
  24.0 1.0 %copy-start.5 = (bf16[256,1024]{1,0:T(8,128)(2,1)S(1)}, bf16[256,1024]{1,0:T(8,128)(2,1)}, u32[]{:S(2)}) copy-start(bf16[256,1024]{1,0:T(8,128)(2,1)} %w_up.1) | copy-start | bytes 1572868
  25.1 1.0 %copy-start.6 = (bf16[1024,256]{1,0:T(8,128)(2,1)S(1)}, bf16[1024,256]{1,0:T(8,128)(2,1)}, u32[]{:S(2)}) copy-start(bf16[1024,256]{1,0:T(8,128)(2,1)} %w_down.3) | copy-start | bytes 1572868
  26.1 1.0 %copy-start.7 = (bf16[1728,128]{1,0:T(8,128)(2,1)S(1)}, bf16[1728,128]{1,0:T(8,128)(2,1)}, u32[]{:S(2)}) copy-start(bf16[1728,128]{1,0:T(8,128)(2,1)} %w_first.1) | copy-start | bytes 1327108
  27.1 0.8 %copy-start.8 = (bf16[128,128]{1,0:T(8,128)(2,1)S(1)}, bf16[128,128]{1,0:T(8,128)(2,1)}, u32[]{:S(2)}) copy-start(bf16[128,128]{1,0:T(8,128)(2,1)} %constant.25.clone.unshuffle_ref) | copy-start | bytes 98308
  27.9 0.8 %copy-start.9 = (bf16[128,128]{1,0:T(8,128)(2,1)S(1)}, bf16[128,128]{1,0:T(8,128)(2,1)}, u32[]{:S(2)}) copy-start(bf16[128,128]{1,0:T(8,128)(2,1)} %constant.26.clone.shuffle_ref) | copy-start | bytes 98308
  28.6 18.2 %copy-start.1 = (bf16[6912,256]{1,0:T(8,128)(2,1)S(1)}, bf16[6912,256]{1,0:T(8,128)(2,1)}, u32[]{:S(2)}) copy-start(bf16[6912,256]{1,0:T(8,128)(2,1)} %w_bottom.3) | copy-start | bytes 10616836
  28.6 18.2 %copy-start.4 = (bf16[3456,128]{1,0:T(8,128)(2,1)S(1)}, bf16[3456,128]{1,0:T(8,128)(2,1)}, u32[]{:S(2)}) copy-start(bf16[3456,128]{1,0:T(8,128)(2,1)} %w_enc.3) | copy-start | bytes 2654212
  43.2 1.7 %collective-permute-start.5 = (bf16[1424,128]{1,0:T(8,128)(2,1)S(1)}, bf16[1424,128]{1,0:T(8,128)(2,1)S(1)}, u32[]{:S(2)}, u32[]{:S(2)}) collective-permute-start(bf16[1424,128]{1,0:T(8,128)(2,1)S(1)} %get-tuple-element.37), channel_id=1, source_target_pairs={{0,8},{8,0},{16,24},{24,16},{1,9},{9,1},{17,25},{25,17},{2,10},{10... | collective-permute-start | bytes 1093640 | tf_op jit(solution)/shard_map/ppermute | solution.py:407
  45.0 10.6 %collective-permute-start.6 = (bf16[1424,128]{1,0:T(8,128)(2,1)S(1)}, bf16[1424,128]{1,0:T(8,128)(2,1)S(1)}, u32[]{:S(2)}, u32[]{:S(2)}) collective-permute-start(bf16[1424,128]{1,0:T(8,128)(2,1)S(1)} %add_convert_fusion.1), channel_id=1, source_target_pairs={{0,16},{8,24},{16,0},{24,8},{1,17},{9,25},{17,1},{25,9},{2,18},{10... | collective-permute-start | bytes 1093640 | tf_op jit(solution)/shard_map/ppermute | solution.py:407
  54.1 1.7 %collective-permute-start.3 = (bf16[928,128]{1,0:T(8,128)(2,1)S(1)}, bf16[928,128]{1,0:T(8,128)(2,1)S(1)}, u32[]{:S(2)}, u32[]{:S(2)}) collective-permute-start(bf16[928,128]{1,0:T(8,128)(2,1)S(1)} %shard_map.154), channel_id=1, source_target_pairs={{0,8},{8,0},{16,24},{24,16},{1,9},{9,1},{17,25},{25,17},{2,10},{10... | collective-permute-start | bytes 712712 | tf_op jit(solution)/shard_map/ppermute | solution.py:407
  55.7 9.2 %collective-permute-start.7 = (bf16[1424,128]{1,0:T(8,128)(2,1)S(1)}, bf16[1424,128]{1,0:T(8,128)(2,1)S(1)}, u32[]{:S(2)}, u32[]{:S(2)}) collective-permute-start(bf16[1424,128]{1,0:T(8,128)(2,1)S(1)} %add_convert_fusion.mine_ref), channel_id=1, source_target_pairs={{0,8},{8,0},{16,24},{24,16},{1,9},{9,1},{17,25},{25,17},{2,10},{10... | collective-permute-start | bytes 1093640 | tf_op jit(solution)/shard_map/ppermute | solution.py:407
  55.9 8.2 %collective-permute-start.4 = (bf16[928,128]{1,0:T(8,128)(2,1)S(1)}, bf16[928,128]{1,0:T(8,128)(2,1)S(1)}, u32[]{:S(2)}, u32[]{:S(2)}) collective-permute-start(bf16[928,128]{1,0:T(8,128)(2,1)S(1)} %add_convert_fusion.2.a_ref), channel_id=1, source_target_pairs={{0,16},{8,24},{16,0},{24,8},{1,17},{9,25},{17,1},{25,9},{2,18},{10... | collective-permute-start | bytes 712712 | tf_op jit(solution)/shard_map/ppermute | solution.py:407

commit v3 on v2

--- a/solution.py
+++ b/solution.py
@@ -3,7 +3,6 @@
 
 import jax
 import jax.numpy as jnp
-import numpy as np
 from jax import lax
 from jax.experimental import pallas as pl
 from jax.experimental.pallas import tpu as pltpu
@@ -13,6 +12,9 @@
 F32 = jnp.float32
 LANES = 128
 MIB = 1024 * 1024
+VMEM = pltpu.MemorySpace.VMEM
+SMEM = pltpu.MemorySpace.SMEM
+HBM = pltpu.MemorySpace.HBM
 
 
 def dot(a, b):
@@ -184,6 +186,18 @@
             at += count
 
 
+def one_hot(ny, nz, back):
+    plane = ny * nz
+    shape = (2 * plane, 2 * plane)
+    row = lax.broadcasted_iota(jnp.int32, shape, 1 if back else 0)
+    column = lax.broadcasted_iota(jnp.int32, shape, 0 if back else 1)
+    tap, at = lax.div(row, plane // 4), lax.rem(row, plane // 4)
+    ox, oy, oz = lax.div(tap, 4), lax.rem(lax.div(tap, 2), 2), lax.rem(tap, 2)
+    y, z = lax.div(at, nz // 2), lax.rem(at, nz // 2)
+    wanted = ox * plane + (2 * y + oy) * nz + 2 * z + oz
+    return (column == wanted).astype(F32).astype(BF)
+
+
 def to_blocks(shuffle, field, d_ref, pairs, plane):
     width = field.shape[1]
     for i in range(pairs):
@@ -203,19 +217,33 @@
     return jnp.concatenate(parts, axis=0)
 
 
+def join_kernel(sx, plane, volume_hbm, cotangent_hbm, out_ref, volume_ref, arrived):
+    first = pltpu.make_async_copy(volume_hbm, volume_ref, arrived.at[0])
+    second = pltpu.make_async_copy(cotangent_hbm, out_ref.at[0, sx // 2 * plane :], arrived.at[1])
+    first.start()
+    second.start()
+    first.wait()
+    for i in range(sx // 2):
+        pair = [volume_ref[2 * i + k].astype(F32) for k in range(2)]
+        out_ref[0, i * plane : (i + 1) * plane, :] = jnp.concatenate(pair, 1).astype(BF)
+    second.wait()
+
+
+def stage_kernel(place_ref, near_ref, sources, *refs):
+    del place_ref, near_ref
+    *held, arrived = refs
+    copies = [pltpu.make_async_copy(a, b, arrived.at[i]) for i, (a, b) in enumerate(zip(sources, held))]
+    for copy in copies:
+        copy.start()
+    for copy in copies:
+        copy.wait()
+
+
 def upper_kernel(
     geo,
     place_ref,
-    near_ref,
-    far_ref,
-    shuffle_ref,
-    unshuffle_ref,
-    w_first,
-    w_enc,
-    w_down,
-    w_bottom,
-    w_up,
-    w_join,
+    gathered,
+    weights,
     decoded_ref,
     keep_ref,
     send_ref,
@@ -240,15 +268,16 @@
 ):
     (n, sx, ny, nz, c0, c1, c2, masks, spots) = geo
     position = place_ref[0]
+    w_first, w_enc, w_down, w_bottom, w_up, w_join = weights
+    shuffle, unshuffle = one_hot(ny, nz, False), one_hot(ny, nz, True)
     plane, nx = ny * nz, sx * n
     rows = nx * plane
     cplane, cx = plane // 4, nx // 2
     crows = cx * cplane
     fine, coarse = (nx, ny, nz), (cx, ny // 2, nz // 2)
-    half = n // 2 if n > 1 else 1
-    for m, mask in enumerate(masks):
-        source = near_ref if m < half else far_ref
-        blocks[lax.bitwise_xor(position, mask)] = source[m % half]
+    for source, held in zip(gathered, masks):
+        for m, mask in enumerate(held):
+            blocks[lax.bitwise_xor(position, mask)] = source[m]
 
     lane = lax.broadcasted_iota(jnp.int32, (plane, LANES), 1)
     vol_rows = sx // 2 * plane
@@ -275,7 +304,7 @@
     skip = silu(z2)
     joined[:, c1:] = skip
     fill(uj, z_windows(skip.astype(F32), nz), 0, c1, 2 * c1)
-    to_blocks(shuffle_ref[...], skip, d_ref, cx, cplane)
+    to_blocks(shuffle, skip, d_ref, cx, cplane)
     z3 = dot(d_ref[...], w_down[...])
     z3_ref[...] = z3
     g1 = silu(z3)
@@ -283,7 +312,7 @@
     fill(uc, yz_windows(g1.astype(F32), *coarse[1:]), cplane)
     z4 = conv(uc, w_bottom, crows, cplane)
     g2 = silu(z4)
-    lifted = from_blocks(unshuffle_ref[...], dot(g2, w_up[...]).astype(BF), cx, cplane, c1)
+    lifted = from_blocks(unshuffle, dot(g2, w_up[...]).astype(BF), cx, cplane, c1)
     joined[:, 0:c1] = lifted.astype(BF)
     fill(uj, z_windows(lifted, nz), 0, 0, 2 * c1)
     z7 = conv_z(uj[...], w_join, fine)
@@ -299,7 +328,7 @@
     b7 = conv_back(ut, w_join, rows, plane)
     skip_back_ref[...] = b7[:, c1:]
 
-    to_blocks(shuffle_ref[...], b7[:, :c1].astype(BF), lb_ref, cx, cplane)
+    to_blocks(shuffle, b7[:, :c1].astype(BF), lb_ref, cx, cplane)
     emit(pack, spots["up"], dot(own_columns(lb_ref[...], 8 * c1 // n, position).astype(BF), g2))
     e3 = dot_t(lb_ref[...], w_up[...]).astype(BF).astype(F32)
     t4 = (e3 * slope(z4)).astype(BF)
@@ -314,7 +343,6 @@
 def lower_kernel(
     geo,
     place_ref,
-    unshuffle_ref,
     w_enc,
     w_down,
     w_bottom,
@@ -336,6 +364,7 @@
     cplane, cx = plane // 4, nx // 2
     crows = cx * cplane
     fine, coarse = (nx, ny, nz), (cx, ny // 2, nz // 2)
+    unshuffle = one_hot(ny, nz, True)
     clear_rims(utc, cplane)
     fill(utc, yz_windows(t4_ref[...].astype(F32), *coarse[1:]), cplane)
     e4 = conv_back(utc, w_bottom, crows, cplane).astype(BF).astype(F32)
@@ -344,8 +373,8 @@
     e5 = dot_t(t3, w_down[...])
     high = e5.astype(BF)
     low = (e5 - high.astype(F32)).astype(BF)
-    e5 = from_blocks(unshuffle_ref[...], high, cx, cplane, c1) + from_blocks(
-        unshuffle_ref[...], low, cx, cplane, c1
+    e5 = from_blocks(unshuffle, high, cx, cplane, c1) + from_blocks(
+        unshuffle, low, cx, cplane, c1
     )
     t2 = ((e5 + skip_back_ref[...]) * slope(z2_ref[...])).astype(BF)
     fill(ut, z_windows(t2.astype(F32), nz))
@@ -372,7 +401,8 @@
         at += count
 
 
-def finish_first(factor, spots, place_ref, mine_ref, other_ref, bottom_ref, up_ref, join_ref, both):
+def finish_first(factor, spots, place_ref, mine_ref, other_ref, bottom_ref, up_ref, join_ref, token, both):
+    token[...] = jnp.zeros(token.shape, F32)
     core = place_ref[1]
     both[core] = mine_ref[...]
     both[1 - core] = other_ref[...]
@@ -393,7 +423,9 @@
         up_ref[v : v + LANES, :] = (source(spots["up"] + v // LANES * rows, rows) * factor).T
 
 
-def finish_second(factor, spots, a_ref, b_ref, first_ref, enc_ref, down_ref):
+def finish_second(factor, spots, earlier, a_ref, b_ref, first_ref, enc_ref, down_ref):
+    del earlier
+
     def source(at, count):
         return a_ref[at : at + count, :].astype(F32) + b_ref[at : at + count, :].astype(F32)
 
@@ -402,45 +434,43 @@
     unpack(source, spots["down"], down_ref, factor)
 
 
+def in_hbm(array):
+    return pltpu.with_memory_space_constraint(array, HBM)
+
+
 def exchange(array, axis, mask):
     devices = lax.axis_size(axis)
     return lax.ppermute(array, axis, [(i, i ^ mask) for i in range(devices)])
 
 
+def add_kernel(a_ref, b_ref, out_ref):
+    out_ref[...] = (a_ref[...].astype(F32) + b_ref[...].astype(F32)).astype(BF)
+
+
 def add(a, b):
-    return (a.astype(F32) + b.astype(F32)).astype(BF)
-
-
-def one_hot_shuffle(ny, nz):
-    plane = ny * nz
-    shuffle = np.zeros((2 * plane, 2 * plane), np.float32)
-    row = 0
-    for ox in range(2):
-        for oy in range(2):
-            for oz in range(2):
-                for y in range(ny // 2):
-                    for z in range(nz // 2):
-                        shuffle[row, ox * plane + (2 * y + oy) * nz + 2 * z + oz] = 1.0
-                        row += 1
-    return shuffle
-
-
-def call(kernel, outs, scratch, scalars, flops=0, vmem=30):
-    whole = pl.BlockSpec(memory_space=pltpu.VMEM)
-
-    def run(*args):
-        specs = [pl.BlockSpec(memory_space=pltpu.SMEM)] * scalars + [whole] * (len(args) - scalars)
-        return pl.pallas_call(
-            kernel,
-            out_shape=tuple(jax.ShapeDtypeStruct(s, d) for s, d in outs),
-            in_specs=specs,
-            out_specs=tuple(whole for _ in outs),
-            scratch_shapes=[pltpu.VMEM(s, d) for s, d in scratch],
-            compiler_params=pltpu.CompilerParams(vmem_limit_bytes=vmem * MIB),
-            cost_estimate=pl.CostEstimate(flops=flops, bytes_accessed=2 * MIB, transcendentals=0),
-        )(*args)
-
-    return run
+    return call(add_kernel, [(a.shape, BF)], [], (VMEM, VMEM), vmem=4)(a, b)[0]
+
+
+def stack_kernel(a_ref, b_ref, out_ref):
+    out_ref[0 : a_ref.shape[0]] = a_ref[...]
+    out_ref[a_ref.shape[0] :] = b_ref[...]
+
+
+def stack(a, b):
+    shape = (a.shape[0] + b.shape[0],) + a.shape[1:]
+    return call(stack_kernel, [(shape, BF)], [], (VMEM, VMEM), vmem=4)(a, b)[0]
+
+
+def call(kernel, outs, scratch, spaces, flops=0, vmem=12):
+    return pl.pallas_call(
+        kernel,
+        out_shape=tuple(jax.ShapeDtypeStruct(s, d) for s, d in outs),
+        in_specs=jax.tree.map(lambda space: pl.BlockSpec(memory_space=space), spaces),
+        out_specs=tuple(pl.BlockSpec(memory_space=VMEM) for _ in outs),
+        scratch_shapes=scratch,
+        compiler_params=pltpu.CompilerParams(vmem_limit_bytes=vmem * MIB),
+        cost_estimate=pl.CostEstimate(flops=flops, bytes_accessed=2 * MIB, transcendentals=0),
+    )
 
 
 def body(volume, w_first, w_enc, w_down, w_bottom, w_up, w_join, cotangent):
@@ -451,16 +481,34 @@
     plane, nx = ny * nz, sx * n
     rows = nx * plane
     cplane, crows = plane // 4, rows // 8
-    vol = volume.reshape(sx // 2, 2, plane, c0).transpose(0, 2, 1, 3).reshape(sx // 2 * plane, 2 * c0)
-    near = jnp.concatenate([vol, cotangent.reshape(sx * plane, c1)], 0)[None]
-    masks, step = [0], n // 2
-    far = near
-    while step:
-        masks = masks + [m ^ step for m in masks]
-        far = exchange(near, "space", step)
+    section = lax.axis_index("section")
+    place = jnp.stack([lax.axis_index("space"), section % 2]).astype(jnp.int32)
+    own_rows = sx * plane // 2 + sx * plane
+    (near,) = call(
+        functools.partial(join_kernel, sx, plane),
+        [((1, own_rows, LANES), BF)],
+        [pltpu.VMEM((sx, plane, c0), BF), pltpu.SemaphoreType.DMA((2,))],
+        (HBM, HBM),
+        vmem=4,
+    )(in_hbm(volume.reshape(sx, plane, c0)), in_hbm(cotangent.reshape(sx * plane, c1)))
+    weights = [w_first, w_enc, w_down, w_bottom, w_up, w_join]
+    stage = call(
+        stage_kernel,
+        [(w.shape, BF) for w in weights],
+        [pltpu.SemaphoreType.DMA((len(weights),))],
+        (SMEM, VMEM, [HBM] * len(weights)),
+        flops=2 * 10**9,
+        vmem=12,
+    )
+    weights = list(stage(place, near, [in_hbm(w) for w in weights]))
+    held, step = [0], n // 2
+    while step > 2:
+        held = held + [m ^ step for m in held]
+        near = stack(near, exchange(near, "space", step))
         step //= 2
-        if step:
-            near = jnp.concatenate([near, far], 0)
+    last = range(1, min(n, 4))
+    gathered = [near] + [exchange(near, "space", mask) for mask in last]
+    masks = tuple(tuple(m ^ mask for m in held) for mask in (0, *last))
 
     fine_own, wide_own = c1 // n, c2 // n
     shapes = {
@@ -482,12 +530,7 @@
 
     upper_spots, upper_rows = layout(("bottom", "up", "join"))
     lower_spots, lower_rows = layout(("down", "enc", "first"))
-    geo = (n, sx, ny, nz, c0, c1, c2, tuple(masks))
-    shuffle = one_hot_shuffle(ny, nz)
-    unshuffle = jnp.asarray(shuffle.T, BF)
-    shuffle = jnp.asarray(shuffle, BF)
-    section = lax.axis_index("section")
-    place = jnp.stack([lax.axis_index("space"), section % 2]).astype(jnp.int32)
+    geo = (n, sx, ny, nz, c0, c1, c2, masks)
     size = upper_rows // 2
     decoded, keep, send, vol2, z1, h1, z2, blocks, z3, t4, skip_back = call(
         functools.partial(upper_kernel, geo + (upper_spots,)),
@@ -505,20 +548,21 @@
             ((rows, c1), F32),
         ],
         [
-            ((n,) + near.shape[1:], BF),
-            ((rows, 2 * LANES), BF),
-            ((rows, 3 * c1), BF),
-            ((rows, 6 * c1), BF),
-            ((rows + 2 * plane, 9 * c1), BF),
-            ((crows + 2 * cplane, 9 * c2), BF),
-            ((rows, 2 * c1), BF),
-            ((crows, 8 * c1), BF),
-            ((rows, c1), BF),
-            ((upper_rows, LANES), BF),
+            pltpu.VMEM((n, own_rows, LANES), BF),
+            pltpu.VMEM((rows, 2 * LANES), BF),
+            pltpu.VMEM((rows, 3 * c1), BF),
+            pltpu.VMEM((rows, 6 * c1), BF),
+            pltpu.VMEM((rows + 2 * plane, 9 * c1), BF),
+            pltpu.VMEM((crows + 2 * cplane, 9 * c2), BF),
+            pltpu.VMEM((rows, 2 * c1), BF),
+            pltpu.VMEM((crows, 8 * c1), BF),
+            pltpu.VMEM((rows, c1), BF),
+            pltpu.VMEM((upper_rows, LANES), BF),
         ],
-        1,
+        (SMEM, [VMEM] * len(gathered), [VMEM] * len(weights)),
         flops=10**10,
-    )(place, near, far, shuffle, unshuffle, w_first, w_enc, w_down, w_bottom, w_up, w_join)
+        vmem=14,
+    )(place, gathered, weights)
     total = add(keep, exchange(send, "section", 1))
     mask = 2
     while mask < crops:
@@ -529,10 +573,10 @@
     (pack,) = call(
         functools.partial(lower_kernel, geo + (lower_spots,)),
         [((lower_rows, LANES), BF)],
-        [((crows + 2 * cplane, 9 * c2), BF), ((rows, 3 * c1), BF)],
-        1,
+        [pltpu.VMEM((crows + 2 * cplane, 9 * c2), BF), pltpu.VMEM((rows, 3 * c1), BF)],
+        (SMEM,) + (VMEM,) * 11,
         flops=6 * 10**9,
-    )(place, unshuffle, w_enc, w_down, w_bottom, vol2, z1, h1, z2, blocks, z3, t4, skip_back)
+    )(place, *weights[1:4], vol2, z1, h1, z2, blocks, z3, t4, skip_back)
     mask = 1
     pack_other = exchange(pack, "section", mask)
     while 2 * mask < crops:
@@ -541,18 +585,20 @@
         pack_other = exchange(pack, "section", mask)
 
     factor = 1.0 / math.sqrt(crops * rows)
-    grad_bottom, grad_up, grad_join = call(
+    grad_bottom, grad_up, grad_join, token = call(
         functools.partial(finish_first, factor, upper_spots),
-        [(shapes["bottom"], F32), (shapes["up"][::-1], F32), (shapes["join"], F32)],
-        [((2, size, LANES), BF)],
-        1,
+        [(shapes["bottom"], F32), (shapes["up"][::-1], F32), (shapes["join"], F32), ((8, LANES), F32)],
+        [pltpu.VMEM((2, size, LANES), BF)],
+        (SMEM, VMEM, VMEM),
+        vmem=12,
     )(place, total, other)
     grad_first, grad_enc, grad_down = call(
         functools.partial(finish_second, factor, lower_spots),
         [(shapes[name], F32) for name in ("first", "enc", "down")],
         [],
-        0,
-    )(pack, pack_other)
+        (VMEM, VMEM, VMEM),
+        vmem=8,
+    )(token, pack, pack_other)
     return (
         decoded.reshape((1, sx, ny, nz, c1)),
         grad_first.T,

time: 67.3 us -> 52.6 us (0.78)
  local copies, waits for them, and re-layouts: 10.1 us -> 0 us
  waiting for transfers between devices: 19.3 us -> 11.2 us
  Pallas kernels: 24.4 us -> 29.4 us
  other arithmetic: 1.13 us -> 0.07 us
    unnamed x20 -> x0, local copies, waits for them, and re-layouts: 9.26 us -> none
    ppermute x8 -> x9, waiting for transfers between devices: 19.3 us -> 11.2 us  [exchange(): return lax.ppermute(array, axis, [(i, i ^ mask) for i in range(devices)])]
    pallas_call x4 -> x10, Pallas kernels: 24.4 us -> 29.4 us  [the longest x1 14.6 us: body(): call(functools.partial(upper_kernel, geo + (upper_spots,)), [((sx * plane...]
    reshape x2 -> x0, local copies, waits for them, and re-layouts: 0.89 us -> none  [body(): volume.reshape(sx // 2, 2, plane, c0).transpose(0, 2, 1, 3)]
    broadcast_in_dim x1 -> x0, other arithmetic: 0.76 us -> none  [body(): near = jnp.concatenate([vol, cotangent.reshape(sx * plane, c1)], 0)[None]]
    ppermute x8 -> x9, starting transfers between devices: 11 us -> 11 us  [exchange(): return lax.ppermute(array, axis, [(i, i ^ mask) for i in range(devices)])]
  transfers between devices with their start and end apart: 8 -> 9, of which waited for: 6 -> 5; matrix products, arithmetic and copies ran while one was open for 0% -> 0% of each run, Pallas kernels for 12% -> 25%
where the time goes in v3:
time: 52.6 us; the launch traced here: 52.4 us
  Pallas kernels  29.4 us (56%)
  waiting for transfers between devices  11.2 us (21%)
  starting transfers between devices  11 us (21%)
  between operations  0.74 us (1%)
    pallas_call x1, Pallas kernels, body(): call(functools.partial(upper_kernel, geo + (upper_spots,)), [((sx * plane...  14.6 us
    ppermute x9, waiting for transfers between devices, exchange(): return lax.ppermute(array, axis, [(i, i ^ mask) for i in range(devices)])  11.2 us
    ppermute x9, starting transfers between devices, exchange(): return lax.ppermute(array, axis, [(i, i ^ mask) for i in range(devices)])  11 us
    pallas_call x1, Pallas kernels, body(): call(functools.partial(lower_kernel, geo + (lower_spots,)), [((lower_rows...  7.32 us
    pallas_call x1, Pallas kernels, body(): weights = list(stage(place, near, [in_hbm(w) for w in weights]))  3.85 us
    pallas_call x1, Pallas kernels, body(): call(functools.partial(finish_first, factor, upper_spots), [(shapes['bott...  1.77 us
  transfers between devices with their start and end apart: 9, of which 5 were waited for; matrix products, arithmetic and copies ran while one was open for 0% of the time, Pallas kernels for 25%

profile of v3, /device:TPU:0, one launch (start us, length us, event | category | flops | bytes accessed | tf_op | source)
XLA Modules:
  0.0 52.4 jit_solution(4171211351530674706)
XLA Ops:
  0.6 0.9 %shard_map.135.a_ref.near_ref = bf16[1,192,128]{2,1,0:T(8,128)(2,1)S(1)} custom-call(bf16[2,64,64]{2,1,0:T(8,128)(2,1)} %bitcast.10, bf16[128,128]{1,0:T(8,128)(2,1)} %bitcast.11), custom_call_target="tpu_custom_call" | custom-call | bytes 2097152 | tf_op jit(solution)/shard_map/pallas_call | solution.py:487
  1.5 4.1 %collective-permute-start = (bf16[1,192,128]{2,1,0:T(8,128)(2,1)S(1)}, bf16[1,192,128]{2,1,0:T(8,128)(2,1)S(1)}, u32[]{:S(2)}, u32[]{:S(2)}) collective-permute-start(bf16[1,192,128]{2,1,0:T(8,128)(2,1)S(1)} %shard_map.135.a_ref.near_ref), channel_id=1, source_target_pairs={{0,4},{1,5},{2,6},{3,7},{4,0},{5,1},{6,2},{7,3},{8,12},{9,13},{10,... | collective-permute-start | bytes 147464 | tf_op jit(solution)/shard_map/ppermute | solution.py:443
  5.6 0.1 pad_add_fusion.place_ref
  5.7 2.5 %collective-permute-done.b_ref = bf16[1,192,128]{2,1,0:T(8,128)(2,1)S(1)} collective-permute-done((bf16[1,192,128]{2,1,0:T(8,128)(2,1)S(1)}, bf16[1,192,128]{2,1,0:T(8,128)(2,1)S(1)}, u32[]{:S(2)}, u32[]{:S(2)}) %collective-permute-start) | collective-permute-done | bytes 49184 | tf_op jit(solution)/shard_map/ppermute | solution.py:443
  8.2 2.4 %collective-permute-start.3 = (bf16[2,192,128]{2,1,0:T(8,128)(2,1)S(1)}, bf16[2,192,128]{2,1,0:T(8,128)(2,1)S(1)}, u32[]{:S(2)}, u32[]{:S(2)}) collective-permute-start(bf16[2,192,128]{2,1,0:T(8,128)(2,1)S(1)} %shard_map.136.gathered_0_), channel_id=1, source_target_pairs={{0,3},{1,2},{2,1},{3,0},{4,7},{5,6},{6,5},{7,4},{8,11},{9,10},{10,... | collective-permute-start | bytes 294920 | tf_op jit(solution)/shard_map/ppermute | solution.py:443
  10.6 0.9 %collective-permute-start.2 = (bf16[2,192,128]{2,1,0:T(8,128)(2,1)S(1)}, bf16[2,192,128]{2,1,0:T(8,128)(2,1)S(1)}, u32[]{:S(2)}, u32[]{:S(2)}) collective-permute-start(bf16[2,192,128]{2,1,0:T(8,128)(2,1)S(1)} %shard_map.136.gathered_0_), channel_id=1, source_target_pairs={{0,2},{1,3},{2,0},{3,1},{4,6},{5,7},{6,4},{7,5},{8,10},{9,11},{10,... | collective-permute-start | bytes 294920 | tf_op jit(solution)/shard_map/ppermute | solution.py:443
  11.5 0.3 collective-permute-start.1
  11.8 3.8 %shard_map.137 = (bf16[1728,128]{1,0:T(8,128)(2,1)S(1)}, bf16[3456,128]{1,0:T(8,128)(2,1)S(1)}, bf16[1024,256]{1,0:T(8,128)(2,1)S(1)}, bf16[6912,256]{1,0:T(8,12...) custom-call(s32[2]{0:T(128)S(1)} %pad_add_fusion.place_ref, ...), custom_call_target="tpu_custom_call" | custom-call | flops 2000000000 | bytes 2097152 | tf_op jit(solution)/shard_map/pallas_call | solution.py:503
  15.6 0.0 collective-permute-done.3.gathered_3_
  15.6 0.0 collective-permute-done.2.gathered_2_
  15.6 0.4 collective-permute-done.1.gathered_1_
  16.1 14.6 %shard_map.138 = (bf16[128,128]{1,0:T(8,128)(2,1)}, bf16[1424,128]{1,0:T(8,128)(2,1)S(1)}, bf16[1424,128]{1,0:T(8,128)(2,1)S(1)}, bf16[1024,128]{1,0:T(8,128)(2,...) custom-call(s32[2]{0:T(128)S(1)} %pad_add_fusion.place_ref, ...), custom_call_target="tpu_custom_call" | custom-call | flops 10000000000 | bytes 2097152 | tf_op jit(solution)/shard_map/pallas_call | solution.py:535
  30.7 0.1 collective-permute-start.4
  30.8 1.7 %collective-permute-done.4.b_ref = bf16[1424,128]{1,0:T(8,128)(2,1)S(1)} collective-permute-done((bf16[1424,128]{1,0:T(8,128)(2,1)S(1)}, bf16[1424,128]{1,0:T(8,128)(2,1)S(1)}, u32[]{:S(2)}, u32[]{:S(2)}) %collective-permute-start.4) | collective-permute-done | bytes 364576 | tf_op jit(solution)/shard_map/ppermute | solution.py:443
  32.4 0.1 shard_map.139.a_ref
  32.5 1.6 %collective-permute-start.5 = (bf16[1424,128]{1,0:T(8,128)(2,1)S(1)}, bf16[1424,128]{1,0:T(8,128)(2,1)S(1)}, u32[]{:S(2)}, u32[]{:S(2)}) collective-permute-start(bf16[1424,128]{1,0:T(8,128)(2,1)S(1)} %shard_map.139.a_ref), channel_id=1, source_target_pairs={{0,16},{8,24},{16,0},{24,8},{1,17},{9,25},{17,1},{25,9},{2,18},{10... | collective-permute-start | bytes 1093640 | tf_op jit(solution)/shard_map/ppermute | solution.py:443
  34.1 7.3 %shard_map.142.a_ref = bf16[928,128]{1,0:T(8,128)(2,1)S(1)} custom-call(s32[2]{0:T(128)S(1)} %pad_add_fusion.place_ref, bf16[3456,128]{1,0:T(8,128)(2,1)S(1)} %get-tuple-element.32.weights_1_.w_enc, bf16[1024,256]{1,0:T(8,128)(2,1)S(1)} %get-tuple-element.33.weights_2_.w_down, bf16[6912,256]{1,0:T(8,128)(2,1)S(1)} %get-tuple-element.34.weights_3_.w_bottom, ...), custom_call_target="tpu_custom_call" | custom-call | flops 6000000000 | bytes 2097152 | tf_op jit(solution)/shard_map/pallas_call | solution.py:573
  41.4 0.1 collective-permute-start.7
  41.5 1.6 %collective-permute-done.5.b_ref = bf16[1424,128]{1,0:T(8,128)(2,1)S(1)} collective-permute-done((bf16[1424,128]{1,0:T(8,128)(2,1)S(1)}, bf16[1424,128]{1,0:T(8,128)(2,1)S(1)}, u32[]{:S(2)}, u32[]{:S(2)}) %collective-permute-start.5) | collective-permute-done | bytes 364576 | tf_op jit(solution)/shard_map/ppermute | solution.py:443
  43.1 0.1 shard_map.140.mine_ref
  43.2 0.1 collective-permute-start.6
  43.3 0.0 collective-permute-done.7.b_ref
  43.3 0.1 shard_map.143.a_ref
  43.4 1.6 %collective-permute-start.8 = (bf16[928,128]{1,0:T(8,128)(2,1)S(1)}, bf16[928,128]{1,0:T(8,128)(2,1)S(1)}, u32[]{:S(2)}, u32[]{:S(2)}) collective-permute-start(bf16[928,128]{1,0:T(8,128)(2,1)S(1)} %shard_map.143.a_ref), channel_id=1, source_target_pairs={{0,16},{8,24},{16,0},{24,8},{1,17},{9,25},{17,1},{25,9},{2,18},{10... | collective-permute-start | bytes 712712 | tf_op jit(solution)/shard_map/ppermute | solution.py:443
  44.9 0.0 collective-permute-done.6.other_ref
  45.0 1.8 %shard_map.141 = (f32[32,6912]{1,0:T(8,128)}, f32[256,128]{1,0:T(8,128)}, f32[16,6912]{1,0:T(8,128)}, f32[8,128]{1,0:T(8,128)S(1)}) custom-call(s32[2]{0:T(128)S(1)} %pad_add_fusion.place_ref, bf16[1424,128]{1,0:T(8,128)(2,1)S(1)} %shard_map.140.mine_ref, bf16[1424,128]{1,0:T(8,128)(2,1)S(1)} %collective-permute-done.6.other_ref), custom_call_target="tpu_custom_call" | custom-call | bytes 2097152 | tf_op jit(solution)/shard_map/pallas_call | solution.py:588
  46.7 4.9 %collective-permute-done.8.b_ref = bf16[928,128]{1,0:T(8,128)(2,1)S(1)} collective-permute-done((bf16[928,128]{1,0:T(8,128)(2,1)S(1)}, bf16[928,128]{1,0:T(8,128)(2,1)S(1)}, u32[]{:S(2)}, u32[]{:S(2)}) %collective-permute-start.8) | collective-permute-done | bytes 237600 | tf_op jit(solution)/shard_map/ppermute | solution.py:443
  51.6 0.8 %shard_map.144 = (f32[16,1728]{1,0:T(8,128)}, f32[16,3456]{1,0:T(8,128)}, f32[32,1024]{1,0:T(8,128)}) custom-call(f32[8,128]{1,0:T(8,128)S(1)} %get-tuple-element.40.earlier, bf16[928,128]{1,0:T(8,128)(2,1)S(1)} %shard_map.143.a_ref, bf16[928,128]{1,0:T(8,128)(2,1)S(1)} %collective-permute-done.8.b_ref), custom_call_target="tpu_custom_call" | custom-call | bytes 2097152 | tf_op jit(solution)/shard_map/pallas_call | solution.py:595
  (1 shorter events, 0.0 us)
Async XLA Ops:
  1.5 6.7 %collective-permute-start = (bf16[1,192,128]{2,1,0:T(8,128)(2,1)S(1)}, bf16[1,192,128]{2,1,0:T(8,128)(2,1)S(1)}, u32[]{:S(2)}, u32[]{:S(2)}) collective-permute-start(bf16[1,192,128]{2,1,0:T(8,128)(2,1)S(1)} %shard_map.135.a_ref.near_ref), channel_id=1, source_target_pairs={{0,4},{1,5},{2,6},{3,7},{4,0},{5,1},{6,2},{7,3},{8,12},{9,13},{10,... | collective-permute-start | bytes 147464 | tf_op jit(solution)/shard_map/ppermute | solution.py:443
  8.2 7.4 %collective-permute-start.3 = (bf16[2,192,128]{2,1,0:T(8,128)(2,1)S(1)}, bf16[2,192,128]{2,1,0:T(8,128)(2,1)S(1)}, u32[]{:S(2)}, u32[]{:S(2)}) collective-permute-start(bf16[2,192,128]{2,1,0:T(8,128)(2,1)S(1)} %shard_map.136.gathered_0_), channel_id=1, source_target_pairs={{0,3},{1,2},{2,1},{3,0},{4,7},{5,6},{6,5},{7,4},{8,11},{9,10},{10,... | collective-permute-start | bytes 294920 | tf_op jit(solution)/shard_map/ppermute | solution.py:443
  10.6 5.0 %collective-permute-start.2 = (bf16[2,192,128]{2,1,0:T(8,128)(2,1)S(1)}, bf16[2,192,128]{2,1,0:T(8,128)(2,1)S(1)}, u32[]{:S(2)}, u32[]{:S(2)}) collective-permute-start(bf16[2,192,128]{2,1,0:T(8,128)(2,1)S(1)} %shard_map.136.gathered_0_), channel_id=1, source_target_pairs={{0,2},{1,3},{2,0},{3,1},{4,6},{5,7},{6,4},{7,5},{8,10},{9,11},{10,... | collective-permute-start | bytes 294920 | tf_op jit(solution)/shard_map/ppermute | solution.py:443
  11.5 4.6 %collective-permute-start.1 = (bf16[2,192,128]{2,1,0:T(8,128)(2,1)S(1)}, bf16[2,192,128]{2,1,0:T(8,128)(2,1)S(1)}, u32[]{:S(2)}, u32[]{:S(2)}) collective-permute-start(bf16[2,192,128]{2,1,0:T(8,128)(2,1)S(1)} %shard_map.136.gathered_0_), channel_id=1, source_target_pairs={{0,1},{1,0},{2,3},{3,2},{4,5},{5,4},{6,7},{7,6},{8,9},{9,8},{10,11... | collective-permute-start | bytes 294920 | tf_op jit(solution)/shard_map/ppermute | solution.py:443
  30.7 1.7 %collective-permute-start.4 = (bf16[1424,128]{1,0:T(8,128)(2,1)S(1)}, bf16[1424,128]{1,0:T(8,128)(2,1)S(1)}, u32[]{:S(2)}, u32[]{:S(2)}) collective-permute-start(bf16[1424,128]{1,0:T(8,128)(2,1)S(1)} %get-tuple-element.39), channel_id=1, source_target_pairs={{0,8},{8,0},{16,24},{24,16},{1,9},{9,1},{17,25},{25,17},{2,10},{10... | collective-permute-start | bytes 1093640 | tf_op jit(solution)/shard_map/ppermute | solution.py:443
  32.5 10.6 %collective-permute-start.5 = (bf16[1424,128]{1,0:T(8,128)(2,1)S(1)}, bf16[1424,128]{1,0:T(8,128)(2,1)S(1)}, u32[]{:S(2)}, u32[]{:S(2)}) collective-permute-start(bf16[1424,128]{1,0:T(8,128)(2,1)S(1)} %shard_map.139.a_ref), channel_id=1, source_target_pairs={{0,16},{8,24},{16,0},{24,8},{1,17},{9,25},{17,1},{25,9},{2,18},{10... | collective-permute-start | bytes 1093640 | tf_op jit(solution)/shard_map/ppermute | solution.py:443
  41.4 1.9 %collective-permute-start.7 = (bf16[928,128]{1,0:T(8,128)(2,1)S(1)}, bf16[928,128]{1,0:T(8,128)(2,1)S(1)}, u32[]{:S(2)}, u32[]{:S(2)}) collective-permute-start(bf16[928,128]{1,0:T(8,128)(2,1)S(1)} %shard_map.142.a_ref), channel_id=1, source_target_pairs={{0,8},{8,0},{16,24},{24,16},{1,9},{9,1},{17,25},{25,17},{2,10},{10... | collective-permute-start | bytes 712712 | tf_op jit(solution)/shard_map/ppermute | solution.py:443
  43.2 1.7 %collective-permute-start.6 = (bf16[1424,128]{1,0:T(8,128)(2,1)S(1)}, bf16[1424,128]{1,0:T(8,128)(2,1)S(1)}, u32[]{:S(2)}, u32[]{:S(2)}) collective-permute-start(bf16[1424,128]{1,0:T(8,128)(2,1)S(1)} %shard_map.140.mine_ref), channel_id=1, source_target_pairs={{0,8},{8,0},{16,24},{24,16},{1,9},{9,1},{17,25},{25,17},{2,10},{10... | collective-permute-start | bytes 1093640 | tf_op jit(solution)/shard_map/ppermute | solution.py:443
  43.4 8.2 %collective-permute-start.8 = (bf16[928,128]{1,0:T(8,128)(2,1)S(1)}, bf16[928,128]{1,0:T(8,128)(2,1)S(1)}, u32[]{:S(2)}, u32[]{:S(2)}) collective-permute-start(bf16[928,128]{1,0:T(8,128)(2,1)S(1)} %shard_map.143.a_ref), channel_id=1, source_target_pairs={{0,16},{8,24},{16,0},{24,8},{1,17},{9,25},{17,1},{25,9},{2,18},{10... | collective-permute-start | bytes 712712 | tf_op jit(solution)/shard_map/ppermute | solution.py:443

commit v4 on v3

--- a/solution.py
+++ b/solution.py
@@ -13,7 +13,6 @@
 LANES = 128
 MIB = 1024 * 1024
 VMEM = pltpu.MemorySpace.VMEM
-SMEM = pltpu.MemorySpace.SMEM
 HBM = pltpu.MemorySpace.HBM
 
 
@@ -114,14 +113,16 @@
     return grouped(w_ref.shape[1], extent, product)
 
 
-def conv_z_back(uz, w_ref, extent):
-    width = w_ref.shape[0] // 27
+def conv_z_back(uz, w_ref, extent, low=0, high=None):
+    every = w_ref.shape[0] // 27
+    high = every if high is None else high
+    width = high - low
 
     def product(groups):
         side = []
         for g in groups:
             taps = [(8 - g) * 3 + 2 - t for t in range(3)]
-            side.append(jnp.concatenate([w_ref[p * width : (p + 1) * width, :] for p in taps], 1))
+            side.append(jnp.concatenate([w_ref[p * every + low : p * every + high, :] for p in taps], 1))
         return dot_t(uz, side[0] if len(side) == 1 else jnp.concatenate(side, 0))
 
     return grouped(width, extent, product)
@@ -154,7 +155,7 @@
     return dot_t(pick, field)
 
 
-def tap_grad(grad, field, extent):
+def tap_shifts(grad, extent):
     nx, ny, nz = extent
     count, rows = grad.shape
     place = lax.broadcasted_iota(jnp.int32, grad.shape, 1)
@@ -171,7 +172,17 @@
                         here = index != (0 if o > 0 else size - 1)
                         inside = here if inside is None else inside & here
                 parts.append(part if inside is None else jnp.where(inside, part, 0.0))
-    return dot(jnp.concatenate(parts, 0).astype(BF), field)
+    return jnp.concatenate(parts, 0).astype(BF)
+
+
+def tap_grad(grad, field, extent):
+    return dot(tap_shifts(grad, extent), field)
+
+
+def split(pack, keep_ref, send_ref, core):
+    size = send_ref.shape[0]
+    keep_ref[0:size, :] = pack[pl.ds(pl.multiple_of(core * size, size), size), :]
+    send_ref[...] = pack[pl.ds(pl.multiple_of((1 - core) * size, size), size), :]
 
 
 def emit(pack_ref, spot, grad, taps=1):
@@ -229,8 +240,8 @@
     second.wait()
 
 
-def stage_kernel(place_ref, near_ref, sources, *refs):
-    del place_ref, near_ref
+def stage_kernel(near_ref, sources, *refs):
+    del near_ref
     *held, arrived = refs
     copies = [pltpu.make_async_copy(a, b, arrived.at[i]) for i, (a, b) in enumerate(zip(sources, held))]
     for copy in copies:
@@ -241,7 +252,6 @@
 
 def upper_kernel(
     geo,
-    place_ref,
     gathered,
     weights,
     decoded_ref,
@@ -254,12 +264,11 @@
     d_ref,
     z3_ref,
     t4_ref,
-    skip_back_ref,
+    ut,
     blocks,
     uv,
     u1,
     uj,
-    ut,
     uc,
     joined,
     lb_ref,
@@ -267,7 +276,7 @@
     pack,
 ):
     (n, sx, ny, nz, c0, c1, c2, masks, spots) = geo
-    position = place_ref[0]
+    position = lax.axis_index("space")
     w_first, w_enc, w_down, w_bottom, w_up, w_join = weights
     shuffle, unshuffle = one_hot(ny, nz, False), one_hot(ny, nz, True)
     plane, nx = ny * nz, sx * n
@@ -322,27 +331,31 @@
 
     cot = jnp.concatenate([blocks[j, vol_rows:, :] for j in range(n)], 0).astype(F32)
     t7 = (cot * slope(z7)).astype(BF)
-    clear_rims(ut, plane)
-    fill(ut, yz_windows(t7.astype(F32), ny, nz), plane)
+    fill(ut, z_windows(t7.astype(F32), nz))
     emit(pack, spots["join"], tap_grad(own_columns(t7, c1 // n, position), joined[...], fine), 27)
-    b7 = conv_back(ut, w_join, rows, plane)
-    skip_back_ref[...] = b7[:, c1:]
-
-    to_blocks(shuffle, b7[:, :c1].astype(BF), lb_ref, cx, cplane)
+    e_lift = conv_z_back(ut[...], w_join, fine, 0, c1).astype(BF)
+    to_blocks(shuffle, e_lift, lb_ref, cx, cplane)
     emit(pack, spots["up"], dot(own_columns(lb_ref[...], 8 * c1 // n, position).astype(BF), g2))
     e3 = dot_t(lb_ref[...], w_up[...]).astype(BF).astype(F32)
     t4 = (e3 * slope(z4)).astype(BF)
     t4_ref[...] = t4
-    emit(pack, spots["bottom"], tap_grad(own_columns(t4, c2 // n, position), g1, coarse), 27)
-    core = place_ref[1]
-    size = keep_ref.shape[0]
-    keep_ref[...] = pack[pl.ds(pl.multiple_of(core * size, size), size), :]
-    send_ref[...] = pack[pl.ds(pl.multiple_of((1 - core) * size, size), size), :]
+    split(pack, keep_ref, send_ref, lax.rem(lax.axis_index("section"), 2))
+    at = send_ref.shape[0]
+    for v in range(0, c2, LANES):
+        keep_ref[at : at + crows, :] = g1[:, v : v + LANES]
+        at += crows
+    mine = own_columns(t4, c2 // n, position).astype(BF)
+    for v in range(0, crows, LANES):
+        keep_ref[at : at + c2 // n, :] = mine[:, v : v + LANES]
+        at += c2 // n
+
+
+def skip_kernel(extent, c1, ut, w_join, out_ref):
+    out_ref[...] = conv_z_back(ut[...], w_join, extent, c1, 2 * c1)
 
 
 def lower_kernel(
     geo,
-    place_ref,
     w_enc,
     w_down,
     w_bottom,
@@ -354,12 +367,14 @@
     z3_ref,
     t4_ref,
     skip_back_ref,
-    pack,
+    keep_ref,
+    send_ref,
     utc,
     ut,
+    pack,
 ):
     (n, sx, ny, nz, c0, c1, c2, masks, spots) = geo
-    position = place_ref[0]
+    position = lax.axis_index("space")
     plane, nx = ny * nz, sx * n
     cplane, cx = plane // 4, nx // 2
     crows = cx * cplane
@@ -390,6 +405,7 @@
         b = taps[(tap + 1) * count : (tap + 2) * count] if tap < 26 else a
         pack[at : at + count, :] = jnp.where(lane < c0, a, b).astype(BF)
         at += count
+    split(pack, keep_ref, send_ref, lax.rem(lax.axis_index("section"), 2))
 
 
 def unpack(source, spot, out, factor):
@@ -401,12 +417,10 @@
         at += count
 
 
-def finish_first(factor, spots, place_ref, mine_ref, other_ref, bottom_ref, up_ref, join_ref, token, both):
-    token[...] = jnp.zeros(token.shape, F32)
-    core = place_ref[1]
-    both[core] = mine_ref[...]
-    both[1 - core] = other_ref[...]
-    size = mine_ref.shape[0]
+def halves(both, mine_ref, other_ref, core):
+    size = both.shape[1]
+    both[core] = mine_ref[0:size, :]
+    both[1 - core] = other_ref[0:size, :]
 
     def source(at, count):
         if (at + count - 1) // size == at // size:
@@ -416,19 +430,45 @@
             [both[0, size - cut : size, :].astype(F32), both[1, 0 : count - cut, :].astype(F32)], 0
         )
 
-    unpack(source, spots["bottom"], bottom_ref, factor)
+    return source
+
+
+def finish_first(
+    factor, spots, extent, mine_ref, other_ref, bottom_ref, up_ref, join_ref, token, both, acts
+):
+    token[...] = jnp.zeros(token.shape, F32)
+    section = lax.axis_index("section")
+    size = both.shape[1]
+    source = halves(both, mine_ref, other_ref, lax.rem(section, 2))
     unpack(source, spots["join"], join_ref, factor)
     rows, width = up_ref.shape[1], up_ref.shape[0]
     for v in range(0, width, LANES):
         up_ref[v : v + LANES, :] = (source(spots["up"] + v // LANES * rows, rows) * factor).T
 
-
-def finish_second(factor, spots, earlier, a_ref, b_ref, first_ref, enc_ref, down_ref):
-    del earlier
-
-    def source(at, count):
-        return a_ref[at : at + count, :].astype(F32) + b_ref[at : at + count, :].astype(F32)
-
+    crops, each = acts.shape[0], acts.shape[1]
+    for j in range(crops // 2):
+        part = slice(size + j * each, size + (j + 1) * each)
+        acts[lax.bitwise_xor(section, 2 * j)] = mine_ref[part, :]
+        acts[lax.bitwise_xor(section, 2 * j + 1)] = other_ref[part, :]
+    voxels = extent[0] * extent[1] * extent[2]
+    count, wide = bottom_ref.shape[0], bottom_ref.shape[1] // 27
+    shifted, fields = [], []
+    for crop in range(crops):
+        at = wide // LANES * voxels
+        fields.append(
+            jnp.concatenate([acts[crop, v : v + voxels, :] for v in range(0, at, voxels)], 1)
+        )
+        own = [acts[crop, v : v + count, :] for v in range(at, each, count)]
+        shifted.append(tap_shifts(jnp.concatenate(own, 1).astype(F32), extent))
+    grad = dot(jnp.concatenate(shifted, 1), jnp.concatenate(fields, 0)) * factor
+    for tap in range(27):
+        bottom_ref[:, tap * wide : (tap + 1) * wide] = grad[tap * count : (tap + 1) * count]
+
+
+def finish_second(
+    factor, spots, mine_ref, other_ref, first_ref, enc_ref, down_ref, both
+):
+    source = halves(both, mine_ref, other_ref, lax.rem(lax.axis_index("section"), 2))
     unpack(source, spots["first"], first_ref, factor)
     unpack(source, spots["enc"], enc_ref, factor)
     unpack(source, spots["down"], down_ref, factor)
@@ -443,12 +483,70 @@
     return lax.ppermute(array, axis, [(i, i ^ mask) for i in range(devices)])
 
 
-def add_kernel(a_ref, b_ref, out_ref):
-    out_ref[...] = (a_ref[...].astype(F32) + b_ref[...].astype(F32)).astype(BF)
-
-
-def add(a, b):
-    return call(add_kernel, [(a.shape, BF)], [], (VMEM, VMEM), vmem=4)(a, b)[0]
+def merge_kernel(size, a_ref, b_ref, *refs):
+    out_ref = refs[-1]
+    out_ref[0:size, :] = (a_ref[0:size, :].astype(F32) + b_ref[0:size, :].astype(F32)).astype(BF)
+    at = size
+    for ref in (a_ref, b_ref):
+        rest = ref.shape[0] - size
+        if rest:
+            out_ref[at : at + rest, :] = ref[size:, :]
+            at += rest
+
+
+def merge(a, b, size, *after):
+    shape = (a.shape[0] + b.shape[0] - size, LANES)
+    kernel = functools.partial(merge_kernel, size)
+    return call(kernel, [(shape, BF)], [], (VMEM,) * (2 + len(after)), vmem=4)(a, b, *after)[0]
+
+
+def between_cores(keep, send, *after):
+    return merge(keep, exchange(send, "section", 1), send.shape[0], *after)
+
+
+def between_chips(total, size, crops, *after):
+    mask = 2
+    while mask < crops:
+        mask *= 2
+        last = after if mask >= crops else ()
+        total = merge(total, exchange(total, "section", mask // 2), size, *last)
+    return total, exchange(total, "section", 1)
+
+
+def in_hbm(array):
+    return pltpu.with_memory_space_constraint(array, HBM)
+
+
+def exchange(array, axis, mask):
+    devices = lax.axis_size(axis)
+    return lax.ppermute(array, axis, [(i, i ^ mask) for i in range(devices)])
+
+
+def merge_kernel(size, a_ref, b_ref, *refs):
+    out_ref = refs[-1]
+    out_ref[0:size, :] = (a_ref[0:size, :].astype(F32) + b_ref[0:size, :].astype(F32)).astype(BF)
+    at = size
+    for ref in (a_ref, b_ref):
+        rest = ref.shape[0] - size
+        if rest:
+            out_ref[at : at + rest, :] = ref[size:, :]
+            at += rest
+
+
+def merge(a, b, size, *after):
+    shape = (a.shape[0] + b.shape[0] - size, LANES)
+    kernel = functools.partial(merge_kernel, size)
+    return call(kernel, [(shape, BF)], [], (VMEM,) * (2 + len(after)), vmem=4)(a, b, *after)[0]
+
+
+def reduced(keep, send, crops, after=()):
+    size = send.shape[0]
+    total = merge(keep, exchange(send, "section", 1), size)
+    mask = 2
+    while mask < crops:
+        mask *= 2
+        total = merge(total, exchange(total, "section", mask // 2), size, *(after if mask >= crops else ()))
+    return total, exchange(total, "section", 1)
 
 
 def stack_kernel(a_ref, b_ref, out_ref):
@@ -481,8 +579,6 @@
     plane, nx = ny * nz, sx * n
     rows = nx * plane
     cplane, crows = plane // 4, rows // 8
-    section = lax.axis_index("section")
-    place = jnp.stack([lax.axis_index("space"), section % 2]).astype(jnp.int32)
     own_rows = sx * plane // 2 + sx * plane
     (near,) = call(
         functools.partial(join_kernel, sx, plane),
@@ -496,11 +592,11 @@
         stage_kernel,
         [(w.shape, BF) for w in weights],
         [pltpu.SemaphoreType.DMA((len(weights),))],
-        (SMEM, VMEM, [HBM] * len(weights)),
+        (VMEM, [HBM] * len(weights)),
         flops=2 * 10**9,
         vmem=12,
     )
-    weights = list(stage(place, near, [in_hbm(w) for w in weights]))
+    weights = list(stage(near, [in_hbm(w) for w in weights]))
     held, step = [0], n // 2
     while step > 2:
         held = held + [m ^ step for m in held]
@@ -528,15 +624,17 @@
             at += count * -(-width // LANES)
         return spots, -(-at // 32) * 32
 
-    upper_spots, upper_rows = layout(("bottom", "up", "join"))
+    upper_spots, upper_rows = layout(("up", "join"))
     lower_spots, lower_rows = layout(("down", "enc", "first"))
     geo = (n, sx, ny, nz, c0, c1, c2, masks)
+    fine, coarse = (nx, ny, nz), (nx // 2, ny // 2, nz // 2)
     size = upper_rows // 2
-    decoded, keep, send, vol2, z1, h1, z2, blocks, z3, t4, skip_back = call(
+    act_rows = c2 // LANES * crows + crows // LANES * wide_own
+    decoded, keep, send, vol2, z1, h1, z2, blocks, z3, t4, ut = call(
         functools.partial(upper_kernel, geo + (upper_spots,)),
         [
             ((sx * plane, c1), BF),
-            ((size, LANES), BF),
+            ((size + act_rows, LANES), BF),
             ((size, LANES), BF),
             ((rows, 2 * c0), BF),
             ((rows, c1), F32),
@@ -545,60 +643,68 @@
             ((crows, 8 * c1), BF),
             ((crows, c2), F32),
             ((crows, c2), BF),
-            ((rows, c1), F32),
+            ((rows, 3 * c1), BF),
         ],
         [
             pltpu.VMEM((n, own_rows, LANES), BF),
             pltpu.VMEM((rows, 2 * LANES), BF),
             pltpu.VMEM((rows, 3 * c1), BF),
             pltpu.VMEM((rows, 6 * c1), BF),
-            pltpu.VMEM((rows + 2 * plane, 9 * c1), BF),
             pltpu.VMEM((crows + 2 * cplane, 9 * c2), BF),
             pltpu.VMEM((rows, 2 * c1), BF),
             pltpu.VMEM((crows, 8 * c1), BF),
             pltpu.VMEM((rows, c1), BF),
             pltpu.VMEM((upper_rows, LANES), BF),
         ],
-        (SMEM, [VMEM] * len(gathered), [VMEM] * len(weights)),
+        ([VMEM] * len(gathered), [VMEM] * len(weights)),
         flops=10**10,
         vmem=14,
-    )(place, gathered, weights)
-    total = add(keep, exchange(send, "section", 1))
-    mask = 2
-    while mask < crops:
-        total = add(total, exchange(total, "section", mask))
-        mask *= 2
-    other = exchange(total, "section", 1)
-
-    (pack,) = call(
+    )(gathered, weights)
+    (skip_back,) = call(
+        functools.partial(skip_kernel, fine, c1),
+        [((rows, c1), F32)],
+        [],
+        (VMEM, VMEM),
+        flops=10**9,
+    )(ut, weights[5])
+    total = between_cores(keep, send, skip_back)
+
+    low_size = lower_rows // 2
+    low_keep, low_send = call(
         functools.partial(lower_kernel, geo + (lower_spots,)),
-        [((lower_rows, LANES), BF)],
-        [pltpu.VMEM((crows + 2 * cplane, 9 * c2), BF), pltpu.VMEM((rows, 3 * c1), BF)],
-        (SMEM,) + (VMEM,) * 11,
+        [((low_size, LANES), BF), ((low_size, LANES), BF)],
+        [
+            pltpu.VMEM((crows + 2 * cplane, 9 * c2), BF),
+            pltpu.VMEM((rows, 3 * c1), BF),
+            pltpu.VMEM((lower_rows, LANES), BF),
+        ],
+        (VMEM,) * 11,
         flops=6 * 10**9,
-    )(place, *weights[1:4], vol2, z1, h1, z2, blocks, z3, t4, skip_back)
-    mask = 1
-    pack_other = exchange(pack, "section", mask)
-    while 2 * mask < crops:
-        pack = add(pack, pack_other)
-        mask *= 2
-        pack_other = exchange(pack, "section", mask)
+    )(*weights[1:4], vol2, z1, h1, z2, blocks, z3, t4, skip_back)
+    total, other = between_chips(total, size, crops, low_send)
 
     factor = 1.0 / math.sqrt(crops * rows)
     grad_bottom, grad_up, grad_join, token = call(
-        functools.partial(finish_first, factor, upper_spots),
-        [(shapes["bottom"], F32), (shapes["up"][::-1], F32), (shapes["join"], F32), ((8, LANES), F32)],
-        [pltpu.VMEM((2, size, LANES), BF)],
-        (SMEM, VMEM, VMEM),
+        functools.partial(finish_first, factor, upper_spots, coarse),
+        [
+            (shapes["bottom"], F32),
+            (shapes["up"][::-1], F32),
+            (shapes["join"], F32),
+            ((8, LANES), F32),
+        ],
+        [pltpu.VMEM((2, size, LANES), BF), pltpu.VMEM((crops, act_rows, LANES), BF)],
+        (VMEM, VMEM),
         vmem=12,
-    )(place, total, other)
+    )(total, other)
+    low_total = between_cores(low_keep, low_send)
+    low_total, low_other = between_chips(low_total, low_size, crops, token)
     grad_first, grad_enc, grad_down = call(
         functools.partial(finish_second, factor, lower_spots),
         [(shapes[name], F32) for name in ("first", "enc", "down")],
-        [],
-        (VMEM, VMEM, VMEM),
+        [pltpu.VMEM((2, low_size, LANES), BF)],
+        (VMEM, VMEM),
         vmem=8,
-    )(token, pack, pack_other)
+    )(low_total, low_other)
     return (
         decoded.reshape((1, sx, ny, nz, c1)),
         grad_first.T,

time: 52.6 us -> 46.5 us (0.88)
  Pallas kernels: 29.4 us -> 25.7 us
  waiting for transfers between devices: 11.2 us -> 9.02 us
    pallas_call x1, Pallas kernels: 14.6 us -> 10.7 us  [body(): call(functools.partial(upper_kernel, geo + (upper_spots,)), [((sx * plane...]
    ppermute x9 -> x10, waiting for transfers between devices: 11.2 us -> 9.02 us  [exchange(): return lax.ppermute(array, axis, [(i, i ^ mask) for i in range(devices)])]
    pallas_call x6 -> x8, Pallas kernels: 13.2 us -> 13.3 us  [the longest x1 6.84 us: body(): call(functools.partial(lower_kernel, geo + (lower_spots,)), [((low_size,...]
    ppermute x9 -> x10, starting transfers between devices: 11 us -> 10.8 us  [exchange(): return lax.ppermute(array, axis, [(i, i ^ mask) for i in range(devices)])]
  transfers between devices with their start and end apart: 9 -> 10, of which waited for: 5 -> 6; matrix products, arithmetic and copies ran while one was open for 0% -> 0% of each run, Pallas kernels for 25% -> 29%
where the time goes in v4:
time: 46.5 us; the launch traced here: 46.3 us
  Pallas kernels  25.7 us (55%)
  starting transfers between devices  10.8 us (23%)
  waiting for transfers between devices  9.02 us (19%)
  between operations  0.72 us (2%)
    ppermute x10, starting transfers between devices, exchange(): return lax.ppermute(array, axis, [(i, i ^ mask) for i in range(devices)])  10.8 us
    pallas_call x1, Pallas kernels, body(): call(functools.partial(upper_kernel, geo + (upper_spots,)), [((sx * plane...  10.7 us
    ppermute x10, waiting for transfers between devices, exchange(): return lax.ppermute(array, axis, [(i, i ^ mask) for i in range(devices)])  9.02 us
    pallas_call x1, Pallas kernels, body(): call(functools.partial(lower_kernel, geo + (lower_spots,)), [((low_size,...  6.84 us
    pallas_call x1, Pallas kernels, body(): weights = list(stage(near, [in_hbm(w) for w in weights]))  3.31 us
    pallas_call x1, Pallas kernels, body(): call(functools.partial(finish_first, factor, upper_spots, coarse), [(shap...  1.6 us
    pallas_call x1, Pallas kernels, body(): call(functools.partial(skip_kernel, fine, c1), [((rows, c1), F32)], [], (...  1.46 us
  transfers between devices with their start and end apart: 10, of which 6 were waited for; matrix products, arithmetic and copies ran while one was open for 0% of the time, Pallas kernels for 29%

profile of v4, /device:TPU:0, one launch (start us, length us, event | category | flops | bytes accessed | tf_op | source)
XLA Modules:
  0.0 46.3 jit_solution(3269506421014396393)
XLA Ops:
  0.6 0.9 %shard_map.135.a_ref.near_ref = bf16[1,192,128]{2,1,0:T(8,128)(2,1)S(1)} custom-call(bf16[2,64,64]{2,1,0:T(8,128)(2,1)} %bitcast.8, bf16[128,128]{1,0:T(8,128)(2,1)} %bitcast.9), custom_call_target="tpu_custom_call" | custom-call | bytes 2097152 | tf_op jit(solution)/shard_map/pallas_call | solution.py:583
  1.5 4.1 %collective-permute-start = (bf16[1,192,128]{2,1,0:T(8,128)(2,1)S(1)}, bf16[1,192,128]{2,1,0:T(8,128)(2,1)S(1)}, u32[]{:S(2)}, u32[]{:S(2)}) collective-permute-start(bf16[1,192,128]{2,1,0:T(8,128)(2,1)S(1)} %shard_map.135.a_ref.near_ref), channel_id=1, source_target_pairs={{0,4},{1,5},{2,6},{3,7},{4,0},{5,1},{6,2},{7,3},{8,12},{9,13},{10,... | collective-permute-start | bytes 147464 | tf_op jit(solution)/shard_map/ppermute | solution.py:522
  5.6 2.6 %collective-permute-done.b_ref = bf16[1,192,128]{2,1,0:T(8,128)(2,1)S(1)} collective-permute-done((bf16[1,192,128]{2,1,0:T(8,128)(2,1)S(1)}, bf16[1,192,128]{2,1,0:T(8,128)(2,1)S(1)}, u32[]{:S(2)}, u32[]{:S(2)}) %collective-permute-start) | collective-permute-done | bytes 49184 | tf_op jit(solution)/shard_map/ppermute | solution.py:522
  8.2 2.4 %collective-permute-start.3 = (bf16[2,192,128]{2,1,0:T(8,128)(2,1)S(1)}, bf16[2,192,128]{2,1,0:T(8,128)(2,1)S(1)}, u32[]{:S(2)}, u32[]{:S(2)}) collective-permute-start(bf16[2,192,128]{2,1,0:T(8,128)(2,1)S(1)} %shard_map.136.gathered_0_), channel_id=1, source_target_pairs={{0,3},{1,2},{2,1},{3,0},{4,7},{5,6},{6,5},{7,4},{8,11},{9,10},{10,... | collective-permute-start | bytes 294920 | tf_op jit(solution)/shard_map/ppermute | solution.py:522
  10.6 0.9 %collective-permute-start.2 = (bf16[2,192,128]{2,1,0:T(8,128)(2,1)S(1)}, bf16[2,192,128]{2,1,0:T(8,128)(2,1)S(1)}, u32[]{:S(2)}, u32[]{:S(2)}) collective-permute-start(bf16[2,192,128]{2,1,0:T(8,128)(2,1)S(1)} %shard_map.136.gathered_0_), channel_id=1, source_target_pairs={{0,2},{1,3},{2,0},{3,1},{4,6},{5,7},{6,4},{7,5},{8,10},{9,11},{10,... | collective-permute-start | bytes 294920 | tf_op jit(solution)/shard_map/ppermute | solution.py:522
  11.5 0.3 collective-permute-start.1
  11.8 3.3 %shard_map.137 = (bf16[1728,128]{1,0:T(8,128)(2,1)S(1)}, bf16[3456,128]{1,0:T(8,128)(2,1)S(1)}, bf16[1024,256]{1,0:T(8,128)(2,1)S(1)}, bf16[6912,256]{1,0:T(8,12...) custom-call(bf16[1,192,128]{2,1,0:T(8,128)(2,1)S(1)} %shard_map.135.a_ref.near_ref, ...), custom_call_target="tpu_custom_call" | custom-call | flops 2000000000 | bytes 2097152 | tf_op jit(solution)/shard_map/pallas_call | solution.py:599
  15.1 0.0 collective-permute-done.3.gathered_3_
  15.1 0.1 collective-permute-done.2.gathered_2_
  15.2 0.9 %collective-permute-done.1.gathered_1_ = bf16[2,192,128]{2,1,0:T(8,128)(2,1)S(1)} collective-permute-done((bf16[2,192,128]{2,1,0:T(8,128)(2,1)S(1)}, bf16[2,192,128]{2,1,0:T(8,128)(2,1)S(1)}, u32[]{:S(2)}, u32[]{:S(2)}) %collective-permute-start.1) | collective-permute-done | bytes 98336 | tf_op jit(solution)/shard_map/ppermute | solution.py:522
  16.1 10.7 %shard_map.138 = (bf16[128,128]{1,0:T(8,128)(2,1)}, bf16[848,128]{1,0:T(8,128)(2,1)S(1)}, bf16[560,128]{1,0:T(8,128)(2,1)S(1)}, bf16[1024,128]{1,0:T(8,128)(2,1)...) custom-call(bf16[2,192,128]{2,1,0:T(8,128)(2,1)S(1)} %shard_map.136., ...), custom_call_target="tpu_custom_call" | custom-call | flops 10000000000 | bytes 2097152 | tf_op jit(solution)/shard_map/pallas_call | solution.py:633
  26.8 0.0 collective-permute-start.6
  26.8 1.5 %shard_map.139.skip_back_ref.refs_0_ = f32[1024,128]{1,0:T(8,128)S(1)} custom-call(bf16[1024,384]{1,0:T(8,128)(2,1)S(1)} %get-tuple-element.47.ut, bf16[6912,128]{1,0:T(8,128)(2,1)S(1)} %get-tuple-element.38.weights_5_.w_join), custom_call_target="tpu_custom_call" | custom-call | flops 1000000000 | bytes 2097152 | tf_op jit(solution)/shard_map/pallas_call | solution.py:663
  28.2 0.0 collective-permute-done.6.b_ref
  28.3 1.6 %collective-permute-start.7 = (bf16[848,128]{1,0:T(8,128)(2,1)S(1)}, bf16[848,128]{1,0:T(8,128)(2,1)S(1)}, u32[]{:S(2)}, u32[]{:S(2)}) collective-permute-start(bf16[848,128]{1,0:T(8,128)(2,1)S(1)} %shard_map.142.a_ref), channel_id=1, source_target_pairs={{0,16},{8,24},{16,0},{24,8},{1,17},{9,25},{17,1},{25,9},{2,18},{10... | collective-permute-start | bytes 651272 | tf_op jit(solution)/shard_map/ppermute | solution.py:522
  29.9 6.8 %shard_map.140 = (bf16[464,128]{1,0:T(8,128)(2,1)S(1)}, bf16[464,128]{1,0:T(8,128)(2,1)S(1)}) custom-call(bf16[3456,128]{1,0:T(8,128)(2,1)S(1)} %get-tuple-element.34.weights_1_.w_enc, bf16[1024,256]{1,0:T(8,128)(2,1)S(1)} %get-tuple-element.35.weights_2_.w_down, bf16[6912,256]{1,0:T(8,128)(2,1)S(1)} %get-tuple-element.36.weights_3_.w_bottom, ...), custom_call_target="tpu_custom_call" | custom-call | flops 6000000000 | bytes 2097152 | tf_op jit(solution)/shard_map/pallas_call | solution.py:673
  36.7 0.0 collective-permute-done.7.b_ref
  36.8 0.3 collective-permute-start.8
  37.1 0.3 collective-permute-start.4
  37.3 1.2 %collective-permute-done.4.b_ref = bf16[464,128]{1,0:T(8,128)(2,1)S(1)} collective-permute-done((bf16[464,128]{1,0:T(8,128)(2,1)S(1)}, bf16[464,128]{1,0:T(8,128)(2,1)S(1)}, u32[]{:S(2)}, u32[]{:S(2)}) %collective-permute-start.4) | collective-permute-done | bytes 118816 | tf_op jit(solution)/shard_map/ppermute | solution.py:522
  38.6 1.0 %collective-permute-start.5 = (bf16[464,128]{1,0:T(8,128)(2,1)S(1)}, bf16[464,128]{1,0:T(8,128)(2,1)S(1)}, u32[]{:S(2)}, u32[]{:S(2)}) collective-permute-start(bf16[464,128]{1,0:T(8,128)(2,1)S(1)} %shard_map.141.a_ref), channel_id=1, source_target_pairs={{0,16},{8,24},{16,0},{24,8},{1,17},{9,25},{17,1},{25,9},{2,18},{10... | collective-permute-start | bytes 356360 | tf_op jit(solution)/shard_map/ppermute | solution.py:522
  39.6 0.0 collective-permute-done.8.other_ref
  39.6 1.6 %shard_map.144 = (f32[32,6912]{1,0:T(8,128)}, f32[256,128]{1,0:T(8,128)}, f32[16,6912]{1,0:T(8,128)}, f32[8,128]{1,0:T(8,128)S(1)}) custom-call(bf16[1136,128]{1,0:T(8,128)(2,1)S(1)} %shard_map.143.mine_ref, bf16[1136,128]{1,0:T(8,128)(2,1)S(1)} %collective-permute-done.8.other_ref), custom_call_target="tpu_custom_call" | custom-call | bytes 2097152 | tf_op jit(solution)/shard_map/pallas_call | solution.py:687
  41.2 2.9 %collective-permute-done.5.b_ref = bf16[464,128]{1,0:T(8,128)(2,1)S(1)} collective-permute-done((bf16[464,128]{1,0:T(8,128)(2,1)S(1)}, bf16[464,128]{1,0:T(8,128)(2,1)S(1)}, u32[]{:S(2)}, u32[]{:S(2)}) %collective-permute-start.5) | collective-permute-done | bytes 118816 | tf_op jit(solution)/shard_map/ppermute | solution.py:522
  44.1 0.1 collective-permute-start.9
  44.2 1.3 %collective-permute-done.9.other_ref = bf16[464,128]{1,0:T(8,128)(2,1)S(1)} collective-permute-done((bf16[464,128]{1,0:T(8,128)(2,1)S(1)}, bf16[464,128]{1,0:T(8,128)(2,1)S(1)}, u32[]{:S(2)}, u32[]{:S(2)}) %collective-permute-start.9) | collective-permute-done | bytes 118816 | tf_op jit(solution)/shard_map/ppermute | solution.py:522
  45.5 0.8 %shard_map.146 = (f32[16,1728]{1,0:T(8,128)}, f32[16,3456]{1,0:T(8,128)}, f32[32,1024]{1,0:T(8,128)}) custom-call(bf16[464,128]{1,0:T(8,128)(2,1)S(1)} %shard_map.145.mine_ref, bf16[464,128]{1,0:T(8,128)(2,1)S(1)} %collective-permute-done.9.other_ref), custom_call_target="tpu_custom_call" | custom-call | bytes 2097152 | tf_op jit(solution)/shard_map/pallas_call | solution.py:701
  (5 shorter events, 0.2 us)
Async XLA Ops:
  1.5 6.7 %collective-permute-start = (bf16[1,192,128]{2,1,0:T(8,128)(2,1)S(1)}, bf16[1,192,128]{2,1,0:T(8,128)(2,1)S(1)}, u32[]{:S(2)}, u32[]{:S(2)}) collective-permute-start(bf16[1,192,128]{2,1,0:T(8,128)(2,1)S(1)} %shard_map.135.a_ref.near_ref), channel_id=1, source_target_pairs={{0,4},{1,5},{2,6},{3,7},{4,0},{5,1},{6,2},{7,3},{8,12},{9,13},{10,... | collective-permute-start | bytes 147464 | tf_op jit(solution)/shard_map/ppermute | solution.py:522
  8.2 6.9 %collective-permute-start.3 = (bf16[2,192,128]{2,1,0:T(8,128)(2,1)S(1)}, bf16[2,192,128]{2,1,0:T(8,128)(2,1)S(1)}, u32[]{:S(2)}, u32[]{:S(2)}) collective-permute-start(bf16[2,192,128]{2,1,0:T(8,128)(2,1)S(1)} %shard_map.136.gathered_0_), channel_id=1, source_target_pairs={{0,3},{1,2},{2,1},{3,0},{4,7},{5,6},{6,5},{7,4},{8,11},{9,10},{10,... | collective-permute-start | bytes 294920 | tf_op jit(solution)/shard_map/ppermute | solution.py:522
  10.6 4.6 %collective-permute-start.2 = (bf16[2,192,128]{2,1,0:T(8,128)(2,1)S(1)}, bf16[2,192,128]{2,1,0:T(8,128)(2,1)S(1)}, u32[]{:S(2)}, u32[]{:S(2)}) collective-permute-start(bf16[2,192,128]{2,1,0:T(8,128)(2,1)S(1)} %shard_map.136.gathered_0_), channel_id=1, source_target_pairs={{0,2},{1,3},{2,0},{3,1},{4,6},{5,7},{6,4},{7,5},{8,10},{9,11},{10,... | collective-permute-start | bytes 294920 | tf_op jit(solution)/shard_map/ppermute | solution.py:522
  11.5 4.6 %collective-permute-start.1 = (bf16[2,192,128]{2,1,0:T(8,128)(2,1)S(1)}, bf16[2,192,128]{2,1,0:T(8,128)(2,1)S(1)}, u32[]{:S(2)}, u32[]{:S(2)}) collective-permute-start(bf16[2,192,128]{2,1,0:T(8,128)(2,1)S(1)} %shard_map.136.gathered_0_), channel_id=1, source_target_pairs={{0,1},{1,0},{2,3},{3,2},{4,5},{5,4},{6,7},{7,6},{8,9},{9,8},{10,11... | collective-permute-start | bytes 294920 | tf_op jit(solution)/shard_map/ppermute | solution.py:522
  26.8 1.5 %collective-permute-start.6 = (bf16[560,128]{1,0:T(8,128)(2,1)S(1)}, bf16[560,128]{1,0:T(8,128)(2,1)S(1)}, u32[]{:S(2)}, u32[]{:S(2)}) collective-permute-start(bf16[560,128]{1,0:T(8,128)(2,1)S(1)} %get-tuple-element.51), channel_id=1, source_target_pairs={{0,8},{8,0},{16,24},{24,16},{1,9},{9,1},{17,25},{25,17},{2,10},{10... | collective-permute-start | bytes 430088 | tf_op jit(solution)/shard_map/ppermute | solution.py:522
  28.3 8.4 %collective-permute-start.7 = (bf16[848,128]{1,0:T(8,128)(2,1)S(1)}, bf16[848,128]{1,0:T(8,128)(2,1)S(1)}, u32[]{:S(2)}, u32[]{:S(2)}) collective-permute-start(bf16[848,128]{1,0:T(8,128)(2,1)S(1)} %shard_map.142.a_ref), channel_id=1, source_target_pairs={{0,16},{8,24},{16,0},{24,8},{1,17},{9,25},{17,1},{25,9},{2,18},{10... | collective-permute-start | bytes 651272 | tf_op jit(solution)/shard_map/ppermute | solution.py:522
  36.8 2.8 %collective-permute-start.8 = (bf16[1136,128]{1,0:T(8,128)(2,1)S(1)}, bf16[1136,128]{1,0:T(8,128)(2,1)S(1)}, u32[]{:S(2)}, u32[]{:S(2)}) collective-permute-start(bf16[1136,128]{1,0:T(8,128)(2,1)S(1)} %shard_map.143.mine_ref), channel_id=1, source_target_pairs={{0,8},{8,0},{16,24},{24,16},{1,9},{9,1},{17,25},{25,17},{2,10},{10... | collective-permute-start | bytes 872456 | tf_op jit(solution)/shard_map/ppermute | solution.py:522
  37.1 1.5 %collective-permute-start.4 = (bf16[464,128]{1,0:T(8,128)(2,1)S(1)}, bf16[464,128]{1,0:T(8,128)(2,1)S(1)}, u32[]{:S(2)}, u32[]{:S(2)}) collective-permute-start(bf16[464,128]{1,0:T(8,128)(2,1)S(1)} %get-tuple-element.49.refs_0_), channel_id=1, source_target_pairs={{0,8},{8,0},{16,24},{24,16},{1,9},{9,1},{17,25},{25,17},{2,10},{10... | collective-permute-start | bytes 356360 | tf_op jit(solution)/shard_map/ppermute | solution.py:522
  38.6 5.4 %collective-permute-start.5 = (bf16[464,128]{1,0:T(8,128)(2,1)S(1)}, bf16[464,128]{1,0:T(8,128)(2,1)S(1)}, u32[]{:S(2)}, u32[]{:S(2)}) collective-permute-start(bf16[464,128]{1,0:T(8,128)(2,1)S(1)} %shard_map.141.a_ref), channel_id=1, source_target_pairs={{0,16},{8,24},{16,0},{24,8},{1,17},{9,25},{17,1},{25,9},{2,18},{10... | collective-permute-start | bytes 356360 | tf_op jit(solution)/shard_map/ppermute | solution.py:522
  44.1 1.4 %collective-permute-start.9 = (bf16[464,128]{1,0:T(8,128)(2,1)S(1)}, bf16[464,128]{1,0:T(8,128)(2,1)S(1)}, u32[]{:S(2)}, u32[]{:S(2)}) collective-permute-start(bf16[464,128]{1,0:T(8,128)(2,1)S(1)} %shard_map.145.mine_ref), channel_id=1, source_target_pairs={{0,8},{8,0},{16,24},{24,16},{1,9},{9,1},{17,25},{25,17},{2,10},{10... | collective-permute-start | bytes 356360 | tf_op jit(solution)/shard_map/ppermute | solution.py:522

commit v5 on v4

--- a/solution.py
+++ b/solution.py
@@ -133,17 +133,6 @@
     total = None
     for ox in range(3):
         part = dot(u_ref[ox * plane : ox * plane + rows, :], w_ref[ox * depth : (ox + 1) * depth, :])
-        total = part if total is None else total + part
-    return total
-
-
-def conv_back(u_ref, w_ref, rows, plane):
-    width = w_ref.shape[0] // 27
-    total = None
-    for ox in range(3):
-        taps = [(2 - ox) * 9 + 8 - t for t in range(9)]
-        flipped = jnp.concatenate([w_ref[tap * width : (tap + 1) * width, :] for tap in taps], axis=1)
-        part = dot_t(u_ref[ox * plane : ox * plane + rows, :], flipped)
         total = part if total is None else total + part
     return total
 
@@ -248,6 +237,22 @@
         copy.start()
     for copy in copies:
         copy.wait()
+
+
+def flip_kernel(near_ref, source, held, flipped, arrived):
+    del near_ref
+    width = source.shape[0] // 27
+    parts = [slice(i * 9 * width, (i + 1) * 9 * width) for i in range(3)]
+    copies = [
+        pltpu.make_async_copy(source.at[part], held.at[part], arrived.at[i]) for i, part in enumerate(parts)
+    ]
+    for copy in copies:
+        copy.start()
+    for i, copy in enumerate(copies):
+        copy.wait()
+        for tap in range(9 * i, 9 * i + 9):
+            to = 26 - tap
+            flipped[to * width : (to + 1) * width, :] = held[tap * width : (tap + 1) * width, :].T
 
 
 def upper_kernel(
@@ -332,13 +337,13 @@
     cot = jnp.concatenate([blocks[j, vol_rows:, :] for j in range(n)], 0).astype(F32)
     t7 = (cot * slope(z7)).astype(BF)
     fill(ut, z_windows(t7.astype(F32), nz))
-    emit(pack, spots["join"], tap_grad(own_columns(t7, c1 // n, position), joined[...], fine), 27)
     e_lift = conv_z_back(ut[...], w_join, fine, 0, c1).astype(BF)
     to_blocks(shuffle, e_lift, lb_ref, cx, cplane)
-    emit(pack, spots["up"], dot(own_columns(lb_ref[...], 8 * c1 // n, position).astype(BF), g2))
     e3 = dot_t(lb_ref[...], w_up[...]).astype(BF).astype(F32)
     t4 = (e3 * slope(z4)).astype(BF)
     t4_ref[...] = t4
+    emit(pack, spots["up"], dot(own_columns(lb_ref[...], 8 * c1 // n, position).astype(BF), g2))
+    emit(pack, spots["join"], tap_grad(own_columns(t7, c1 // n, position), joined[...], fine), 27)
     split(pack, keep_ref, send_ref, lax.rem(lax.axis_index("section"), 2))
     at = send_ref.shape[0]
     for v in range(0, c2, LANES):
@@ -358,20 +363,18 @@
     geo,
     w_enc,
     w_down,
-    w_bottom,
-    vol_ref,
+    back_bottom,
     z1_ref,
-    h1_ref,
     z2_ref,
     d_ref,
     z3_ref,
     t4_ref,
     skip_back_ref,
-    keep_ref,
-    send_ref,
+    pack,
+    t2_ref,
+    t1_ref,
     utc,
     ut,
-    pack,
 ):
     (n, sx, ny, nz, c0, c1, c2, masks, spots) = geo
     position = lax.axis_index("space")
@@ -382,7 +385,7 @@
     unshuffle = one_hot(ny, nz, True)
     clear_rims(utc, cplane)
     fill(utc, yz_windows(t4_ref[...].astype(F32), *coarse[1:]), cplane)
-    e4 = conv_back(utc, w_bottom, crows, cplane).astype(BF).astype(F32)
+    e4 = conv(utc, back_bottom, crows, cplane).astype(BF).astype(F32)
     t3 = (e4 * slope(z3_ref[...])).astype(BF)
     emit(pack, spots["down"], dot(own_columns(t3, c2 // n, position).astype(BF), d_ref[...]))
     e5 = dot_t(t3, w_down[...])
@@ -393,11 +396,19 @@
     )
     t2 = ((e5 + skip_back_ref[...]) * slope(z2_ref[...])).astype(BF)
     fill(ut, z_windows(t2.astype(F32), nz))
-    emit(pack, spots["enc"], tap_grad(own_columns(t2, c1 // n, position), h1_ref[...], fine), 27)
+    t2_ref[...] = t2
     e6 = conv_z_back(ut[...], w_enc, fine).astype(BF).astype(F32)
-    t1 = (e6 * slope(z1_ref[...])).astype(BF)
+    t1_ref[...] = (e6 * slope(z1_ref[...])).astype(BF)
+
+
+def first_kernel(geo, down_ref, t2_ref, t1_ref, h1_ref, vol_ref, keep_ref, send_ref, pack):
+    (n, sx, ny, nz, c0, c1, c2, masks, spots) = geo
+    position = lax.axis_index("space")
+    fine = (sx * n, ny, nz)
     count = c1 // n
-    taps = tap_grad(own_columns(t1, count, position), vol_ref[...], fine)
+    pack[0 : down_ref.shape[0], :] = down_ref[...]
+    emit(pack, spots["enc"], tap_grad(own_columns(t2_ref[...], count, position), h1_ref[...], fine), 27)
+    taps = tap_grad(own_columns(t1_ref[...], count, position), vol_ref[...], fine)
     lane = lax.broadcasted_iota(jnp.int32, (count, LANES), 1)
     at = spots["first"]
     for tap in range(0, 27, 2):
@@ -465,22 +476,11 @@
         bottom_ref[:, tap * wide : (tap + 1) * wide] = grad[tap * count : (tap + 1) * count]
 
 
-def finish_second(
-    factor, spots, mine_ref, other_ref, first_ref, enc_ref, down_ref, both
-):
+def finish_second(factor, spots, mine_ref, other_ref, first_ref, enc_ref, down_ref, both):
     source = halves(both, mine_ref, other_ref, lax.rem(lax.axis_index("section"), 2))
+    unpack(source, spots["down"], down_ref, factor)
     unpack(source, spots["first"], first_ref, factor)
     unpack(source, spots["enc"], enc_ref, factor)
-    unpack(source, spots["down"], down_ref, factor)
-
-
-def in_hbm(array):
-    return pltpu.with_memory_space_constraint(array, HBM)
-
-
-def exchange(array, axis, mask):
-    devices = lax.axis_size(axis)
-    return lax.ppermute(array, axis, [(i, i ^ mask) for i in range(devices)])
 
 
 def merge_kernel(size, a_ref, b_ref, *refs):
@@ -549,14 +549,15 @@
     return total, exchange(total, "section", 1)
 
 
-def stack_kernel(a_ref, b_ref, out_ref):
+def stack_kernel(a_ref, b_ref, *refs):
+    out_ref = refs[-1]
     out_ref[0 : a_ref.shape[0]] = a_ref[...]
     out_ref[a_ref.shape[0] :] = b_ref[...]
 
 
-def stack(a, b):
+def stack(a, b, *after):
     shape = (a.shape[0] + b.shape[0],) + a.shape[1:]
-    return call(stack_kernel, [(shape, BF)], [], (VMEM, VMEM), vmem=4)(a, b)[0]
+    return call(stack_kernel, [(shape, BF)], [], (VMEM,) * (2 + len(after)), vmem=4)(a, b, *after)[0]
 
 
 def call(kernel, outs, scratch, spaces, flops=0, vmem=12):
@@ -587,21 +588,27 @@
         (HBM, HBM),
         vmem=4,
     )(in_hbm(volume.reshape(sx, plane, c0)), in_hbm(cotangent.reshape(sx * plane, c1)))
-    weights = [w_first, w_enc, w_down, w_bottom, w_up, w_join]
-    stage = call(
+    held_bottom, back_bottom = call(
+        flip_kernel,
+        [(w_bottom.shape, BF)] * 2,
+        [pltpu.SemaphoreType.DMA((3,))],
+        (VMEM, HBM),
+        flops=10**9,
+    )(near, in_hbm(w_bottom))
+    held, step = [0], n // 2
+    while step > 2:
+        held = held + [m ^ step for m in held]
+        near = stack(near, exchange(near, "space", step), back_bottom)
+        step //= 2
+    weights = [w_first, w_enc, w_down, w_up, w_join]
+    weights = call(
         stage_kernel,
         [(w.shape, BF) for w in weights],
         [pltpu.SemaphoreType.DMA((len(weights),))],
         (VMEM, [HBM] * len(weights)),
-        flops=2 * 10**9,
-        vmem=12,
-    )
-    weights = list(stage(near, [in_hbm(w) for w in weights]))
-    held, step = [0], n // 2
-    while step > 2:
-        held = held + [m ^ step for m in held]
-        near = stack(near, exchange(near, "space", step))
-        step //= 2
+        flops=10**9,
+    )(near, [in_hbm(w) for w in weights])
+    weights = [*weights[:3], held_bottom, *weights[3:]]
     last = range(1, min(n, 4))
     gathered = [near] + [exchange(near, "space", mask) for mask in last]
     masks = tuple(tuple(m ^ mask for m in held) for mask in (0, *last))
@@ -670,19 +677,22 @@
     total = between_cores(keep, send, skip_back)
 
     low_size = lower_rows // 2
+    down, t2, t1 = call(
+        functools.partial(lower_kernel, geo + (lower_spots,)),
+        [((lower_spots["enc"], LANES), BF), ((rows, c1), BF), ((rows, c1), BF)],
+        [pltpu.VMEM((crows + 2 * cplane, 9 * c2), BF), pltpu.VMEM((rows, 3 * c1), BF)],
+        (VMEM,) * 9,
+        flops=6 * 10**9,
+    )(weights[1], weights[2], back_bottom, z1, z2, blocks, z3, t4, skip_back)
     low_keep, low_send = call(
-        functools.partial(lower_kernel, geo + (lower_spots,)),
+        functools.partial(first_kernel, geo + (lower_spots,)),
         [((low_size, LANES), BF), ((low_size, LANES), BF)],
-        [
-            pltpu.VMEM((crows + 2 * cplane, 9 * c2), BF),
-            pltpu.VMEM((rows, 3 * c1), BF),
-            pltpu.VMEM((lower_rows, LANES), BF),
-        ],
-        (VMEM,) * 11,
-        flops=6 * 10**9,
-    )(*weights[1:4], vol2, z1, h1, z2, blocks, z3, t4, skip_back)
-    total, other = between_chips(total, size, crops, low_send)
-
+        [pltpu.VMEM((lower_rows, LANES), BF)],
+        (VMEM,) * 5,
+        flops=10**9,
+    )(down, t2, t1, h1, vol2)
+    low_total = between_cores(low_keep, low_send)
+    total, other = between_chips(total, size, crops, low_total)
     factor = 1.0 / math.sqrt(crops * rows)
     grad_bottom, grad_up, grad_join, token = call(
         functools.partial(finish_first, factor, upper_spots, coarse),
@@ -696,7 +706,6 @@
         (VMEM, VMEM),
         vmem=12,
     )(total, other)
-    low_total = between_cores(low_keep, low_send)
     low_total, low_other = between_chips(low_total, low_size, crops, token)
     grad_first, grad_enc, grad_down = call(
         functools.partial(finish_second, factor, lower_spots),

time: 46.5 us -> 44.2 us (0.951)
  waiting for transfers between devices: 9.02 us -> 7.34 us
  Pallas kernels: 25.7 us -> 24.8 us
    ppermute x10, waiting for transfers between devices: 9.02 us -> 7.34 us  [exchange(): return lax.ppermute(array, axis, [(i, i ^ mask) for i in range(devices)])]
    pallas_call x3 -> x5, Pallas kernels: 10.1 us -> 9.58 us  [the longest x1 4 us: body(): call(functools.partial(lower_kernel, geo + (lower_spots,)), [((lower_spot...]
  transfers between devices with their start and end apart: 10 -> 10, of which waited for: 6 -> 8; matrix products, arithmetic and copies ran while one was open for 0% -> 0% of each run, Pallas kernels for 29% -> 29%
where the time goes in v5:
time: 44.2 us; the launch traced here: 44 us
  Pallas kernels  24.8 us (56%)
  starting transfers between devices  11.1 us (25%)
  waiting for transfers between devices  7.34 us (17%)
  between operations  0.73 us (2%)
    ppermute x10, starting transfers between devices, exchange(): return lax.ppermute(array, axis, [(i, i ^ mask) for i in range(devices)])  11.1 us
    pallas_call x1, Pallas kernels, body(): call(functools.partial(upper_kernel, geo + (upper_spots,)), [((sx * plane...  10.3 us
    ppermute x10, waiting for transfers between devices, exchange(): return lax.ppermute(array, axis, [(i, i ^ mask) for i in range(devices)])  7.34 us
    pallas_call x1, Pallas kernels, body(): call(functools.partial(lower_kernel, geo + (lower_spots,)), [((lower_spot...  4 us
    pallas_call x1, Pallas kernels, body(): call(flip_kernel, [(w_bottom.shape, BF)] * 2, [pltpu.SemaphoreType.DMA((3...  2.37 us
    pallas_call x1, Pallas kernels, body(): call(stage_kernel, [(w.shape, BF) for w in weights], [pltpu.SemaphoreType...  2.25 us
    pallas_call x1, Pallas kernels, body(): call(functools.partial(finish_first, factor, upper_spots, coarse), [(shap...  1.59 us
    pallas_call x1, Pallas kernels, body(): call(functools.partial(skip_kernel, fine, c1), [((rows, c1), F32)], [], (...  1.47 us
  transfers between devices with their start and end apart: 10, of which 8 were waited for; matrix products, arithmetic and copies ran while one was open for 0% of the time, Pallas kernels for 29%

profile of v5, /device:TPU:0, one launch (start us, length us, event | category | flops | bytes accessed | tf_op | source)
XLA Modules:
  0.0 44.0 jit_solution(11250014955035204878)
XLA Ops:
  0.6 0.9 %shard_map.135.near_ref.a_ref = bf16[1,192,128]{2,1,0:T(8,128)(2,1)S(1)} custom-call(bf16[2,64,64]{2,1,0:T(8,128)(2,1)} %bitcast.8, bf16[128,128]{1,0:T(8,128)(2,1)} %bitcast.9), custom_call_target="tpu_custom_call" | custom-call | bytes 2097152 | tf_op jit(solution)/shard_map/pallas_call | solution.py:584
  1.5 4.1 %collective-permute-start = (bf16[1,192,128]{2,1,0:T(8,128)(2,1)S(1)}, bf16[1,192,128]{2,1,0:T(8,128)(2,1)S(1)}, u32[]{:S(2)}, u32[]{:S(2)}) collective-permute-start(bf16[1,192,128]{2,1,0:T(8,128)(2,1)S(1)} %shard_map.135.near_ref.a_ref), channel_id=1, source_target_pairs={{0,4},{1,5},{2,6},{3,7},{4,0},{5,1},{6,2},{7,3},{8,12},{9,13},{10,... | collective-permute-start | bytes 147464 | tf_op jit(solution)/shard_map/ppermute | solution.py:522
  5.6 2.4 %shard_map.136 = (bf16[6912,256]{1,0:T(8,128)(2,1)S(1)}, bf16[6912,256]{1,0:T(8,128)(2,1)S(1)}) custom-call(bf16[1,192,128]{2,1,0:T(8,128)(2,1)S(1)} %shard_map.135.near_ref.a_ref, bf16[6912,256]{1,0:T(8,128)(2,1)} %source.1), custom_call_target="tpu_custom_call" | custom-call | flops 1000000000 | bytes 2097152 | tf_op jit(solution)/shard_map/pallas_call | solution.py:591
  8.0 0.2 collective-permute-done.b_ref
  8.2 2.4 %collective-permute-start.3 = (bf16[2,192,128]{2,1,0:T(8,128)(2,1)S(1)}, bf16[2,192,128]{2,1,0:T(8,128)(2,1)S(1)}, u32[]{:S(2)}, u32[]{:S(2)}) collective-permute-start(bf16[2,192,128]{2,1,0:T(8,128)(2,1)S(1)} %shard_map.137.near_ref.gathered_0_), channel_id=1, source_target_pairs={{0,3},{1,2},{2,1},{3,0},{4,7},{5,6},{6,5},{7,4},{8,11},{9,10},{10,... | collective-permute-start | bytes 294920 | tf_op jit(solution)/shard_map/ppermute | solution.py:522
  10.6 0.9 %collective-permute-start.2 = (bf16[2,192,128]{2,1,0:T(8,128)(2,1)S(1)}, bf16[2,192,128]{2,1,0:T(8,128)(2,1)S(1)}, u32[]{:S(2)}, u32[]{:S(2)}) collective-permute-start(bf16[2,192,128]{2,1,0:T(8,128)(2,1)S(1)} %shard_map.137.near_ref.gathered_0_), channel_id=1, source_target_pairs={{0,2},{1,3},{2,0},{3,1},{4,6},{5,7},{6,4},{7,5},{8,10},{9,11},{10,... | collective-permute-start | bytes 294920 | tf_op jit(solution)/shard_map/ppermute | solution.py:522
  11.5 0.3 collective-permute-start.1
  11.8 2.2 %shard_map.138 = (bf16[1728,128]{1,0:T(8,128)(2,1)S(1)}, bf16[3456,128]{1,0:T(8,128)(2,1)S(1)}, bf16[1024,256]{1,0:T(8,128)(2,1)S(1)}, bf16[256,1024]{1,0:T(8,128)(2,1)S(1)}, bf16[6912,128]{1,0:T(8,128)(2,1)S(1)}) custom-call(bf16[2,192,128]{2,1,0:T(8,128)(2,1)S(1)} %shard_map.137.near_ref.gathered_0_, bf16[1728,128]{1,0:T(8,128)(2,1)} %sources_0_.1, ...), custom_call_target="tpu_custom_call" | custom-call | flops 1000000000 | bytes 2097152 | tf_op jit(solution)/shard_map/pallas_call | solution.py:604
  14.0 0.6 %collective-permute-done.3.gathered_3_ = bf16[2,192,128]{2,1,0:T(8,128)(2,1)S(1)} collective-permute-done((bf16[2,192,128]{2,1,0:T(8,128)(2,1)S(1)}, bf16[2,192,128]{2,1,0:T(8,128)(2,1)S(1)}, u32[]{:S(2)}, u32[]{:S(2)}) %collective-permute-start.3) | collective-permute-done | bytes 98336 | tf_op jit(solution)/shard_map/ppermute | solution.py:522
  14.6 1.0 %collective-permute-done.2.gathered_2_ = bf16[2,192,128]{2,1,0:T(8,128)(2,1)S(1)} collective-permute-done((bf16[2,192,128]{2,1,0:T(8,128)(2,1)S(1)}, bf16[2,192,128]{2,1,0:T(8,128)(2,1)S(1)}, u32[]{:S(2)}, u32[]{:S(2)}) %collective-permute-start.2) | collective-permute-done | bytes 98336 | tf_op jit(solution)/shard_map/ppermute | solution.py:522
  15.6 0.4 %collective-permute-done.1.gathered_1_ = bf16[2,192,128]{2,1,0:T(8,128)(2,1)S(1)} collective-permute-done((bf16[2,192,128]{2,1,0:T(8,128)(2,1)S(1)}, bf16[2,192,128]{2,1,0:T(8,128)(2,1)S(1)}, u32[]{:S(2)}, u32[]{:S(2)}) %collective-permute-start.1) | collective-permute-done | bytes 98336 | tf_op jit(solution)/shard_map/ppermute | solution.py:522
  16.1 10.3 %shard_map.139 = (bf16[128,128]{1,0:T(8,128)(2,1)}, bf16[848,128]{1,0:T(8,128)(2,1)S(1)}, bf16[560,128]{1,0:T(8,128)(2,1)S(1)}, bf16[1024,128]{1,0:T(8,128)(2,1)...) custom-call(bf16[2,192,128]{2,1,0:T(8,128)(2,1)S(1)} %shard_map.137., ...), custom_call_target="tpu_custom_call" | custom-call | flops 10000000000 | bytes 2097152 | tf_op jit(solution)/shard_map/pallas_call | solution.py:640
  26.4 0.1 collective-permute-start.6
  26.5 1.5 %shard_map.140.skip_back_ref.refs_0_ = f32[1024,128]{1,0:T(8,128)S(1)} custom-call(bf16[1024,384]{1,0:T(8,128)(2,1)S(1)} %get-tuple-element.50.ut, bf16[6912,128]{1,0:T(8,128)(2,1)S(1)} %get-tuple-element.43.weights_5_.w_join), custom_call_target="tpu_custom_call" | custom-call | flops 1000000000 | bytes 2097152 | tf_op jit(solution)/shard_map/pallas_call | solution.py:670
  28.0 0.0 collective-permute-done.6.b_ref
  28.0 1.6 %collective-permute-start.7 = (bf16[848,128]{1,0:T(8,128)(2,1)S(1)}, bf16[848,128]{1,0:T(8,128)(2,1)S(1)}, u32[]{:S(2)}, u32[]{:S(2)}) collective-permute-start(bf16[848,128]{1,0:T(8,128)(2,1)S(1)} %shard_map.144.a_ref), channel_id=1, source_target_pairs={{0,16},{8,24},{16,0},{24,8},{1,17},{9,25},{17,1},{25,9},{2,18},{10... | collective-permute-start | bytes 651272 | tf_op jit(solution)/shard_map/ppermute | solution.py:522
  29.6 4.0 %shard_map.141 = (bf16[256,128]{1,0:T(8,128)(2,1)S(1)}, bf16[1024,128]{1,0:T(8,128)(2,1)S(1)}, bf16[1024,128]{1,0:T(8,128)(2,1)S(1)}) custom-call(bf16[3456,128]{1,0:T(8,128)(2,1)S(1)} %get-tuple-element.39.weights_1_.w_enc, bf16[1024,256]{1,0:T(8,128)(2,1)S(1)} %get-tuple-element.40.weights_2_.w_down, ...), custom_call_target="tpu_custom_call" | custom-call | flops 6000000000 | bytes 2097152 | tf_op jit(solution)/shard_map/pallas_call | solution.py:680
  33.6 1.0 %shard_map.142 = (bf16[464,128]{1,0:T(8,128)(2,1)S(1)}, bf16[464,128]{1,0:T(8,128)(2,1)S(1)}) custom-call(bf16[256,128]{1,0:T(8,128)(2,1)S(1)} %get-tuple-element.51.down_ref, bf16[1024,128]{1,0:T(8,128)(2,1)S(1)} %get-tuple-element.52.t2_ref, bf16[1024,128]{1,0:T(8,128)(2,1)S(1)} %get-tuple-element.53.t1_ref, ...), custom_call_target="tpu_custom_call" | custom-call | flops 1000000000 | bytes 2097152 | tf_op jit(solution)/shard_map/pallas_call | solution.py:687
  34.5 0.3 collective-permute-start.4
  34.8 1.1 %collective-permute-done.4.b_ref = bf16[464,128]{1,0:T(8,128)(2,1)S(1)} collective-permute-done((bf16[464,128]{1,0:T(8,128)(2,1)S(1)}, bf16[464,128]{1,0:T(8,128)(2,1)S(1)}, u32[]{:S(2)}, u32[]{:S(2)}) %collective-permute-start.4) | collective-permute-done | bytes 118816 | tf_op jit(solution)/shard_map/ppermute | solution.py:522
  36.0 0.0 collective-permute-done.7.b_ref
  36.0 0.3 collective-permute-start.8
  36.3 1.2 %collective-permute-start.5 = (bf16[464,128]{1,0:T(8,128)(2,1)S(1)}, bf16[464,128]{1,0:T(8,128)(2,1)S(1)}, u32[]{:S(2)}, u32[]{:S(2)}) collective-permute-start(bf16[464,128]{1,0:T(8,128)(2,1)S(1)} %shard_map.143.refs_0_.a_ref), channel_id=1, source_target_pairs={{0,16},{8,24},{16,0},{24,8},{1,17},{9,25},{17,1},{25,9},{2,18},{10... | collective-permute-start | bytes 356360 | tf_op jit(solution)/shard_map/ppermute | solution.py:522
  37.5 0.2 collective-permute-done.8.other_ref
  37.7 1.6 %shard_map.146 = (f32[32,6912]{1,0:T(8,128)}, f32[256,128]{1,0:T(8,128)}, f32[16,6912]{1,0:T(8,128)}, f32[8,128]{1,0:T(8,128)S(1)}) custom-call(bf16[1136,128]{1,0:T(8,128)(2,1)S(1)} %shard_map.145.mine_ref, bf16[1136,128]{1,0:T(8,128)(2,1)S(1)} %collective-permute-done.8.other_ref), custom_call_target="tpu_custom_call" | custom-call | bytes 2097152 | tf_op jit(solution)/shard_map/pallas_call | solution.py:697
  39.3 2.5 %collective-permute-done.5.b_ref = bf16[464,128]{1,0:T(8,128)(2,1)S(1)} collective-permute-done((bf16[464,128]{1,0:T(8,128)(2,1)S(1)}, bf16[464,128]{1,0:T(8,128)(2,1)S(1)}, u32[]{:S(2)}, u32[]{:S(2)}) %collective-permute-start.5) | collective-permute-done | bytes 118816 | tf_op jit(solution)/shard_map/ppermute | solution.py:522
  41.8 0.1 collective-permute-start.9
  41.9 1.3 %collective-permute-done.9.other_ref = bf16[464,128]{1,0:T(8,128)(2,1)S(1)} collective-permute-done((bf16[464,128]{1,0:T(8,128)(2,1)S(1)}, bf16[464,128]{1,0:T(8,128)(2,1)S(1)}, u32[]{:S(2)}, u32[]{:S(2)}) %collective-permute-start.9) | collective-permute-done | bytes 118816 | tf_op jit(solution)/shard_map/ppermute | solution.py:522
  43.2 0.8 %shard_map.148 = (f32[16,1728]{1,0:T(8,128)}, f32[16,3456]{1,0:T(8,128)}, f32[32,1024]{1,0:T(8,128)}) custom-call(bf16[464,128]{1,0:T(8,128)(2,1)S(1)} %shard_map.147.mine_ref, bf16[464,128]{1,0:T(8,128)(2,1)S(1)} %collective-permute-done.9.other_ref), custom_call_target="tpu_custom_call" | custom-call | bytes 2097152 | tf_op jit(solution)/shard_map/pallas_call | solution.py:710
  (5 shorter events, 0.2 us)
Async XLA Ops:
  1.5 6.7 %collective-permute-start = (bf16[1,192,128]{2,1,0:T(8,128)(2,1)S(1)}, bf16[1,192,128]{2,1,0:T(8,128)(2,1)S(1)}, u32[]{:S(2)}, u32[]{:S(2)}) collective-permute-start(bf16[1,192,128]{2,1,0:T(8,128)(2,1)S(1)} %shard_map.135.near_ref.a_ref), channel_id=1, source_target_pairs={{0,4},{1,5},{2,6},{3,7},{4,0},{5,1},{6,2},{7,3},{8,12},{9,13},{10,... | collective-permute-start | bytes 147464 | tf_op jit(solution)/shard_map/ppermute | solution.py:522
  8.2 6.4 %collective-permute-start.3 = (bf16[2,192,128]{2,1,0:T(8,128)(2,1)S(1)}, bf16[2,192,128]{2,1,0:T(8,128)(2,1)S(1)}, u32[]{:S(2)}, u32[]{:S(2)}) collective-permute-start(bf16[2,192,128]{2,1,0:T(8,128)(2,1)S(1)} %shard_map.137.near_ref.gathered_0_), channel_id=1, source_target_pairs={{0,3},{1,2},{2,1},{3,0},{4,7},{5,6},{6,5},{7,4},{8,11},{9,10},{10,... | collective-permute-start | bytes 294920 | tf_op jit(solution)/shard_map/ppermute | solution.py:522
  10.6 5.0 %collective-permute-start.2 = (bf16[2,192,128]{2,1,0:T(8,128)(2,1)S(1)}, bf16[2,192,128]{2,1,0:T(8,128)(2,1)S(1)}, u32[]{:S(2)}, u32[]{:S(2)}) collective-permute-start(bf16[2,192,128]{2,1,0:T(8,128)(2,1)S(1)} %shard_map.137.near_ref.gathered_0_), channel_id=1, source_target_pairs={{0,2},{1,3},{2,0},{3,1},{4,6},{5,7},{6,4},{7,5},{8,10},{9,11},{10,... | collective-permute-start | bytes 294920 | tf_op jit(solution)/shard_map/ppermute | solution.py:522
  11.5 4.6 %collective-permute-start.1 = (bf16[2,192,128]{2,1,0:T(8,128)(2,1)S(1)}, bf16[2,192,128]{2,1,0:T(8,128)(2,1)S(1)}, u32[]{:S(2)}, u32[]{:S(2)}) collective-permute-start(bf16[2,192,128]{2,1,0:T(8,128)(2,1)S(1)} %shard_map.137.near_ref.gathered_0_), channel_id=1, source_target_pairs={{0,1},{1,0},{2,3},{3,2},{4,5},{5,4},{6,7},{7,6},{8,9},{9,8},{10,11... | collective-permute-start | bytes 294920 | tf_op jit(solution)/shard_map/ppermute | solution.py:522
  26.4 1.6 %collective-permute-start.6 = (bf16[560,128]{1,0:T(8,128)(2,1)S(1)}, bf16[560,128]{1,0:T(8,128)(2,1)S(1)}, u32[]{:S(2)}, u32[]{:S(2)}) collective-permute-start(bf16[560,128]{1,0:T(8,128)(2,1)S(1)} %get-tuple-element.59), channel_id=1, source_target_pairs={{0,8},{8,0},{16,24},{24,16},{1,9},{9,1},{17,25},{25,17},{2,10},{10... | collective-permute-start | bytes 430088 | tf_op jit(solution)/shard_map/ppermute | solution.py:522
  28.0 8.0 %collective-permute-start.7 = (bf16[848,128]{1,0:T(8,128)(2,1)S(1)}, bf16[848,128]{1,0:T(8,128)(2,1)S(1)}, u32[]{:S(2)}, u32[]{:S(2)}) collective-permute-start(bf16[848,128]{1,0:T(8,128)(2,1)S(1)} %shard_map.144.a_ref), channel_id=1, source_target_pairs={{0,16},{8,24},{16,0},{24,8},{1,17},{9,25},{17,1},{25,9},{2,18},{10... | collective-permute-start | bytes 651272 | tf_op jit(solution)/shard_map/ppermute | solution.py:522
  34.5 1.4 %collective-permute-start.4 = (bf16[464,128]{1,0:T(8,128)(2,1)S(1)}, bf16[464,128]{1,0:T(8,128)(2,1)S(1)}, u32[]{:S(2)}, u32[]{:S(2)}) collective-permute-start(bf16[464,128]{1,0:T(8,128)(2,1)S(1)} %get-tuple-element.57), channel_id=1, source_target_pairs={{0,8},{8,0},{16,24},{24,16},{1,9},{9,1},{17,25},{25,17},{2,10},{10... | collective-permute-start | bytes 356360 | tf_op jit(solution)/shard_map/ppermute | solution.py:522
  36.0 1.6 %collective-permute-start.8 = (bf16[1136,128]{1,0:T(8,128)(2,1)S(1)}, bf16[1136,128]{1,0:T(8,128)(2,1)S(1)}, u32[]{:S(2)}, u32[]{:S(2)}) collective-permute-start(bf16[1136,128]{1,0:T(8,128)(2,1)S(1)} %shard_map.145.mine_ref), channel_id=1, source_target_pairs={{0,8},{8,0},{16,24},{24,16},{1,9},{9,1},{17,25},{25,17},{2,10},{10... | collective-permute-start | bytes 872456 | tf_op jit(solution)/shard_map/ppermute | solution.py:522
  36.3 5.4 %collective-permute-start.5 = (bf16[464,128]{1,0:T(8,128)(2,1)S(1)}, bf16[464,128]{1,0:T(8,128)(2,1)S(1)}, u32[]{:S(2)}, u32[]{:S(2)}) collective-permute-start(bf16[464,128]{1,0:T(8,128)(2,1)S(1)} %shard_map.143.refs_0_.a_ref), channel_id=1, source_target_pairs={{0,16},{8,24},{16,0},{24,8},{1,17},{9,25},{17,1},{25,9},{2,18},{10... | collective-permute-start | bytes 356360 | tf_op jit(solution)/shard_map/ppermute | solution.py:522
  41.8 1.4 %collective-permute-start.9 = (bf16[464,128]{1,0:T(8,128)(2,1)S(1)}, bf16[464,128]{1,0:T(8,128)(2,1)S(1)}, u32[]{:S(2)}, u32[]{:S(2)}) collective-permute-start(bf16[464,128]{1,0:T(8,128)(2,1)S(1)} %shard_map.147.mine_ref), channel_id=1, source_target_pairs={{0,8},{8,0},{16,24},{24,16},{1,9},{9,1},{17,25},{25,17},{2,10},{10... | collective-permute-start | bytes 356360 | tf_op jit(solution)/shard_map/ppermute | solution.py:522

commit v6 on v5

--- a/solution.py
+++ b/solution.py
@@ -25,7 +25,7 @@
 
 
 def sigmoid(z):
-    return 1.0 / (1.0 + jnp.exp(-z))
+    return jax.nn.sigmoid(z)
 
 
 def silu(z):
@@ -37,9 +37,19 @@
     return s * (1.0 + z * (1.0 - s))
 
 
+def mod(index, size):
+    return index & (size - 1) if size & (size - 1) == 0 else lax.rem(index, size)
+
+
+def over(index, size):
+    if size & (size - 1) == 0:
+        return lax.shift_right_logical(index, size.bit_length() - 1)
+    return lax.div(index, size)
+
+
 def z_windows(field, size_z):
     rows = field.shape[0]
-    at_z = lax.rem(lax.broadcasted_iota(jnp.int32, field.shape, 0), size_z)
+    at_z = mod(lax.broadcasted_iota(jnp.int32, field.shape, 0), size_z)
     out = []
     for oz in (-1, 0, 1):
         part = field
@@ -53,7 +63,7 @@
 def yz_windows(field, size_y, size_z):
     rows = field.shape[0]
     place = lax.broadcasted_iota(jnp.int32, field.shape, 0)
-    at_y = lax.rem(lax.div(place, size_z), size_y)
+    at_y = mod(over(place, size_z), size_y)
     shifted = z_windows(field, size_z)
     out = []
     for oy in (-1, 0, 1):
@@ -148,7 +158,7 @@
     nx, ny, nz = extent
     count, rows = grad.shape
     place = lax.broadcasted_iota(jnp.int32, grad.shape, 1)
-    at = (lax.div(place, ny * nz), lax.rem(lax.div(place, nz), ny), lax.rem(place, nz))
+    at = (over(place, ny * nz), mod(over(place, nz), ny), mod(place, nz))
     parts = []
     for ox in (-1, 0, 1):
         for oy in (-1, 0, 1):
@@ -191,9 +201,9 @@
     shape = (2 * plane, 2 * plane)
     row = lax.broadcasted_iota(jnp.int32, shape, 1 if back else 0)
     column = lax.broadcasted_iota(jnp.int32, shape, 0 if back else 1)
-    tap, at = lax.div(row, plane // 4), lax.rem(row, plane // 4)
-    ox, oy, oz = lax.div(tap, 4), lax.rem(lax.div(tap, 2), 2), lax.rem(tap, 2)
-    y, z = lax.div(at, nz // 2), lax.rem(at, nz // 2)
+    tap, at = over(row, plane // 4), mod(row, plane // 4)
+    ox, oy, oz = over(tap, 4), mod(over(tap, 2), 2), mod(tap, 2)
+    y, z = over(at, nz // 2), mod(at, nz // 2)
     wanted = ox * plane + (2 * y + oy) * nz + 2 * z + oz
     return (column == wanted).astype(F32).astype(BF)
 
@@ -259,7 +269,7 @@
     geo,
     gathered,
     weights,
-    decoded_ref,
+    own_ref,
     keep_ref,
     send_ref,
     vol_ref,
@@ -332,7 +342,7 @@
     z7 = conv_z(uj[...], w_join, fine)
     out_map[...] = silu(z7)
     kept = sx * plane
-    decoded_ref[...] = out_map[pl.ds(pl.multiple_of(position * kept, kept), kept), :]
+    own_ref[...] = out_map[pl.ds(pl.multiple_of(position * kept, kept), kept), :]
 
     cot = jnp.concatenate([blocks[j, vol_rows:, :] for j in range(n)], 0).astype(F32)
     t7 = (cot * slope(z7)).astype(BF)
@@ -444,9 +454,9 @@
     return source
 
 
-def finish_first(
-    factor, spots, extent, mine_ref, other_ref, bottom_ref, up_ref, join_ref, token, both, acts
-):
+def finish_first(factor, spots, extent, *refs):
+    own_ref, mine_ref, other_ref, decoded_ref, bottom_ref, up_ref, join_ref, token, both, acts = refs
+    decoded_ref[...] = own_ref[...]
     token[...] = jnp.zeros(token.shape, F32)
     section = lax.axis_index("section")
     size = both.shape[1]
@@ -609,7 +619,7 @@
         flops=10**9,
     )(near, [in_hbm(w) for w in weights])
     weights = [*weights[:3], held_bottom, *weights[3:]]
-    last = range(1, min(n, 4))
+    last = [m for m in (2, 3, 1) if m < n]
     gathered = [near] + [exchange(near, "space", mask) for mask in last]
     masks = tuple(tuple(m ^ mask for m in held) for mask in (0, *last))
 
@@ -637,7 +647,7 @@
     fine, coarse = (nx, ny, nz), (nx // 2, ny // 2, nz // 2)
     size = upper_rows // 2
     act_rows = c2 // LANES * crows + crows // LANES * wide_own
-    decoded, keep, send, vol2, z1, h1, z2, blocks, z3, t4, ut = call(
+    own, keep, send, vol2, z1, h1, z2, blocks, z3, t4, ut = call(
         functools.partial(upper_kernel, geo + (upper_spots,)),
         [
             ((sx * plane, c1), BF),
@@ -694,18 +704,19 @@
     low_total = between_cores(low_keep, low_send)
     total, other = between_chips(total, size, crops, low_total)
     factor = 1.0 / math.sqrt(crops * rows)
-    grad_bottom, grad_up, grad_join, token = call(
+    decoded, grad_bottom, grad_up, grad_join, token = call(
         functools.partial(finish_first, factor, upper_spots, coarse),
         [
+            ((sx * plane, c1), BF),
             (shapes["bottom"], F32),
             (shapes["up"][::-1], F32),
             (shapes["join"], F32),
             ((8, LANES), F32),
         ],
         [pltpu.VMEM((2, size, LANES), BF), pltpu.VMEM((crops, act_rows, LANES), BF)],
-        (VMEM, VMEM),
+        (VMEM, VMEM, VMEM),
         vmem=12,
-    )(total, other)
+    )(own, total, other)
     low_total, low_other = between_chips(low_total, low_size, crops, token)
     grad_first, grad_enc, grad_down = call(
         functools.partial(finish_second, factor, lower_spots),

time: 44.2 us -> 43.8 us (level)
  transfers between devices with their start and end apart: 10 -> 10, of which waited for: 8 -> 7; matrix products, arithmetic and copies ran while one was open for 0% -> 0% of each run, Pallas kernels for 29% -> 29%
where the time goes in v6:
time: 43.8 us; the launch traced here: 43.6 us
  Pallas kernels  24.7 us (56%)
  starting transfers between devices  11.2 us (26%)
  waiting for transfers between devices  7.03 us (16%)
  between operations  0.73 us (2%)
    ppermute x10, starting transfers between devices, exchange(): return lax.ppermute(array, axis, [(i, i ^ mask) for i in range(devices)])  11.2 us
    pallas_call x1, Pallas kernels, body(): call(functools.partial(upper_kernel, geo + (upper_spots,)), [((sx * plane...  10.2 us
    ppermute x10, waiting for transfers between devices, exchange(): return lax.ppermute(array, axis, [(i, i ^ mask) for i in range(devices)])  7.03 us
    pallas_call x1, Pallas kernels, body(): call(functools.partial(lower_kernel, geo + (lower_spots,)), [((lower_spot...  3.96 us
    pallas_call x1, Pallas kernels, body(): call(flip_kernel, [(w_bottom.shape, BF)] * 2, [pltpu.SemaphoreType.DMA((3...  2.37 us
    pallas_call x1, Pallas kernels, body(): call(stage_kernel, [(w.shape, BF) for w in weights], [pltpu.SemaphoreType...  2.25 us
    pallas_call x1, Pallas kernels, body(): call(functools.partial(finish_first, factor, upper_spots, coarse), [((sx...  1.63 us
    pallas_call x1, Pallas kernels, body(): call(functools.partial(skip_kernel, fine, c1), [((rows, c1), F32)], [], (...  1.47 us
  transfers between devices with their start and end apart: 10, of which 7 were waited for; matrix products, arithmetic and copies ran while one was open for 0% of the time, Pallas kernels for 29%

profile of v6, /device:TPU:0, one launch (start us, length us, event | category | flops | bytes accessed | tf_op | source)
XLA Modules:
  0.0 43.6 jit_solution(10163343496807026590)
XLA Ops:
  0.6 0.9 %shard_map.135.near_ref.a_ref = bf16[1,192,128]{2,1,0:T(8,128)(2,1)S(1)} custom-call(bf16[2,64,64]{2,1,0:T(8,128)(2,1)} %bitcast.8, bf16[128,128]{1,0:T(8,128)(2,1)} %bitcast.9), custom_call_target="tpu_custom_call" | custom-call | bytes 2097152 | tf_op jit(solution)/shard_map/pallas_call | solution.py:594
  1.5 4.1 %collective-permute-start = (bf16[1,192,128]{2,1,0:T(8,128)(2,1)S(1)}, bf16[1,192,128]{2,1,0:T(8,128)(2,1)S(1)}, u32[]{:S(2)}, u32[]{:S(2)}) collective-permute-start(bf16[1,192,128]{2,1,0:T(8,128)(2,1)S(1)} %shard_map.135.near_ref.a_ref), channel_id=1, source_target_pairs={{0,4},{1,5},{2,6},{3,7},{4,0},{5,1},{6,2},{7,3},{8,12},{9,13},{10,... | collective-permute-start | bytes 147464 | tf_op jit(solution)/shard_map/ppermute | solution.py:532
  5.6 2.4 %shard_map.136 = (bf16[6912,256]{1,0:T(8,128)(2,1)S(1)}, bf16[6912,256]{1,0:T(8,128)(2,1)S(1)}) custom-call(bf16[1,192,128]{2,1,0:T(8,128)(2,1)S(1)} %shard_map.135.near_ref.a_ref, bf16[6912,256]{1,0:T(8,128)(2,1)} %source.1), custom_call_target="tpu_custom_call" | custom-call | flops 1000000000 | bytes 2097152 | tf_op jit(solution)/shard_map/pallas_call | solution.py:601
  8.0 0.2 collective-permute-done.b_ref
  8.2 1.8 %collective-permute-start.3 = (bf16[2,192,128]{2,1,0:T(8,128)(2,1)S(1)}, bf16[2,192,128]{2,1,0:T(8,128)(2,1)S(1)}, u32[]{:S(2)}, u32[]{:S(2)}) collective-permute-start(bf16[2,192,128]{2,1,0:T(8,128)(2,1)S(1)} %shard_map.137.near_ref.gathered_0_), channel_id=1, source_target_pairs={{0,1},{1,0},{2,3},{3,2},{4,5},{5,4},{6,7},{7,6},{8,9},{9,8},{10,11... | collective-permute-start | bytes 294920 | tf_op jit(solution)/shard_map/ppermute | solution.py:532
  10.0 1.1 %collective-permute-start.2 = (bf16[2,192,128]{2,1,0:T(8,128)(2,1)S(1)}, bf16[2,192,128]{2,1,0:T(8,128)(2,1)S(1)}, u32[]{:S(2)}, u32[]{:S(2)}) collective-permute-start(bf16[2,192,128]{2,1,0:T(8,128)(2,1)S(1)} %shard_map.137.near_ref.gathered_0_), channel_id=1, source_target_pairs={{0,3},{1,2},{2,1},{3,0},{4,7},{5,6},{6,5},{7,4},{8,11},{9,10},{10,... | collective-permute-start | bytes 294920 | tf_op jit(solution)/shard_map/ppermute | solution.py:532
  11.1 0.6 %collective-permute-start.1 = (bf16[2,192,128]{2,1,0:T(8,128)(2,1)S(1)}, bf16[2,192,128]{2,1,0:T(8,128)(2,1)S(1)}, u32[]{:S(2)}, u32[]{:S(2)}) collective-permute-start(bf16[2,192,128]{2,1,0:T(8,128)(2,1)S(1)} %shard_map.137.near_ref.gathered_0_), channel_id=1, source_target_pairs={{0,2},{1,3},{2,0},{3,1},{4,6},{5,7},{6,4},{7,5},{8,10},{9,11},{10,... | collective-permute-start | bytes 294920 | tf_op jit(solution)/shard_map/ppermute | solution.py:532
  11.8 2.2 %shard_map.138 = (bf16[1728,128]{1,0:T(8,128)(2,1)S(1)}, bf16[3456,128]{1,0:T(8,128)(2,1)S(1)}, bf16[1024,256]{1,0:T(8,128)(2,1)S(1)}, bf16[256,1024]{1,0:T(8,128)(2,1)S(1)}, bf16[6912,128]{1,0:T(8,128)(2,1)S(1)}) custom-call(bf16[2,192,128]{2,1,0:T(8,128)(2,1)S(1)} %shard_map.137.near_ref.gathered_0_, bf16[1728,128]{1,0:T(8,128)(2,1)} %sources_0_.1, ...), custom_call_target="tpu_custom_call" | custom-call | flops 1000000000 | bytes 2097152 | tf_op jit(solution)/shard_map/pallas_call | solution.py:614
  14.0 0.0 collective-permute-done.3.gathered_3_
  14.0 1.7 %collective-permute-done.2.gathered_2_ = bf16[2,192,128]{2,1,0:T(8,128)(2,1)S(1)} collective-permute-done((bf16[2,192,128]{2,1,0:T(8,128)(2,1)S(1)}, bf16[2,192,128]{2,1,0:T(8,128)(2,1)S(1)}, u32[]{:S(2)}, u32[]{:S(2)}) %collective-permute-start.2) | collective-permute-done | bytes 98336 | tf_op jit(solution)/shard_map/ppermute | solution.py:532
  15.8 0.1 collective-permute-done.1.gathered_1_
  15.9 10.2 %shard_map.139 = (bf16[128,128]{1,0:T(8,128)(2,1)S(1)}, bf16[848,128]{1,0:T(8,128)(2,1)S(1)}, bf16[560,128]{1,0:T(8,128)(2,1)S(1)}, bf16[1024,128]{1,0:T(8,128)(...) custom-call(bf16[2,192,128]{2,1,0:T(8,128)(2,1)S(1)} %shard_map.137., ...), custom_call_target="tpu_custom_call" | custom-call | flops 10000000000 | bytes 2097152 | tf_op jit(solution)/shard_map/pallas_call | solution.py:650
  26.1 0.1 collective-permute-start.4
  26.1 1.5 %shard_map.140.refs_0_.skip_back_ref = f32[1024,128]{1,0:T(8,128)S(1)} custom-call(bf16[1024,384]{1,0:T(8,128)(2,1)S(1)} %get-tuple-element.48.ut, bf16[6912,128]{1,0:T(8,128)(2,1)S(1)} %get-tuple-element.44.weights_5_.w_join), custom_call_target="tpu_custom_call" | custom-call | flops 1000000000 | bytes 2097152 | tf_op jit(solution)/shard_map/pallas_call | solution.py:680
  27.6 0.0 collective-permute-done.4.b_ref
  27.7 1.6 %collective-permute-start.5 = (bf16[848,128]{1,0:T(8,128)(2,1)S(1)}, bf16[848,128]{1,0:T(8,128)(2,1)S(1)}, u32[]{:S(2)}, u32[]{:S(2)}) collective-permute-start(bf16[848,128]{1,0:T(8,128)(2,1)S(1)} %shard_map.141.a_ref), channel_id=1, source_target_pairs={{0,16},{8,24},{16,0},{24,8},{1,17},{9,25},{17,1},{25,9},{2,18},{10... | collective-permute-start | bytes 651272 | tf_op jit(solution)/shard_map/ppermute | solution.py:532
  29.2 4.0 %shard_map.142 = (bf16[256,128]{1,0:T(8,128)(2,1)S(1)}, bf16[1024,128]{1,0:T(8,128)(2,1)S(1)}, bf16[1024,128]{1,0:T(8,128)(2,1)S(1)}) custom-call(bf16[3456,128]{1,0:T(8,128)(2,1)S(1)} %get-tuple-element.40.weights_1_.w_enc, bf16[1024,256]{1,0:T(8,128)(2,1)S(1)} %get-tuple-element.41.weights_2_.w_down, ...), custom_call_target="tpu_custom_call" | custom-call | flops 6000000000 | bytes 2097152 | tf_op jit(solution)/shard_map/pallas_call | solution.py:690
  33.2 1.0 %shard_map.143 = (bf16[464,128]{1,0:T(8,128)(2,1)S(1)}, bf16[464,128]{1,0:T(8,128)(2,1)S(1)}) custom-call(bf16[256,128]{1,0:T(8,128)(2,1)S(1)} %get-tuple-element.54.down_ref, bf16[1024,128]{1,0:T(8,128)(2,1)S(1)} %get-tuple-element.55.t2_ref, bf16[1024,128]{1,0:T(8,128)(2,1)S(1)} %get-tuple-element.56.t1_ref, ...), custom_call_target="tpu_custom_call" | custom-call | flops 1000000000 | bytes 2097152 | tf_op jit(solution)/shard_map/pallas_call | solution.py:697
  34.1 0.3 collective-permute-start.6
  34.4 1.1 %collective-permute-done.6.b_ref = bf16[464,128]{1,0:T(8,128)(2,1)S(1)} collective-permute-done((bf16[464,128]{1,0:T(8,128)(2,1)S(1)}, bf16[464,128]{1,0:T(8,128)(2,1)S(1)}, u32[]{:S(2)}, u32[]{:S(2)}) %collective-permute-start.6) | collective-permute-done | bytes 118816 | tf_op jit(solution)/shard_map/ppermute | solution.py:532
  35.6 0.0 collective-permute-done.5.b_ref
  35.6 0.3 collective-permute-start.7
  35.9 1.2 %collective-permute-start.8 = (bf16[464,128]{1,0:T(8,128)(2,1)S(1)}, bf16[464,128]{1,0:T(8,128)(2,1)S(1)}, u32[]{:S(2)}, u32[]{:S(2)}) collective-permute-start(bf16[464,128]{1,0:T(8,128)(2,1)S(1)} %shard_map.144.refs_0_.a_ref), channel_id=1, source_target_pairs={{0,16},{8,24},{16,0},{24,8},{1,17},{9,25},{17,1},{25,9},{2,18},{10... | collective-permute-start | bytes 356360 | tf_op jit(solution)/shard_map/ppermute | solution.py:532
  37.2 0.1 collective-permute-done.7.refs_2_
  37.3 1.6 %shard_map.146 = (bf16[128,128]{1,0:T(8,128)(2,1)}, f32[32,6912]{1,0:T(8,128)}, f32[256,128]{1,0:T(8,128)}, f32[16,6912]{1,0:T(8,128)}, f32[8,128]{1,0:T(8,128)S(1)}) custom-call(bf16[128,128]{1,0:T(8,128)(2,1)S(1)} %get-tuple-element.45.refs_0_, bf16[1136,128]{1,0:T(8,128)(2,1)S(1)} %shard_map.145.refs_1_, bf16[1136,128]{1,0:T(8,128)(2,1)S(1)} %collective-permute-done.7.refs_2_), custom_call_target="tpu_custom_call" | custom-call | bytes 2097152 | tf_op jit(solution)/shard_map/pallas_call | solution.py:707
  38.9 2.4 %collective-permute-done.8.b_ref = bf16[464,128]{1,0:T(8,128)(2,1)S(1)} collective-permute-done((bf16[464,128]{1,0:T(8,128)(2,1)S(1)}, bf16[464,128]{1,0:T(8,128)(2,1)S(1)}, u32[]{:S(2)}, u32[]{:S(2)}) %collective-permute-start.8) | collective-permute-done | bytes 118816 | tf_op jit(solution)/shard_map/ppermute | solution.py:532
  41.4 0.1 collective-permute-start.9
  41.5 1.3 %collective-permute-done.9.other_ref = bf16[464,128]{1,0:T(8,128)(2,1)S(1)} collective-permute-done((bf16[464,128]{1,0:T(8,128)(2,1)S(1)}, bf16[464,128]{1,0:T(8,128)(2,1)S(1)}, u32[]{:S(2)}, u32[]{:S(2)}) %collective-permute-start.9) | collective-permute-done | bytes 118816 | tf_op jit(solution)/shard_map/ppermute | solution.py:532
  42.8 0.8 %shard_map.148 = (f32[16,1728]{1,0:T(8,128)}, f32[16,3456]{1,0:T(8,128)}, f32[32,1024]{1,0:T(8,128)}) custom-call(bf16[464,128]{1,0:T(8,128)(2,1)S(1)} %shard_map.147.mine_ref, bf16[464,128]{1,0:T(8,128)(2,1)S(1)} %collective-permute-done.9.other_ref), custom_call_target="tpu_custom_call" | custom-call | bytes 2097152 | tf_op jit(solution)/shard_map/pallas_call | solution.py:721
  (5 shorter events, 0.2 us)
Async XLA Ops:
  1.5 6.7 %collective-permute-start = (bf16[1,192,128]{2,1,0:T(8,128)(2,1)S(1)}, bf16[1,192,128]{2,1,0:T(8,128)(2,1)S(1)}, u32[]{:S(2)}, u32[]{:S(2)}) collective-permute-start(bf16[1,192,128]{2,1,0:T(8,128)(2,1)S(1)} %shard_map.135.near_ref.a_ref), channel_id=1, source_target_pairs={{0,4},{1,5},{2,6},{3,7},{4,0},{5,1},{6,2},{7,3},{8,12},{9,13},{10,... | collective-permute-start | bytes 147464 | tf_op jit(solution)/shard_map/ppermute | solution.py:532
  8.2 5.8 %collective-permute-start.3 = (bf16[2,192,128]{2,1,0:T(8,128)(2,1)S(1)}, bf16[2,192,128]{2,1,0:T(8,128)(2,1)S(1)}, u32[]{:S(2)}, u32[]{:S(2)}) collective-permute-start(bf16[2,192,128]{2,1,0:T(8,128)(2,1)S(1)} %shard_map.137.near_ref.gathered_0_), channel_id=1, source_target_pairs={{0,1},{1,0},{2,3},{3,2},{4,5},{5,4},{6,7},{7,6},{8,9},{9,8},{10,11... | collective-permute-start | bytes 294920 | tf_op jit(solution)/shard_map/ppermute | solution.py:532
  10.0 5.8 %collective-permute-start.2 = (bf16[2,192,128]{2,1,0:T(8,128)(2,1)S(1)}, bf16[2,192,128]{2,1,0:T(8,128)(2,1)S(1)}, u32[]{:S(2)}, u32[]{:S(2)}) collective-permute-start(bf16[2,192,128]{2,1,0:T(8,128)(2,1)S(1)} %shard_map.137.near_ref.gathered_0_), channel_id=1, source_target_pairs={{0,3},{1,2},{2,1},{3,0},{4,7},{5,6},{6,5},{7,4},{8,11},{9,10},{10,... | collective-permute-start | bytes 294920 | tf_op jit(solution)/shard_map/ppermute | solution.py:532
  11.1 4.7 %collective-permute-start.1 = (bf16[2,192,128]{2,1,0:T(8,128)(2,1)S(1)}, bf16[2,192,128]{2,1,0:T(8,128)(2,1)S(1)}, u32[]{:S(2)}, u32[]{:S(2)}) collective-permute-start(bf16[2,192,128]{2,1,0:T(8,128)(2,1)S(1)} %shard_map.137.near_ref.gathered_0_), channel_id=1, source_target_pairs={{0,2},{1,3},{2,0},{3,1},{4,6},{5,7},{6,4},{7,5},{8,10},{9,11},{10,... | collective-permute-start | bytes 294920 | tf_op jit(solution)/shard_map/ppermute | solution.py:532
  26.1 1.6 %collective-permute-start.4 = (bf16[560,128]{1,0:T(8,128)(2,1)S(1)}, bf16[560,128]{1,0:T(8,128)(2,1)S(1)}, u32[]{:S(2)}, u32[]{:S(2)}) collective-permute-start(bf16[560,128]{1,0:T(8,128)(2,1)S(1)} %get-tuple-element.47), channel_id=1, source_target_pairs={{0,8},{8,0},{16,24},{24,16},{1,9},{9,1},{17,25},{25,17},{2,10},{10... | collective-permute-start | bytes 430088 | tf_op jit(solution)/shard_map/ppermute | solution.py:532
  27.7 7.9 %collective-permute-start.5 = (bf16[848,128]{1,0:T(8,128)(2,1)S(1)}, bf16[848,128]{1,0:T(8,128)(2,1)S(1)}, u32[]{:S(2)}, u32[]{:S(2)}) collective-permute-start(bf16[848,128]{1,0:T(8,128)(2,1)S(1)} %shard_map.141.a_ref), channel_id=1, source_target_pairs={{0,16},{8,24},{16,0},{24,8},{1,17},{9,25},{17,1},{25,9},{2,18},{10... | collective-permute-start | bytes 651272 | tf_op jit(solution)/shard_map/ppermute | solution.py:532
  34.1 1.4 %collective-permute-start.6 = (bf16[464,128]{1,0:T(8,128)(2,1)S(1)}, bf16[464,128]{1,0:T(8,128)(2,1)S(1)}, u32[]{:S(2)}, u32[]{:S(2)}) collective-permute-start(bf16[464,128]{1,0:T(8,128)(2,1)S(1)} %get-tuple-element.60), channel_id=1, source_target_pairs={{0,8},{8,0},{16,24},{24,16},{1,9},{9,1},{17,25},{25,17},{2,10},{10... | collective-permute-start | bytes 356360 | tf_op jit(solution)/shard_map/ppermute | solution.py:532
  35.6 1.6 %collective-permute-start.7 = (bf16[1136,128]{1,0:T(8,128)(2,1)S(1)}, bf16[1136,128]{1,0:T(8,128)(2,1)S(1)}, u32[]{:S(2)}, u32[]{:S(2)}) collective-permute-start(bf16[1136,128]{1,0:T(8,128)(2,1)S(1)} %shard_map.145.refs_1_), channel_id=1, source_target_pairs={{0,8},{8,0},{16,24},{24,16},{1,9},{9,1},{17,25},{25,17},{2,10},{10... | collective-permute-start | bytes 872456 | tf_op jit(solution)/shard_map/ppermute | solution.py:532
  35.9 5.4 %collective-permute-start.8 = (bf16[464,128]{1,0:T(8,128)(2,1)S(1)}, bf16[464,128]{1,0:T(8,128)(2,1)S(1)}, u32[]{:S(2)}, u32[]{:S(2)}) collective-permute-start(bf16[464,128]{1,0:T(8,128)(2,1)S(1)} %shard_map.144.refs_0_.a_ref), channel_id=1, source_target_pairs={{0,16},{8,24},{16,0},{24,8},{1,17},{9,25},{17,1},{25,9},{2,18},{10... | collective-permute-start | bytes 356360 | tf_op jit(solution)/shard_map/ppermute | solution.py:532
  41.4 1.4 %collective-permute-start.9 = (bf16[464,128]{1,0:T(8,128)(2,1)S(1)}, bf16[464,128]{1,0:T(8,128)(2,1)S(1)}, u32[]{:S(2)}, u32[]{:S(2)}) collective-permute-start(bf16[464,128]{1,0:T(8,128)(2,1)S(1)} %shard_map.147.mine_ref), channel_id=1, source_target_pairs={{0,8},{8,0},{16,24},{24,16},{1,9},{9,1},{17,25},{25,17},{2,10},{10... | collective-permute-start | bytes 356360 | tf_op jit(solution)/shard_map/ppermute | solution.py:532

commit v7 on v6

--- a/solution.py
+++ b/solution.py
@@ -154,7 +154,7 @@
     return dot_t(pick, field)
 
 
-def tap_shifts(grad, extent):
+def tap_shifts(grad, extent, depths=(-1, 0, 1)):
     nx, ny, nz = extent
     count, rows = grad.shape
     place = lax.broadcasted_iota(jnp.int32, grad.shape, 1)
@@ -162,7 +162,7 @@
     parts = []
     for ox in (-1, 0, 1):
         for oy in (-1, 0, 1):
-            for oz in (-1, 0, 1):
+            for oz in depths:
                 by = ((ox * ny) + oy) * nz + oz
                 part = pltpu.roll(grad, by % rows, 1) if by else grad
                 inside = None
@@ -353,7 +353,8 @@
     t4 = (e3 * slope(z4)).astype(BF)
     t4_ref[...] = t4
     emit(pack, spots["up"], dot(own_columns(lb_ref[...], 8 * c1 // n, position).astype(BF), g2))
-    emit(pack, spots["join"], tap_grad(own_columns(t7, c1 // n, position), joined[...], fine), 27)
+    taps = dot(tap_shifts(own_columns(t7, c1 // n, position), fine, (0,)), uj[...])
+    emit(pack, spots["join"], taps, 9)
     split(pack, keep_ref, send_ref, lax.rem(lax.axis_index("section"), 2))
     at = send_ref.shape[0]
     for v in range(0, c2, LANES):

time: 43.8 us -> 43.5 us (level)
  no operation moved by 1% of the time
where the time goes in v7:
time: 43.5 us; the launch traced here: 43.3 us
  Pallas kernels  24.3 us (56%)
  starting transfers between devices  11.2 us (26%)
  waiting for transfers between devices  7.03 us (16%)
  between operations  0.73 us (2%)
    ppermute x10, starting transfers between devices, exchange(): return lax.ppermute(array, axis, [(i, i ^ mask) for i in range(devices)])  11.2 us
    pallas_call x1, Pallas kernels, body(): call(functools.partial(upper_kernel, geo + (upper_spots,)), [((sx * plane...  9.91 us
    ppermute x10, waiting for transfers between devices, exchange(): return lax.ppermute(array, axis, [(i, i ^ mask) for i in range(devices)])  7.03 us
    pallas_call x1, Pallas kernels, body(): call(functools.partial(lower_kernel, geo + (lower_spots,)), [((lower_spot...  3.96 us
    pallas_call x1, Pallas kernels, body(): call(flip_kernel, [(w_bottom.shape, BF)] * 2, [pltpu.SemaphoreType.DMA((3...  2.37 us
    pallas_call x1, Pallas kernels, body(): call(stage_kernel, [(w.shape, BF) for w in weights], [pltpu.SemaphoreType...  2.25 us
    pallas_call x1, Pallas kernels, body(): call(functools.partial(finish_first, factor, upper_spots, coarse), [((sx...  1.63 us
    pallas_call x1, Pallas kernels, body(): call(functools.partial(skip_kernel, fine, c1), [((rows, c1), F32)], [], (...  1.46 us
  transfers between devices with their start and end apart: 10, of which 7 were waited for; matrix products, arithmetic and copies ran while one was open for 0% of the time, Pallas kernels for 29%

profile of v7, /device:TPU:0, one launch (start us, length us, event | category | flops | bytes accessed | tf_op | source)
XLA Modules:
  0.0 43.3 jit_solution(4286164236238931665)
XLA Ops:
  0.6 0.9 %shard_map.135.near_ref.a_ref = bf16[1,192,128]{2,1,0:T(8,128)(2,1)S(1)} custom-call(bf16[2,64,64]{2,1,0:T(8,128)(2,1)} %bitcast.8, bf16[128,128]{1,0:T(8,128)(2,1)} %bitcast.9), custom_call_target="tpu_custom_call" | custom-call | bytes 2097152 | tf_op jit(solution)/shard_map/pallas_call | solution.py:595
  1.5 4.1 %collective-permute-start = (bf16[1,192,128]{2,1,0:T(8,128)(2,1)S(1)}, bf16[1,192,128]{2,1,0:T(8,128)(2,1)S(1)}, u32[]{:S(2)}, u32[]{:S(2)}) collective-permute-start(bf16[1,192,128]{2,1,0:T(8,128)(2,1)S(1)} %shard_map.135.near_ref.a_ref), channel_id=1, source_target_pairs={{0,4},{1,5},{2,6},{3,7},{4,0},{5,1},{6,2},{7,3},{8,12},{9,13},{10,... | collective-permute-start | bytes 147464 | tf_op jit(solution)/shard_map/ppermute | solution.py:533
  5.6 2.4 %shard_map.136 = (bf16[6912,256]{1,0:T(8,128)(2,1)S(1)}, bf16[6912,256]{1,0:T(8,128)(2,1)S(1)}) custom-call(bf16[1,192,128]{2,1,0:T(8,128)(2,1)S(1)} %shard_map.135.near_ref.a_ref, bf16[6912,256]{1,0:T(8,128)(2,1)} %source.1), custom_call_target="tpu_custom_call" | custom-call | flops 1000000000 | bytes 2097152 | tf_op jit(solution)/shard_map/pallas_call | solution.py:602
  8.0 0.2 collective-permute-done.b_ref
  8.2 1.8 %collective-permute-start.3 = (bf16[2,192,128]{2,1,0:T(8,128)(2,1)S(1)}, bf16[2,192,128]{2,1,0:T(8,128)(2,1)S(1)}, u32[]{:S(2)}, u32[]{:S(2)}) collective-permute-start(bf16[2,192,128]{2,1,0:T(8,128)(2,1)S(1)} %shard_map.137.near_ref.gathered_0_), channel_id=1, source_target_pairs={{0,1},{1,0},{2,3},{3,2},{4,5},{5,4},{6,7},{7,6},{8,9},{9,8},{10,11... | collective-permute-start | bytes 294920 | tf_op jit(solution)/shard_map/ppermute | solution.py:533
  10.0 1.1 %collective-permute-start.2 = (bf16[2,192,128]{2,1,0:T(8,128)(2,1)S(1)}, bf16[2,192,128]{2,1,0:T(8,128)(2,1)S(1)}, u32[]{:S(2)}, u32[]{:S(2)}) collective-permute-start(bf16[2,192,128]{2,1,0:T(8,128)(2,1)S(1)} %shard_map.137.near_ref.gathered_0_), channel_id=1, source_target_pairs={{0,3},{1,2},{2,1},{3,0},{4,7},{5,6},{6,5},{7,4},{8,11},{9,10},{10,... | collective-permute-start | bytes 294920 | tf_op jit(solution)/shard_map/ppermute | solution.py:533
  11.1 0.6 %collective-permute-start.1 = (bf16[2,192,128]{2,1,0:T(8,128)(2,1)S(1)}, bf16[2,192,128]{2,1,0:T(8,128)(2,1)S(1)}, u32[]{:S(2)}, u32[]{:S(2)}) collective-permute-start(bf16[2,192,128]{2,1,0:T(8,128)(2,1)S(1)} %shard_map.137.near_ref.gathered_0_), channel_id=1, source_target_pairs={{0,2},{1,3},{2,0},{3,1},{4,6},{5,7},{6,4},{7,5},{8,10},{9,11},{10,... | collective-permute-start | bytes 294920 | tf_op jit(solution)/shard_map/ppermute | solution.py:533
  11.8 2.2 %shard_map.138 = (bf16[1728,128]{1,0:T(8,128)(2,1)S(1)}, bf16[3456,128]{1,0:T(8,128)(2,1)S(1)}, bf16[1024,256]{1,0:T(8,128)(2,1)S(1)}, bf16[256,1024]{1,0:T(8,128)(2,1)S(1)}, bf16[6912,128]{1,0:T(8,128)(2,1)S(1)}) custom-call(bf16[2,192,128]{2,1,0:T(8,128)(2,1)S(1)} %shard_map.137.near_ref.gathered_0_, bf16[1728,128]{1,0:T(8,128)(2,1)} %sources_0_.1, ...), custom_call_target="tpu_custom_call" | custom-call | flops 1000000000 | bytes 2097152 | tf_op jit(solution)/shard_map/pallas_call | solution.py:615
  14.0 0.0 collective-permute-done.3.gathered_3_
  14.0 1.7 %collective-permute-done.2.gathered_2_ = bf16[2,192,128]{2,1,0:T(8,128)(2,1)S(1)} collective-permute-done((bf16[2,192,128]{2,1,0:T(8,128)(2,1)S(1)}, bf16[2,192,128]{2,1,0:T(8,128)(2,1)S(1)}, u32[]{:S(2)}, u32[]{:S(2)}) %collective-permute-start.2) | collective-permute-done | bytes 98336 | tf_op jit(solution)/shard_map/ppermute | solution.py:533
  15.8 0.1 collective-permute-done.1.gathered_1_
  15.9 9.9 %shard_map.139 = (bf16[128,128]{1,0:T(8,128)(2,1)S(1)}, bf16[848,128]{1,0:T(8,128)(2,1)S(1)}, bf16[560,128]{1,0:T(8,128)(2,1)S(1)}, bf16[1024,128]{1,0:T(8,128)(...) custom-call(bf16[2,192,128]{2,1,0:T(8,128)(2,1)S(1)} %shard_map.137., ...), custom_call_target="tpu_custom_call" | custom-call | flops 10000000000 | bytes 2097152 | tf_op jit(solution)/shard_map/pallas_call | solution.py:651
  25.8 0.1 collective-permute-start.4
  25.8 1.5 %shard_map.140.refs_0_.skip_back_ref = f32[1024,128]{1,0:T(8,128)S(1)} custom-call(bf16[1024,384]{1,0:T(8,128)(2,1)S(1)} %get-tuple-element.48.ut, bf16[6912,128]{1,0:T(8,128)(2,1)S(1)} %get-tuple-element.44.weights_5_.w_join), custom_call_target="tpu_custom_call" | custom-call | flops 1000000000 | bytes 2097152 | tf_op jit(solution)/shard_map/pallas_call | solution.py:681
  27.3 0.0 collective-permute-done.4.b_ref
  27.4 1.6 %collective-permute-start.5 = (bf16[848,128]{1,0:T(8,128)(2,1)S(1)}, bf16[848,128]{1,0:T(8,128)(2,1)S(1)}, u32[]{:S(2)}, u32[]{:S(2)}) collective-permute-start(bf16[848,128]{1,0:T(8,128)(2,1)S(1)} %shard_map.141.a_ref), channel_id=1, source_target_pairs={{0,16},{8,24},{16,0},{24,8},{1,17},{9,25},{17,1},{25,9},{2,18},{10... | collective-permute-start | bytes 651272 | tf_op jit(solution)/shard_map/ppermute | solution.py:533
  28.9 4.0 %shard_map.142 = (bf16[256,128]{1,0:T(8,128)(2,1)S(1)}, bf16[1024,128]{1,0:T(8,128)(2,1)S(1)}, bf16[1024,128]{1,0:T(8,128)(2,1)S(1)}) custom-call(bf16[3456,128]{1,0:T(8,128)(2,1)S(1)} %get-tuple-element.40.weights_1_.w_enc, bf16[1024,256]{1,0:T(8,128)(2,1)S(1)} %get-tuple-element.41.weights_2_.w_down, ...), custom_call_target="tpu_custom_call" | custom-call | flops 6000000000 | bytes 2097152 | tf_op jit(solution)/shard_map/pallas_call | solution.py:691
  32.9 1.0 %shard_map.143 = (bf16[464,128]{1,0:T(8,128)(2,1)S(1)}, bf16[464,128]{1,0:T(8,128)(2,1)S(1)}) custom-call(bf16[256,128]{1,0:T(8,128)(2,1)S(1)} %get-tuple-element.54.down_ref, bf16[1024,128]{1,0:T(8,128)(2,1)S(1)} %get-tuple-element.55.t2_ref, bf16[1024,128]{1,0:T(8,128)(2,1)S(1)} %get-tuple-element.56.t1_ref, ...), custom_call_target="tpu_custom_call" | custom-call | flops 1000000000 | bytes 2097152 | tf_op jit(solution)/shard_map/pallas_call | solution.py:698
  33.8 0.3 collective-permute-start.6
  34.1 1.1 %collective-permute-done.6.b_ref = bf16[464,128]{1,0:T(8,128)(2,1)S(1)} collective-permute-done((bf16[464,128]{1,0:T(8,128)(2,1)S(1)}, bf16[464,128]{1,0:T(8,128)(2,1)S(1)}, u32[]{:S(2)}, u32[]{:S(2)}) %collective-permute-start.6) | collective-permute-done | bytes 118816 | tf_op jit(solution)/shard_map/ppermute | solution.py:533
  35.3 0.0 collective-permute-done.5.b_ref
  35.3 0.3 collective-permute-start.7
  35.6 1.2 %collective-permute-start.8 = (bf16[464,128]{1,0:T(8,128)(2,1)S(1)}, bf16[464,128]{1,0:T(8,128)(2,1)S(1)}, u32[]{:S(2)}, u32[]{:S(2)}) collective-permute-start(bf16[464,128]{1,0:T(8,128)(2,1)S(1)} %shard_map.144.refs_0_.a_ref), channel_id=1, source_target_pairs={{0,16},{8,24},{16,0},{24,8},{1,17},{9,25},{17,1},{25,9},{2,18},{10... | collective-permute-start | bytes 356360 | tf_op jit(solution)/shard_map/ppermute | solution.py:533
  36.9 0.1 collective-permute-done.7.refs_2_
  37.0 1.6 %shard_map.146 = (bf16[128,128]{1,0:T(8,128)(2,1)}, f32[32,6912]{1,0:T(8,128)}, f32[256,128]{1,0:T(8,128)}, f32[16,6912]{1,0:T(8,128)}, f32[8,128]{1,0:T(8,128)S(1)}) custom-call(bf16[128,128]{1,0:T(8,128)(2,1)S(1)} %get-tuple-element.45.refs_0_, bf16[1136,128]{1,0:T(8,128)(2,1)S(1)} %shard_map.145.refs_1_, bf16[1136,128]{1,0:T(8,128)(2,1)S(1)} %collective-permute-done.7.refs_2_), custom_call_target="tpu_custom_call" | custom-call | bytes 2097152 | tf_op jit(solution)/shard_map/pallas_call | solution.py:708
  38.6 2.4 %collective-permute-done.8.b_ref = bf16[464,128]{1,0:T(8,128)(2,1)S(1)} collective-permute-done((bf16[464,128]{1,0:T(8,128)(2,1)S(1)}, bf16[464,128]{1,0:T(8,128)(2,1)S(1)}, u32[]{:S(2)}, u32[]{:S(2)}) %collective-permute-start.8) | collective-permute-done | bytes 118816 | tf_op jit(solution)/shard_map/ppermute | solution.py:533
  41.1 0.1 collective-permute-start.9
  41.2 1.3 %collective-permute-done.9.other_ref = bf16[464,128]{1,0:T(8,128)(2,1)S(1)} collective-permute-done((bf16[464,128]{1,0:T(8,128)(2,1)S(1)}, bf16[464,128]{1,0:T(8,128)(2,1)S(1)}, u32[]{:S(2)}, u32[]{:S(2)}) %collective-permute-start.9) | collective-permute-done | bytes 118816 | tf_op jit(solution)/shard_map/ppermute | solution.py:533
  42.5 0.8 %shard_map.148 = (f32[16,1728]{1,0:T(8,128)}, f32[16,3456]{1,0:T(8,128)}, f32[32,1024]{1,0:T(8,128)}) custom-call(bf16[464,128]{1,0:T(8,128)(2,1)S(1)} %shard_map.147.mine_ref, bf16[464,128]{1,0:T(8,128)(2,1)S(1)} %collective-permute-done.9.other_ref), custom_call_target="tpu_custom_call" | custom-call | bytes 2097152 | tf_op jit(solution)/shard_map/pallas_call | solution.py:722
  (5 shorter events, 0.2 us)
Async XLA Ops:
  1.5 6.7 %collective-permute-start = (bf16[1,192,128]{2,1,0:T(8,128)(2,1)S(1)}, bf16[1,192,128]{2,1,0:T(8,128)(2,1)S(1)}, u32[]{:S(2)}, u32[]{:S(2)}) collective-permute-start(bf16[1,192,128]{2,1,0:T(8,128)(2,1)S(1)} %shard_map.135.near_ref.a_ref), channel_id=1, source_target_pairs={{0,4},{1,5},{2,6},{3,7},{4,0},{5,1},{6,2},{7,3},{8,12},{9,13},{10,... | collective-permute-start | bytes 147464 | tf_op jit(solution)/shard_map/ppermute | solution.py:533
  8.2 5.8 %collective-permute-start.3 = (bf16[2,192,128]{2,1,0:T(8,128)(2,1)S(1)}, bf16[2,192,128]{2,1,0:T(8,128)(2,1)S(1)}, u32[]{:S(2)}, u32[]{:S(2)}) collective-permute-start(bf16[2,192,128]{2,1,0:T(8,128)(2,1)S(1)} %shard_map.137.near_ref.gathered_0_), channel_id=1, source_target_pairs={{0,1},{1,0},{2,3},{3,2},{4,5},{5,4},{6,7},{7,6},{8,9},{9,8},{10,11... | collective-permute-start | bytes 294920 | tf_op jit(solution)/shard_map/ppermute | solution.py:533
  10.0 5.8 %collective-permute-start.2 = (bf16[2,192,128]{2,1,0:T(8,128)(2,1)S(1)}, bf16[2,192,128]{2,1,0:T(8,128)(2,1)S(1)}, u32[]{:S(2)}, u32[]{:S(2)}) collective-permute-start(bf16[2,192,128]{2,1,0:T(8,128)(2,1)S(1)} %shard_map.137.near_ref.gathered_0_), channel_id=1, source_target_pairs={{0,3},{1,2},{2,1},{3,0},{4,7},{5,6},{6,5},{7,4},{8,11},{9,10},{10,... | collective-permute-start | bytes 294920 | tf_op jit(solution)/shard_map/ppermute | solution.py:533
  11.1 4.7 %collective-permute-start.1 = (bf16[2,192,128]{2,1,0:T(8,128)(2,1)S(1)}, bf16[2,192,128]{2,1,0:T(8,128)(2,1)S(1)}, u32[]{:S(2)}, u32[]{:S(2)}) collective-permute-start(bf16[2,192,128]{2,1,0:T(8,128)(2,1)S(1)} %shard_map.137.near_ref.gathered_0_), channel_id=1, source_target_pairs={{0,2},{1,3},{2,0},{3,1},{4,6},{5,7},{6,4},{7,5},{8,10},{9,11},{10,... | collective-permute-start | bytes 294920 | tf_op jit(solution)/shard_map/ppermute | solution.py:533
  25.8 1.6 %collective-permute-start.4 = (bf16[560,128]{1,0:T(8,128)(2,1)S(1)}, bf16[560,128]{1,0:T(8,128)(2,1)S(1)}, u32[]{:S(2)}, u32[]{:S(2)}) collective-permute-start(bf16[560,128]{1,0:T(8,128)(2,1)S(1)} %get-tuple-element.47), channel_id=1, source_target_pairs={{0,8},{8,0},{16,24},{24,16},{1,9},{9,1},{17,25},{25,17},{2,10},{10... | collective-permute-start | bytes 430088 | tf_op jit(solution)/shard_map/ppermute | solution.py:533
  27.4 7.9 %collective-permute-start.5 = (bf16[848,128]{1,0:T(8,128)(2,1)S(1)}, bf16[848,128]{1,0:T(8,128)(2,1)S(1)}, u32[]{:S(2)}, u32[]{:S(2)}) collective-permute-start(bf16[848,128]{1,0:T(8,128)(2,1)S(1)} %shard_map.141.a_ref), channel_id=1, source_target_pairs={{0,16},{8,24},{16,0},{24,8},{1,17},{9,25},{17,1},{25,9},{2,18},{10... | collective-permute-start | bytes 651272 | tf_op jit(solution)/shard_map/ppermute | solution.py:533
  33.8 1.4 %collective-permute-start.6 = (bf16[464,128]{1,0:T(8,128)(2,1)S(1)}, bf16[464,128]{1,0:T(8,128)(2,1)S(1)}, u32[]{:S(2)}, u32[]{:S(2)}) collective-permute-start(bf16[464,128]{1,0:T(8,128)(2,1)S(1)} %get-tuple-element.60), channel_id=1, source_target_pairs={{0,8},{8,0},{16,24},{24,16},{1,9},{9,1},{17,25},{25,17},{2,10},{10... | collective-permute-start | bytes 356360 | tf_op jit(solution)/shard_map/ppermute | solution.py:533
  35.3 1.6 %collective-permute-start.7 = (bf16[1136,128]{1,0:T(8,128)(2,1)S(1)}, bf16[1136,128]{1,0:T(8,128)(2,1)S(1)}, u32[]{:S(2)}, u32[]{:S(2)}) collective-permute-start(bf16[1136,128]{1,0:T(8,128)(2,1)S(1)} %shard_map.145.refs_1_), channel_id=1, source_target_pairs={{0,8},{8,0},{16,24},{24,16},{1,9},{9,1},{17,25},{25,17},{2,10},{10... | collective-permute-start | bytes 872456 | tf_op jit(solution)/shard_map/ppermute | solution.py:533
  35.6 5.4 %collective-permute-start.8 = (bf16[464,128]{1,0:T(8,128)(2,1)S(1)}, bf16[464,128]{1,0:T(8,128)(2,1)S(1)}, u32[]{:S(2)}, u32[]{:S(2)}) collective-permute-start(bf16[464,128]{1,0:T(8,128)(2,1)S(1)} %shard_map.144.refs_0_.a_ref), channel_id=1, source_target_pairs={{0,16},{8,24},{16,0},{24,8},{1,17},{9,25},{17,1},{25,9},{2,18},{10... | collective-permute-start | bytes 356360 | tf_op jit(solution)/shard_map/ppermute | solution.py:533
  41.1 1.4 %collective-permute-start.9 = (bf16[464,128]{1,0:T(8,128)(2,1)S(1)}, bf16[464,128]{1,0:T(8,128)(2,1)S(1)}, u32[]{:S(2)}, u32[]{:S(2)}) collective-permute-start(bf16[464,128]{1,0:T(8,128)(2,1)S(1)} %shard_map.147.mine_ref), channel_id=1, source_target_pairs={{0,8},{8,0},{16,24},{24,16},{1,9},{9,1},{17,25},{25,17},{2,10},{10... | collective-permute-start | bytes 356360 | tf_op jit(solution)/shard_map/ppermute | solution.py:533

commit v8 on v7

--- a/solution.py
+++ b/solution.py
@@ -274,7 +274,7 @@
     send_ref,
     vol_ref,
     z1_ref,
-    h1_ref,
+    u1,
     z2_ref,
     d_ref,
     z3_ref,
@@ -282,7 +282,6 @@
     ut,
     blocks,
     uv,
-    u1,
     uj,
     uc,
     joined,
@@ -321,7 +320,6 @@
     z1 = conv_z(uv[:, 0 : 3 * c0], w_first, fine)
     z1_ref[...] = z1
     h1 = silu(z1)
-    h1_ref[...] = h1
     fill(u1, z_windows(h1.astype(F32), nz))
     z2 = conv_z(u1[...], w_enc, fine)
     z2_ref[...] = z2
@@ -418,7 +416,8 @@
     fine = (sx * n, ny, nz)
     count = c1 // n
     pack[0 : down_ref.shape[0], :] = down_ref[...]
-    emit(pack, spots["enc"], tap_grad(own_columns(t2_ref[...], count, position), h1_ref[...], fine), 27)
+    taps = dot(tap_shifts(own_columns(t2_ref[...], count, position), fine, (0,)), h1_ref[...])
+    emit(pack, spots["enc"], taps, 9)
     taps = tap_grad(own_columns(t1_ref[...], count, position), vol_ref[...], fine)
     lane = lax.broadcasted_iota(jnp.int32, (count, LANES), 1)
     at = spots["first"]
@@ -656,7 +655,7 @@
             ((size, LANES), BF),
             ((rows, 2 * c0), BF),
             ((rows, c1), F32),
-            ((rows, c1), BF),
+            ((rows, 3 * c1), BF),
             ((rows, c1), F32),
             ((crows, 8 * c1), BF),
             ((crows, c2), F32),
@@ -666,7 +665,6 @@
         [
             pltpu.VMEM((n, own_rows, LANES), BF),
             pltpu.VMEM((rows, 2 * LANES), BF),
-            pltpu.VMEM((rows, 3 * c1), BF),
             pltpu.VMEM((rows, 6 * c1), BF),
             pltpu.VMEM((crows + 2 * cplane, 9 * c2), BF),
             pltpu.VMEM((rows, 2 * c1), BF),

time: 43.5 us -> 43.6 us (level)
  no operation moved by 1% of the time
where the time goes in v8:
time: 43.6 us; the launch traced here: 43.4 us
  Pallas kernels  24.4 us (56%)
  starting transfers between devices  11.1 us (25%)
  waiting for transfers between devices  7.11 us (16%)
  between operations  0.74 us (2%)
    ppermute x10, starting transfers between devices, exchange(): return lax.ppermute(array, axis, [(i, i ^ mask) for i in range(devices)])  11.1 us
    pallas_call x1, Pallas kernels, body(): call(functools.partial(upper_kernel, geo + (upper_spots,)), [((sx * plane...  9.9 us
    ppermute x10, waiting for transfers between devices, exchange(): return lax.ppermute(array, axis, [(i, i ^ mask) for i in range(devices)])  7.11 us
    pallas_call x1, Pallas kernels, body(): call(functools.partial(lower_kernel, geo + (lower_spots,)), [((lower_spot...  3.96 us
    pallas_call x1, Pallas kernels, body(): call(flip_kernel, [(w_bottom.shape, BF)] * 2, [pltpu.SemaphoreType.DMA((3...  2.37 us
    pallas_call x1, Pallas kernels, body(): call(stage_kernel, [(w.shape, BF) for w in weights], [pltpu.SemaphoreType...  2.25 us
    pallas_call x1, Pallas kernels, body(): call(functools.partial(finish_first, factor, upper_spots, coarse), [((sx...  1.63 us
    pallas_call x1, Pallas kernels, body(): call(functools.partial(skip_kernel, fine, c1), [((rows, c1), F32)], [], (...  1.47 us
  transfers between devices with their start and end apart: 10, of which 7 were waited for; matrix products, arithmetic and copies ran while one was open for 0% of the time, Pallas kernels for 29%

profile of v8, /device:TPU:0, one launch (start us, length us, event | category | flops | bytes accessed | tf_op | source)
XLA Modules:
  0.0 43.4 jit_solution(12839585264751993099)
XLA Ops:
  0.6 0.9 %shard_map.135.near_ref.a_ref = bf16[1,192,128]{2,1,0:T(8,128)(2,1)S(1)} custom-call(bf16[2,64,64]{2,1,0:T(8,128)(2,1)} %bitcast.8, bf16[128,128]{1,0:T(8,128)(2,1)} %bitcast.9), custom_call_target="tpu_custom_call" | custom-call | bytes 2097152 | tf_op jit(solution)/shard_map/pallas_call | solution.py:594
  1.5 4.1 %collective-permute-start = (bf16[1,192,128]{2,1,0:T(8,128)(2,1)S(1)}, bf16[1,192,128]{2,1,0:T(8,128)(2,1)S(1)}, u32[]{:S(2)}, u32[]{:S(2)}) collective-permute-start(bf16[1,192,128]{2,1,0:T(8,128)(2,1)S(1)} %shard_map.135.near_ref.a_ref), channel_id=1, source_target_pairs={{0,4},{1,5},{2,6},{3,7},{4,0},{5,1},{6,2},{7,3},{8,12},{9,13},{10,... | collective-permute-start | bytes 147464 | tf_op jit(solution)/shard_map/ppermute | solution.py:532
  5.6 2.4 %shard_map.136 = (bf16[6912,256]{1,0:T(8,128)(2,1)S(1)}, bf16[6912,256]{1,0:T(8,128)(2,1)S(1)}) custom-call(bf16[1,192,128]{2,1,0:T(8,128)(2,1)S(1)} %shard_map.135.near_ref.a_ref, bf16[6912,256]{1,0:T(8,128)(2,1)} %source.1), custom_call_target="tpu_custom_call" | custom-call | flops 1000000000 | bytes 2097152 | tf_op jit(solution)/shard_map/pallas_call | solution.py:601
  8.0 0.2 collective-permute-done.b_ref
  8.2 1.8 %collective-permute-start.3 = (bf16[2,192,128]{2,1,0:T(8,128)(2,1)S(1)}, bf16[2,192,128]{2,1,0:T(8,128)(2,1)S(1)}, u32[]{:S(2)}, u32[]{:S(2)}) collective-permute-start(bf16[2,192,128]{2,1,0:T(8,128)(2,1)S(1)} %shard_map.137.near_ref.gathered_0_), channel_id=1, source_target_pairs={{0,1},{1,0},{2,3},{3,2},{4,5},{5,4},{6,7},{7,6},{8,9},{9,8},{10,11... | collective-permute-start | bytes 294920 | tf_op jit(solution)/shard_map/ppermute | solution.py:532
  10.0 1.1 %collective-permute-start.2 = (bf16[2,192,128]{2,1,0:T(8,128)(2,1)S(1)}, bf16[2,192,128]{2,1,0:T(8,128)(2,1)S(1)}, u32[]{:S(2)}, u32[]{:S(2)}) collective-permute-start(bf16[2,192,128]{2,1,0:T(8,128)(2,1)S(1)} %shard_map.137.near_ref.gathered_0_), channel_id=1, source_target_pairs={{0,3},{1,2},{2,1},{3,0},{4,7},{5,6},{6,5},{7,4},{8,11},{9,10},{10,... | collective-permute-start | bytes 294920 | tf_op jit(solution)/shard_map/ppermute | solution.py:532
  11.1 0.6 %collective-permute-start.1 = (bf16[2,192,128]{2,1,0:T(8,128)(2,1)S(1)}, bf16[2,192,128]{2,1,0:T(8,128)(2,1)S(1)}, u32[]{:S(2)}, u32[]{:S(2)}) collective-permute-start(bf16[2,192,128]{2,1,0:T(8,128)(2,1)S(1)} %shard_map.137.near_ref.gathered_0_), channel_id=1, source_target_pairs={{0,2},{1,3},{2,0},{3,1},{4,6},{5,7},{6,4},{7,5},{8,10},{9,11},{10,... | collective-permute-start | bytes 294920 | tf_op jit(solution)/shard_map/ppermute | solution.py:532
  11.8 2.2 %shard_map.138 = (bf16[1728,128]{1,0:T(8,128)(2,1)S(1)}, bf16[3456,128]{1,0:T(8,128)(2,1)S(1)}, bf16[1024,256]{1,0:T(8,128)(2,1)S(1)}, bf16[256,1024]{1,0:T(8,128)(2,1)S(1)}, bf16[6912,128]{1,0:T(8,128)(2,1)S(1)}) custom-call(bf16[2,192,128]{2,1,0:T(8,128)(2,1)S(1)} %shard_map.137.near_ref.gathered_0_, bf16[1728,128]{1,0:T(8,128)(2,1)} %sources_0_.1, ...), custom_call_target="tpu_custom_call" | custom-call | flops 1000000000 | bytes 2097152 | tf_op jit(solution)/shard_map/pallas_call | solution.py:614
  14.0 0.0 collective-permute-done.3.gathered_3_
  14.0 1.7 %collective-permute-done.2.gathered_2_ = bf16[2,192,128]{2,1,0:T(8,128)(2,1)S(1)} collective-permute-done((bf16[2,192,128]{2,1,0:T(8,128)(2,1)S(1)}, bf16[2,192,128]{2,1,0:T(8,128)(2,1)S(1)}, u32[]{:S(2)}, u32[]{:S(2)}) %collective-permute-start.2) | collective-permute-done | bytes 98336 | tf_op jit(solution)/shard_map/ppermute | solution.py:532
  15.8 0.1 collective-permute-done.1.gathered_1_
  15.9 9.9 %shard_map.139 = (bf16[128,128]{1,0:T(8,128)(2,1)S(1)}, bf16[848,128]{1,0:T(8,128)(2,1)S(1)}, bf16[560,128]{1,0:T(8,128)(2,1)S(1)}, bf16[1024,128]{1,0:T(8,128)(...) custom-call(bf16[2,192,128]{2,1,0:T(8,128)(2,1)S(1)} %shard_map.137., ...), custom_call_target="tpu_custom_call" | custom-call | flops 10000000000 | bytes 2097152 | tf_op jit(solution)/shard_map/pallas_call | solution.py:650
  25.8 0.1 collective-permute-start.4
  25.8 1.5 %shard_map.140.refs_0_.skip_back_ref = f32[1024,128]{1,0:T(8,128)S(1)} custom-call(bf16[1024,384]{1,0:T(8,128)(2,1)S(1)} %get-tuple-element.48.ut, bf16[6912,128]{1,0:T(8,128)(2,1)S(1)} %get-tuple-element.44.weights_5_.w_join), custom_call_target="tpu_custom_call" | custom-call | flops 1000000000 | bytes 2097152 | tf_op jit(solution)/shard_map/pallas_call | solution.py:679
  27.3 0.0 collective-permute-done.4.b_ref
  27.4 1.6 %collective-permute-start.5 = (bf16[848,128]{1,0:T(8,128)(2,1)S(1)}, bf16[848,128]{1,0:T(8,128)(2,1)S(1)}, u32[]{:S(2)}, u32[]{:S(2)}) collective-permute-start(bf16[848,128]{1,0:T(8,128)(2,1)S(1)} %shard_map.141.a_ref), channel_id=1, source_target_pairs={{0,16},{8,24},{16,0},{24,8},{1,17},{9,25},{17,1},{25,9},{2,18},{10... | collective-permute-start | bytes 651272 | tf_op jit(solution)/shard_map/ppermute | solution.py:532
  28.9 4.0 %shard_map.142 = (bf16[256,128]{1,0:T(8,128)(2,1)S(1)}, bf16[1024,128]{1,0:T(8,128)(2,1)S(1)}, bf16[1024,128]{1,0:T(8,128)(2,1)S(1)}) custom-call(bf16[3456,128]{1,0:T(8,128)(2,1)S(1)} %get-tuple-element.40.weights_1_.w_enc, bf16[1024,256]{1,0:T(8,128)(2,1)S(1)} %get-tuple-element.41.weights_2_.w_down, ...), custom_call_target="tpu_custom_call" | custom-call | flops 6000000000 | bytes 2097152 | tf_op jit(solution)/shard_map/pallas_call | solution.py:689
  32.9 1.0 %shard_map.143 = (bf16[464,128]{1,0:T(8,128)(2,1)S(1)}, bf16[464,128]{1,0:T(8,128)(2,1)S(1)}) custom-call(bf16[256,128]{1,0:T(8,128)(2,1)S(1)} %get-tuple-element.54.down_ref, bf16[1024,128]{1,0:T(8,128)(2,1)S(1)} %get-tuple-element.55.t2_ref, bf16[1024,128]{1,0:T(8,128)(2,1)S(1)} %get-tuple-element.56.t1_ref, ...), custom_call_target="tpu_custom_call" | custom-call | flops 1000000000 | bytes 2097152 | tf_op jit(solution)/shard_map/pallas_call | solution.py:696
  33.9 0.3 collective-permute-start.6
  34.2 1.1 %collective-permute-done.6.b_ref = bf16[464,128]{1,0:T(8,128)(2,1)S(1)} collective-permute-done((bf16[464,128]{1,0:T(8,128)(2,1)S(1)}, bf16[464,128]{1,0:T(8,128)(2,1)S(1)}, u32[]{:S(2)}, u32[]{:S(2)}) %collective-permute-start.6) | collective-permute-done | bytes 118816 | tf_op jit(solution)/shard_map/ppermute | solution.py:532
  35.3 0.0 collective-permute-done.5.b_ref
  35.4 0.3 collective-permute-start.7
  35.7 1.2 %collective-permute-start.8 = (bf16[464,128]{1,0:T(8,128)(2,1)S(1)}, bf16[464,128]{1,0:T(8,128)(2,1)S(1)}, u32[]{:S(2)}, u32[]{:S(2)}) collective-permute-start(bf16[464,128]{1,0:T(8,128)(2,1)S(1)} %shard_map.144.refs_0_.a_ref), channel_id=1, source_target_pairs={{0,16},{8,24},{16,0},{24,8},{1,17},{9,25},{17,1},{25,9},{2,18},{10... | collective-permute-start | bytes 356360 | tf_op jit(solution)/shard_map/ppermute | solution.py:532
  36.9 0.2 collective-permute-done.7.refs_2_
  37.0 1.6 %shard_map.146 = (bf16[128,128]{1,0:T(8,128)(2,1)}, f32[32,6912]{1,0:T(8,128)}, f32[256,128]{1,0:T(8,128)}, f32[16,6912]{1,0:T(8,128)}, f32[8,128]{1,0:T(8,128)S(1)}) custom-call(bf16[128,128]{1,0:T(8,128)(2,1)S(1)} %get-tuple-element.45.refs_0_, bf16[1136,128]{1,0:T(8,128)(2,1)S(1)} %shard_map.145.refs_1_, bf16[1136,128]{1,0:T(8,128)(2,1)S(1)} %collective-permute-done.7.refs_2_), custom_call_target="tpu_custom_call" | custom-call | bytes 2097152 | tf_op jit(solution)/shard_map/pallas_call | solution.py:706
  38.7 2.4 %collective-permute-done.8.b_ref = bf16[464,128]{1,0:T(8,128)(2,1)S(1)} collective-permute-done((bf16[464,128]{1,0:T(8,128)(2,1)S(1)}, bf16[464,128]{1,0:T(8,128)(2,1)S(1)}, u32[]{:S(2)}, u32[]{:S(2)}) %collective-permute-start.8) | collective-permute-done | bytes 118816 | tf_op jit(solution)/shard_map/ppermute | solution.py:532
  41.2 0.1 collective-permute-start.9
  41.2 1.3 %collective-permute-done.9.other_ref = bf16[464,128]{1,0:T(8,128)(2,1)S(1)} collective-permute-done((bf16[464,128]{1,0:T(8,128)(2,1)S(1)}, bf16[464,128]{1,0:T(8,128)(2,1)S(1)}, u32[]{:S(2)}, u32[]{:S(2)}) %collective-permute-start.9) | collective-permute-done | bytes 118816 | tf_op jit(solution)/shard_map/ppermute | solution.py:532
  42.5 0.8 %shard_map.148 = (f32[16,1728]{1,0:T(8,128)}, f32[16,3456]{1,0:T(8,128)}, f32[32,1024]{1,0:T(8,128)}) custom-call(bf16[464,128]{1,0:T(8,128)(2,1)S(1)} %shard_map.147.mine_ref, bf16[464,128]{1,0:T(8,128)(2,1)S(1)} %collective-permute-done.9.other_ref), custom_call_target="tpu_custom_call" | custom-call | bytes 2097152 | tf_op jit(solution)/shard_map/pallas_call | solution.py:720
  (5 shorter events, 0.2 us)
Async XLA Ops:
  1.5 6.7 %collective-permute-start = (bf16[1,192,128]{2,1,0:T(8,128)(2,1)S(1)}, bf16[1,192,128]{2,1,0:T(8,128)(2,1)S(1)}, u32[]{:S(2)}, u32[]{:S(2)}) collective-permute-start(bf16[1,192,128]{2,1,0:T(8,128)(2,1)S(1)} %shard_map.135.near_ref.a_ref), channel_id=1, source_target_pairs={{0,4},{1,5},{2,6},{3,7},{4,0},{5,1},{6,2},{7,3},{8,12},{9,13},{10,... | collective-permute-start | bytes 147464 | tf_op jit(solution)/shard_map/ppermute | solution.py:532
  8.2 5.8 %collective-permute-start.3 = (bf16[2,192,128]{2,1,0:T(8,128)(2,1)S(1)}, bf16[2,192,128]{2,1,0:T(8,128)(2,1)S(1)}, u32[]{:S(2)}, u32[]{:S(2)}) collective-permute-start(bf16[2,192,128]{2,1,0:T(8,128)(2,1)S(1)} %shard_map.137.near_ref.gathered_0_), channel_id=1, source_target_pairs={{0,1},{1,0},{2,3},{3,2},{4,5},{5,4},{6,7},{7,6},{8,9},{9,8},{10,11... | collective-permute-start | bytes 294920 | tf_op jit(solution)/shard_map/ppermute | solution.py:532
  10.0 5.8 %collective-permute-start.2 = (bf16[2,192,128]{2,1,0:T(8,128)(2,1)S(1)}, bf16[2,192,128]{2,1,0:T(8,128)(2,1)S(1)}, u32[]{:S(2)}, u32[]{:S(2)}) collective-permute-start(bf16[2,192,128]{2,1,0:T(8,128)(2,1)S(1)} %shard_map.137.near_ref.gathered_0_), channel_id=1, source_target_pairs={{0,3},{1,2},{2,1},{3,0},{4,7},{5,6},{6,5},{7,4},{8,11},{9,10},{10,... | collective-permute-start | bytes 294920 | tf_op jit(solution)/shard_map/ppermute | solution.py:532
  11.1 4.7 %collective-permute-start.1 = (bf16[2,192,128]{2,1,0:T(8,128)(2,1)S(1)}, bf16[2,192,128]{2,1,0:T(8,128)(2,1)S(1)}, u32[]{:S(2)}, u32[]{:S(2)}) collective-permute-start(bf16[2,192,128]{2,1,0:T(8,128)(2,1)S(1)} %shard_map.137.near_ref.gathered_0_), channel_id=1, source_target_pairs={{0,2},{1,3},{2,0},{3,1},{4,6},{5,7},{6,4},{7,5},{8,10},{9,11},{10,... | collective-permute-start | bytes 294920 | tf_op jit(solution)/shard_map/ppermute | solution.py:532
  25.8 1.6 %collective-permute-start.4 = (bf16[560,128]{1,0:T(8,128)(2,1)S(1)}, bf16[560,128]{1,0:T(8,128)(2,1)S(1)}, u32[]{:S(2)}, u32[]{:S(2)}) collective-permute-start(bf16[560,128]{1,0:T(8,128)(2,1)S(1)} %get-tuple-element.47), channel_id=1, source_target_pairs={{0,8},{8,0},{16,24},{24,16},{1,9},{9,1},{17,25},{25,17},{2,10},{10... | collective-permute-start | bytes 430088 | tf_op jit(solution)/shard_map/ppermute | solution.py:532
  27.4 8.0 %collective-permute-start.5 = (bf16[848,128]{1,0:T(8,128)(2,1)S(1)}, bf16[848,128]{1,0:T(8,128)(2,1)S(1)}, u32[]{:S(2)}, u32[]{:S(2)}) collective-permute-start(bf16[848,128]{1,0:T(8,128)(2,1)S(1)} %shard_map.141.a_ref), channel_id=1, source_target_pairs={{0,16},{8,24},{16,0},{24,8},{1,17},{9,25},{17,1},{25,9},{2,18},{10... | collective-permute-start | bytes 651272 | tf_op jit(solution)/shard_map/ppermute | solution.py:532
  33.9 1.4 %collective-permute-start.6 = (bf16[464,128]{1,0:T(8,128)(2,1)S(1)}, bf16[464,128]{1,0:T(8,128)(2,1)S(1)}, u32[]{:S(2)}, u32[]{:S(2)}) collective-permute-start(bf16[464,128]{1,0:T(8,128)(2,1)S(1)} %get-tuple-element.60), channel_id=1, source_target_pairs={{0,8},{8,0},{16,24},{24,16},{1,9},{9,1},{17,25},{25,17},{2,10},{10... | collective-permute-start | bytes 356360 | tf_op jit(solution)/shard_map/ppermute | solution.py:532
  35.4 1.6 %collective-permute-start.7 = (bf16[1136,128]{1,0:T(8,128)(2,1)S(1)}, bf16[1136,128]{1,0:T(8,128)(2,1)S(1)}, u32[]{:S(2)}, u32[]{:S(2)}) collective-permute-start(bf16[1136,128]{1,0:T(8,128)(2,1)S(1)} %shard_map.145.refs_1_), channel_id=1, source_target_pairs={{0,8},{8,0},{16,24},{24,16},{1,9},{9,1},{17,25},{25,17},{2,10},{10... | collective-permute-start | bytes 872456 | tf_op jit(solution)/shard_map/ppermute | solution.py:532
  35.7 5.4 %collective-permute-start.8 = (bf16[464,128]{1,0:T(8,128)(2,1)S(1)}, bf16[464,128]{1,0:T(8,128)(2,1)S(1)}, u32[]{:S(2)}, u32[]{:S(2)}) collective-permute-start(bf16[464,128]{1,0:T(8,128)(2,1)S(1)} %shard_map.144.refs_0_.a_ref), channel_id=1, source_target_pairs={{0,16},{8,24},{16,0},{24,8},{1,17},{9,25},{17,1},{25,9},{2,18},{10... | collective-permute-start | bytes 356360 | tf_op jit(solution)/shard_map/ppermute | solution.py:532
  41.2 1.4 %collective-permute-start.9 = (bf16[464,128]{1,0:T(8,128)(2,1)S(1)}, bf16[464,128]{1,0:T(8,128)(2,1)S(1)}, u32[]{:S(2)}, u32[]{:S(2)}) collective-permute-start(bf16[464,128]{1,0:T(8,128)(2,1)S(1)} %shard_map.147.mine_ref), channel_id=1, source_target_pairs={{0,8},{8,0},{16,24},{24,16},{1,9},{9,1},{17,25},{25,17},{2,10},{10... | collective-permute-start | bytes 356360 | tf_op jit(solution)/shard_map/ppermute | solution.py:532
